TPU v7x, 32 devices: a whole 2x2x4 slice. The times are simulated.
32 devices in a mesh: ctx: 8 (over z, y), fsdp: 4 (over x, core).
Axes of the slice: x: 2, y: 2, z: 4, core: 2. Of those that a mesh axis runs over, the one named last changes fastest.
Arguments:
- residual_in: bfloat16 [4, 1024, 768], P('fsdp', 'ctx'), may hold values from -6 to 6
- cotangent: float32 [4, 1024, 768], P('fsdp', 'ctx'), may hold values from -6 to 6
- group_order: int32 [16], replicated, may hold values from 0 to 15, each once
- gain_first: float32 [768], P('fsdp'), may hold values from 0.5 to 1.5
- shift_first: float32 [768], P('fsdp'), may hold values from -3 to 3
- gain_second: float32 [768], P('fsdp'), may hold values from 0.5 to 1.5
- shift_second: float32 [768], P('fsdp'), may hold values from -3 to 3
- heads_weight: float32 [768, 2304], P('fsdp')
- heads_bias: float32 [2304], P('fsdp'), may hold values from -3 to 3
- output_weight: float32 [768, 768], P('fsdp'), may hold values from -6 to 6
- output_bias: float32 [768], P('fsdp'), may hold values from -3 to 3
- up_weight: float32 [768, 3072], P('fsdp'), may hold values from -0.21875 to 0.21875
- up_bias: float32 [3072], P('fsdp'), may hold values from -3 to 3
- down_weight: float32 [768, 3072], P('fsdp'), may hold values from -0.109375 to 0.109375
- down_bias: float32 [768], P('fsdp'), may hold values from -3 to 3
- heads_moment: float32 [768, 2304], P('fsdp')
- output_moment: float32 [768, 768], P('fsdp')
- up_moment: float32 [768, 3072], P('fsdp')
- down_moment: float32 [768, 3072], P('fsdp')
Outputs:
- block_out: bfloat16 [4, 1024, 768], P('fsdp', 'ctx')
- input_grad: float32 [4, 1024, 768], P('fsdp', 'ctx')
- grad_gain_first: float32 [768], P('fsdp')
- grad_shift_first: float32 [768], P('fsdp')
- grad_gain_second: float32 [768], P('fsdp')
- grad_shift_second: float32 [768], P('fsdp')
- grad_heads_weight: float32 [768, 2304], P('fsdp')
- grad_heads_bias: float32 [2304], P('fsdp')
- grad_output_weight: float32 [768, 768], P('fsdp')
- grad_output_bias: float32 [768], P('fsdp')
- grad_up_weight: float32 [768, 3072], P('fsdp')
- grad_up_bias: float32 [3072], P('fsdp')
- grad_down_weight: float32 [768, 3072], P('fsdp')
- grad_down_bias: float32 [768], P('fsdp')
- new_gain_first: float32 [768], P('fsdp')
- new_shift_first: float32 [768], P('fsdp')
- new_gain_second: float32 [768], P('fsdp')
- new_shift_second: float32 [768], P('fsdp')
- new_heads_weight: float32 [768, 2304], P('fsdp')
- new_heads_bias: float32 [2304], P('fsdp')
- new_output_weight: float32 [768, 768], P('fsdp')
- new_output_bias: float32 [768], P('fsdp')
- new_up_weight: float32 [768, 3072], P('fsdp')
- new_up_bias: float32 [3072], P('fsdp')
- new_down_weight: float32 [768, 3072], P('fsdp')
- new_down_bias: float32 [768], P('fsdp')
- new_heads_moment: float32 [768, 2304], P('fsdp')
- new_output_moment: float32 [768, 768], P('fsdp')
- new_up_moment: float32 [768, 3072], P('fsdp')
- new_down_moment: float32 [768, 3072], P('fsdp')
Inputs may be any that keep to these rules, and one draw needn't show every extreme that they name: Storage slot s of every sequence, rows s * 64 to (s + 1) * 64 - 1, holds group group_order[s] of the sequence; each group once.
All inputs are finite; a program needn't handle non-finite values.
Results may differ from a plain program's by a relative error of at most 0.035.
Values may be sent and summed in bfloat16 or wider, within the bound.
No kernel may reach another device: no remote copies, remote signals or barrier semaphores. Data moves between devices by JAX's collectives and lax.ppermute only.
A program may use at most 192 MiB of HBM per device.

v0:
```python
import math

import jax
import jax.numpy as jnp
from jax import lax
from jax.sharding import PartitionSpec as P

HEADS = 12
HD = 64
ROT = 16
NS_ITERS = 5


mom_rate = 0.95
schulz_coeffs = (3.4445, -4.775, 2.0315)
step_rates = (0.04, 0.3, 0.04, 0.04)
vector_rate = 0.3
norm_eps = 1e-05
neg_large = -1e30


def broadcast(x, axis, root):
    mine = lax.axis_index(axis) == root
    return lax.psum(jnp.where(mine, x, jnp.zeros_like(x)), axis)


def layer_norm(inputs, gain, shift):
    average = jnp.mean(inputs, axis=-1, keepdims=True)
    centred = inputs - average
    variance = jnp.mean(centred * centred, axis=-1, keepdims=True)
    inverse = lax.rsqrt(variance + norm_eps)
    normed = centred * inverse
    return (normed, inverse, normed * gain + shift)


def norm_back(delta, normed, inverse, gain):
    scaled = delta * gain
    first = jnp.mean(scaled, axis=-1, keepdims=True)
    second = jnp.mean(scaled * normed, axis=-1, keepdims=True)
    return inverse * (scaled - first - normed * second)


def gelu_value(pre):
    return 0.5 * pre * (1.0 + lax.erf(pre / math.sqrt(2.0)))


def gelu_slope(pre):
    return 0.5 * (1.0 + lax.erf(pre / math.sqrt(2.0))) + pre * jnp.exp(
        -0.5 * pre * pre
    ) / math.sqrt(2.0 * math.pi)


def slot_places(group_order, first_row, count, group):
    positions = first_row + jnp.arange(count, dtype=jnp.int32)
    slots = positions // group
    table = jnp.arange(group_order.shape[0], dtype=jnp.int32)
    picked = jnp.sum(jnp.where(slots[:, None] == table[None, :], group_order[None, :], 0), axis=1)
    return picked * group + positions % group


def rotary_tables(places):
    halfway = ROT // 2
    rates = 10000.0 ** (-2.0 * jnp.arange(halfway, dtype=jnp.float32) / ROT)
    angle = places.astype(jnp.float32)[:, None] * rates[None, :]
    return (jnp.cos(angle), jnp.sin(angle))


def rotate(heads, cosine, sine, sign):
    halfway = ROT // 2
    first = heads[..., :halfway]
    second = heads[..., halfway:ROT]
    cosine = cosine[:, None, :]
    sine = sign * sine[:, None, :]
    return jnp.concatenate(
        [first * cosine - second * sine, second * cosine + first * sine, heads[..., ROT:]], axis=-1
    )


def local(
    residual_in,
    cotangent,
    group_order,
    gain_first,
    shift_first,
    gain_second,
    shift_second,
    heads_weight,
    heads_bias,
    output_weight,
    output_bias,
    up_weight,
    up_bias,
    down_weight,
    down_bias,
    heads_moment,
    output_moment,
    up_moment,
    down_moment,
):
    single = jnp.float32
    half = jnp.bfloat16
    ctx_count = lax.axis_size("ctx")
    shard_count = lax.axis_size("fsdp")
    ctx_place = lax.axis_index("ctx")
    shard_place = lax.axis_index("fsdp")
    seqs, rows, width = residual_in.shape
    length = rows * ctx_count
    group = rows // 2
    scale = 1.0 / math.sqrt(HD)
    query_places = slot_places(group_order, ctx_place * rows, rows, group)
    key_places = slot_places(group_order, 0, length, group)
    copies = (
        lax.all_gather(heads_weight.astype(half), "fsdp", axis=0, tiled=True),
        lax.all_gather(output_weight.astype(half), "fsdp", axis=0, tiled=True),
        lax.all_gather(up_weight.astype(half), "fsdp", axis=0, tiled=True),
        lax.all_gather(down_weight.astype(half), "fsdp", axis=0, tiled=True),
        lax.all_gather(gain_first.astype(half), "fsdp", axis=0, tiled=True),
        lax.all_gather(shift_first.astype(half), "fsdp", axis=0, tiled=True),
        lax.all_gather(gain_second.astype(half), "fsdp", axis=0, tiled=True),
        lax.all_gather(shift_second.astype(half), "fsdp", axis=0, tiled=True),
        lax.all_gather(heads_bias.astype(half), "fsdp", axis=0, tiled=True),
        lax.all_gather(output_bias.astype(half), "fsdp", axis=0, tiled=True),
        lax.all_gather(up_bias.astype(half), "fsdp", axis=0, tiled=True),
        lax.all_gather(down_bias.astype(half), "fsdp", axis=0, tiled=True),
    )
    heads_copy, output_copy, up_copy, down_copy = (copies[0], copies[1], copies[2], copies[3])
    gain_one, shift_one, gain_two, shift_two, heads_shift, output_shift, up_shift, down_shift = [
        piece.astype(single) for piece in copies[4:]
    ]
    inputs = residual_in.astype(single)
    first_hat, first_inv, first_norm = layer_norm(inputs, gain_one, shift_one)
    second_hat, second_inv, second_norm = layer_norm(inputs, gain_two, shift_two)
    first_in = first_norm.astype(half)
    second_in = second_norm.astype(half)
    projected = (
        jnp.einsum("std,de->ste", first_in, heads_copy, preferred_element_type=single) + heads_shift
    )
    cosine, sine = rotary_tables(query_places)
    split = projected.reshape(seqs, rows, 3, HEADS, HD)
    query = rotate(split[:, :, 0], cosine, sine, 1.0).astype(half)
    keys = rotate(split[:, :, 1], cosine, sine, 1.0).astype(half).reshape(seqs, rows, width)
    values = split[:, :, 2].astype(half).reshape(seqs, rows, width)
    peak = jnp.full((seqs, HEADS, rows), neg_large, single)
    key_piece = lax.all_gather(keys, "ctx", axis=1, tiled=True)
    value_piece = lax.all_gather(values, "ctx", axis=1, tiled=True)
    count = key_piece.shape[1]
    places = slot_places(group_order, jnp.int32(0), count, group)
    key_heads = key_piece.reshape(seqs, count, HEADS, HD)
    value_heads = value_piece.reshape(seqs, count, HEADS, HD)
    score = jnp.einsum("sqhd,skhd->shqk", query, key_heads, preferred_element_type=single) * scale
    allowed = (places[None, :] <= query_places[:, None])[None, None]
    new_peak = jnp.maximum(peak, jnp.max(jnp.where(allowed, score, neg_large), axis=-1))
    weights = jnp.where(allowed, jnp.exp(score - new_peak[..., None]), 0.0)
    total = jnp.sum(weights, axis=-1)
    mixed = jnp.einsum(
        "shqk,skhd->shqd", weights.astype(half), value_heads, preferred_element_type=single
    )
    state = (new_peak, total, mixed)
    peak, total, mixed = state
    lse = peak + jnp.log(total)
    attn = (
        jnp.transpose(mixed / total[..., None], (0, 2, 1, 3))
        .reshape(seqs, rows, width)
        .astype(half)
    )
    output_part = (
        jnp.einsum("std,de->ste", attn, output_copy, preferred_element_type=single) + output_shift
    )
    up_pre = jnp.einsum("std,df->stf", second_in, up_copy, preferred_element_type=single) + up_shift
    active = gelu_value(up_pre).astype(half)
    mlp_part = (
        jnp.einsum("stf,df->std", active, down_copy, preferred_element_type=single) + down_shift
    )
    block_out = (inputs + output_part + mlp_part).astype(half)
    grad_half = cotangent.astype(half)
    down_local = jnp.einsum("std,stf->df", grad_half, active, preferred_element_type=single)
    up_delta = jnp.einsum(
        "std,df->stf", grad_half, down_copy, preferred_element_type=single
    ) * gelu_slope(up_pre)
    up_half = up_delta.astype(half)
    up_local = jnp.einsum("std,stf->df", second_in, up_half, preferred_element_type=single)
    second_delta = jnp.einsum("stf,df->std", up_half, up_copy, preferred_element_type=single)
    output_local = jnp.einsum("std,ste->de", attn, grad_half, preferred_element_type=single)
    attn_delta = jnp.einsum(
        "ste,de->std", grad_half, output_copy, preferred_element_type=single
    ).astype(half)
    attn_heads = attn_delta.reshape(seqs, rows, HEADS, HD)
    delta = jnp.transpose(
        jnp.sum(
            attn_heads.astype(single) * attn.reshape(seqs, rows, HEADS, HD).astype(single), axis=-1
        ),
        (0, 2, 1),
    )
    every_key, every_value = (
        lax.all_gather(keys, "ctx", axis=1, tiled=True),
        lax.all_gather(values, "ctx", axis=1, tiled=True),
    )
    block = math.gcd(length, 512)
    count = length // block
    key_blocks = jnp.moveaxis(every_key.reshape(seqs, count, block, HEADS, HD), 1, 0)
    value_blocks = jnp.moveaxis(every_value.reshape(seqs, count, block, HEADS, HD), 1, 0)
    place_blocks = key_places.reshape(count, block)

    def back_block(query_grad, data):
        key_block, value_block, place_block = data
        score = (
            jnp.einsum("sqhd,skhd->shqk", query, key_block, preferred_element_type=single) * scale
        )
        allowed = (place_block[None, :] <= query_places[:, None])[None, None]
        prob = jnp.where(allowed, jnp.exp(score - lse[..., None]), 0.0)
        prob_half = prob.astype(half)
        prob_grad = jnp.einsum(
            "sqhd,skhd->shqk", attn_heads, value_block, preferred_element_type=single
        )
        score_delta = (prob * (prob_grad - delta[..., None])).astype(half)
        query_grad = (
            query_grad
            + jnp.einsum("shqk,skhd->sqhd", score_delta, key_block, preferred_element_type=single)
            * scale
        )
        key_grad = (
            jnp.einsum("shqk,sqhd->skhd", score_delta, query, preferred_element_type=single) * scale
        )
        value_grad = jnp.einsum(
            "shqk,sqhd->skhd", prob_half, attn_heads, preferred_element_type=single
        )
        joined = jnp.concatenate(
            [key_grad.reshape(seqs, block, width), value_grad.reshape(seqs, block, width)], axis=-1
        )
        return (query_grad, joined)

    query_grad, stacked = lax.scan(
        back_block,
        jnp.zeros((seqs, rows, HEADS, HD), single),
        (key_blocks, value_blocks, place_blocks),
    )
    key_grads = jnp.moveaxis(stacked, 0, 1).reshape(seqs, length, 2 * width)
    home = lax.psum_scatter(key_grads, "ctx", scatter_dimension=1, tiled=True)
    key_delta = rotate(home[..., :width].reshape(seqs, rows, HEADS, HD), cosine, sine, -1.0)
    query_delta = rotate(query_grad, cosine, sine, -1.0)
    heads_delta = jnp.concatenate(
        [
            query_delta.reshape(seqs, rows, width),
            key_delta.reshape(seqs, rows, width),
            home[..., width:],
        ],
        axis=-1,
    )
    heads_half = heads_delta.astype(half)
    heads_local = jnp.einsum("std,ste->de", first_in, heads_half, preferred_element_type=single)
    first_delta = jnp.einsum("ste,de->std", heads_half, heads_copy, preferred_element_type=single)
    input_grad = (
        cotangent
        + norm_back(first_delta, first_hat, first_inv, gain_one)
        + norm_back(second_delta, second_hat, second_inv, gain_two)
    )
    columns = (
        lax.psum_scatter(heads_local, "ctx", scatter_dimension=1, tiled=True),
        lax.psum_scatter(output_local, "ctx", scatter_dimension=1, tiled=True),
        lax.psum_scatter(up_local, "ctx", scatter_dimension=1, tiled=True),
        lax.psum_scatter(down_local, "ctx", scatter_dimension=1, tiled=True),
    )
    parts = (
        lax.psum_scatter(columns[0], "fsdp", scatter_dimension=0, tiled=True),
        lax.psum_scatter(columns[1], "fsdp", scatter_dimension=0, tiled=True),
        lax.psum_scatter(columns[2], "fsdp", scatter_dimension=0, tiled=True),
        lax.psum_scatter(columns[3], "fsdp", scatter_dimension=0, tiled=True),
    )
    full_grads = (
        lax.all_gather(parts[0], "ctx", axis=1, tiled=True),
        lax.all_gather(parts[1], "ctx", axis=1, tiled=True),
        lax.all_gather(parts[2], "ctx", axis=1, tiled=True),
        lax.all_gather(parts[3], "ctx", axis=1, tiled=True),
    )
    weights_all = (heads_weight, output_weight, up_weight, down_weight)
    moments_all = (heads_moment, output_moment, up_moment, down_moment)
    new_moments = []
    nest_blocks = []
    for which in range(4):
        moment = mom_rate * moments_all[which] + full_grads[which]
        nest = full_grads[which] + mom_rate * moment
        cols = nest.shape[1] // ctx_count
        new_moments.append(moment)
        nest_blocks.append(lax.dynamic_slice_in_dim(nest, ctx_place * cols, cols, 1))
    sums = lax.psum(
        (
            jnp.sum(first_delta * first_hat, axis=(0, 1)),
            jnp.sum(first_delta, axis=(0, 1)),
            jnp.sum(second_delta * second_hat, axis=(0, 1)),
            jnp.sum(second_delta, axis=(0, 1)),
            jnp.sum(heads_delta, axis=(0, 1)),
            jnp.sum(cotangent, axis=(0, 1)),
            jnp.sum(up_delta, axis=(0, 1)),
            jnp.sum(nest_blocks[0] * nest_blocks[0]),
            jnp.sum(nest_blocks[1] * nest_blocks[1]),
            jnp.sum(nest_blocks[2] * nest_blocks[2]),
            jnp.sum(nest_blocks[3] * nest_blocks[3]),
        ),
        ("ctx", "fsdp"),
    )
    gathered = (
        lax.all_gather(nest_blocks[0], "fsdp", axis=0, tiled=True),
        lax.all_gather(nest_blocks[1], "fsdp", axis=0, tiled=True),
        lax.all_gather(nest_blocks[2], "fsdp", axis=0, tiled=True),
        lax.all_gather(nest_blocks[3], "fsdp", axis=0, tiled=True),
    )
    widths = [piece.shape[1] for piece in gathered]
    widest = max(widths)
    owners = [which * shard_count // 4 for which in range(4)]
    selected = jnp.zeros((width, widest), single)
    square_sum = jnp.zeros((), single)
    for which in range(4):
        chosen = (shard_place == owners[which]).astype(single)
        selected = selected + chosen * jnp.pad(
            gathered[which], ((0, 0), (0, widest - widths[which]))
        )
        square_sum = square_sum + chosen * sums[7 + which]
    ortho = (selected / (jnp.sqrt(square_sum) + 1e-07)).astype(half)
    for turn in range(NS_ITERS):
        partial_value = jnp.einsum("rw,sw->rs", ortho, ortho, preferred_element_type=single)
        gram = lax.psum(partial_value.astype(jnp.bfloat16), "ctx").astype(jnp.float32).astype(half)
        mix = (
            schulz_coeffs[1] * gram.astype(single)
            + schulz_coeffs[2] * jnp.dot(gram, gram, preferred_element_type=single)
        ).astype(half)
        ortho = (
            schulz_coeffs[0] * ortho.astype(single)
            + jnp.dot(mix, ortho, preferred_element_type=single)
        ).astype(half)
    shard_rows = width // shard_count
    updated = []
    for which in range(4):
        received = broadcast(ortho, "fsdp", owners[which])
        piece = lax.dynamic_slice(
            received, (shard_place * shard_rows, 0), (shard_rows, widths[which])
        )
        total_cols = weights_all[which].shape[1]
        current = lax.dynamic_slice_in_dim(
            weights_all[which], ctx_place * widths[which], widths[which], 1
        )
        updated.append(current - step_rates[which] * math.sqrt(total_cols) * piece.astype(single))
    new_weights = (
        lax.all_gather(updated[0], "ctx", axis=1, tiled=True),
        lax.all_gather(updated[1], "ctx", axis=1, tiled=True),
        lax.all_gather(updated[2], "ctx", axis=1, tiled=True),
        lax.all_gather(updated[3], "ctx", axis=1, tiled=True),
    )
    vector_values = (
        gain_first,
        shift_first,
        gain_second,
        shift_second,
        heads_bias,
        output_bias,
        up_bias,
        down_bias,
    )
    vector_grads = (sums[0], sums[1], sums[2], sums[3], sums[4], sums[5], sums[6], sums[5])
    grad_shards = []
    new_shards = []
    for which in range(8):
        size_here = vector_values[which].shape[0]
        whole_grad = vector_grads[which]
        shard = lax.dynamic_slice_in_dim(whole_grad, shard_place * size_here, size_here)
        grad_shards.append(shard)
        new_shards.append(
            vector_values[which]
            - vector_rate * shard * lax.rsqrt(jnp.mean(whole_grad * whole_grad) + norm_eps)
        )
    return (
        block_out,
        input_grad,
        grad_shards[0],
        grad_shards[1],
        grad_shards[2],
        grad_shards[3],
        full_grads[0],
        grad_shards[4],
        full_grads[1],
        grad_shards[5],
        full_grads[2],
        grad_shards[6],
        full_grads[3],
        grad_shards[7],
        new_shards[0],
        new_shards[1],
        new_shards[2],
        new_shards[3],
        new_weights[0],
        new_shards[4],
        new_weights[1],
        new_shards[5],
        new_weights[2],
        new_shards[6],
        new_weights[3],
        new_shards[7],
        new_moments[0],
        new_moments[1],
        new_moments[2],
        new_moments[3],
    )


def solution(mesh):
    in_specs = (
        P("fsdp", "ctx", None),
        P("fsdp", "ctx", None),
        P(),
        P("fsdp"),
        P("fsdp"),
        P("fsdp"),
        P("fsdp"),
        P("fsdp", None),
        P("fsdp"),
        P("fsdp", None),
        P("fsdp"),
        P("fsdp", None),
        P("fsdp"),
        P("fsdp", None),
        P("fsdp"),
        P("fsdp", None),
        P("fsdp", None),
        P("fsdp", None),
        P("fsdp", None),
    )
    out_specs = (
        P("fsdp", "ctx", None),
        P("fsdp", "ctx", None),
        P("fsdp"),
        P("fsdp"),
        P("fsdp"),
        P("fsdp"),
        P("fsdp", None),
        P("fsdp"),
        P("fsdp", None),
        P("fsdp"),
        P("fsdp", None),
        P("fsdp"),
        P("fsdp", None),
        P("fsdp"),
        P("fsdp"),
        P("fsdp"),
        P("fsdp"),
        P("fsdp"),
        P("fsdp", None),
        P("fsdp"),
        P("fsdp", None),
        P("fsdp"),
        P("fsdp", None),
        P("fsdp"),
        P("fsdp", None),
        P("fsdp"),
        P("fsdp", None),
        P("fsdp", None),
        P("fsdp", None),
        P("fsdp", None),
    )
    return jax.shard_map(local, mesh=mesh, in_specs=in_specs, out_specs=out_specs, check_vma=False)
```

profile of v0, /device:TPU:0, one launch (start us, length us, event | category | flops | bytes accessed | tf_op | source)
XLA Modules:
  0.0 1918.1 jit_solution(9995885561238253200)
XLA Ops:
  14.6 14.0 all-reduce.10
  30.0 13.9 all-gather.16.cloned.1.call-done
  49.4 3.0 convert_element_type.325
  55.2 8.5 all-gather.22.cloned.1.call-done
  66.4 45.2 %all-gather.18.cloned.1.call-done = bf16[1,1024,768]{1,2,0:T(8,128)(2,1)} async-done(((bf16[1,128,768]{1,2,0:T(8,128)(2,1)}), bf16[1,1024,768]{1,2,0:T(8,128)(2,1)}) %all-gather.18.cloned.1.call-update) | async-done | bytes 1572880 | tf_op jit(solution)/shard_map/all_gather | solution.py:144
  116.0 41.7 %all-gather.20.cloned.1.call-done = bf16[1,1024,768]{1,2,0:T(8,128)(2,1)} async-done(((bf16[1,128,768]{1,2,0:T(8,128)(2,1)}), bf16[1,1024,768]{1,2,0:T(8,128)(2,1)}) %all-gather.20.cloned.1.call-update) | async-done | bytes 1572880 | tf_op jit(solution)/shard_map/all_gather | solution.py:145
  165.5 3.8 multiply_reduce_fusion.2
  169.3 34.3 %while.13 = (s32[]{:T(128)}, f32[1,128,12,64]{1,3,2,0:T(8,128)}, f32[2,1,512,1536]{3,2,0,1:T(8,128)}, bf16[2,1,512,12,64]{2,4,3,1,0:T(8,128)(2,1)}, s32[2,512]{1...) while((s32[]{:T(128)}, f32[1,128,12,64]{1,3,2,0:T(8,128)}, ...), condition=%wide.region_8.9_spmd.clone, body=%wide.region_7.8_spmd.clone.sunk | while | flops 512720896 | bytes 53467980 | solution.py:232
  171.4 3.3 fusion.200
  174.7 2.9 fusion.201
  188.5 3.3 fusion.200
  191.8 2.9 fusion.201
  203.5 6.9 copy.220
  211.2 5.4 all-gather
  216.7 3.3 convolution_add_fusion.1
  220.0 5.0 convolution_bitcast_fusion
  225.1 9.8 all-gather.26.cloned.1.call-done
  234.8 4.4 fusion.133
  239.2 5.2 fusion.76
  245.4 111.4 %reduce-scatter.18.cloned.1.call-done = f32[1,128,1536]{1,2,0:T(8,128)} async-done(((f32[1,1024,1536]{1,2,0:T(8,128)}), f32[1,128,1536]{1,2,0:T(8,128)}) %reduce-scatter.18.cloned.1.call-update) | async-done | bytes 786448 | tf_op jit(solution)/shard_map/reduce_scatter | solution.py:238
  360.9 4.1 fusion.80
  367.9 155.0 %reduce-scatter.26.cloned.1.call-done = f32[768,384]{0,1:T(8,128)} async-done(((f32[768,3072]{0,1:T(8,128)}), f32[768,384]{0,1:T(8,128)}) %reduce-scatter.26.cloned.1.call-update) | async-done | bytes 1179664 | tf_op jit(solution)/shard_map/reduce_scatter | solution.py:261
  525.6 163.5 %reduce-scatter.24.cloned.1.call-done = f32[768,384]{1,0:T(8,128)} async-done(((f32[768,3072]{1,0:T(8,128)}), f32[768,384]{1,0:T(8,128)}) %reduce-scatter.24.cloned.1.call-update) | async-done | bytes 1179664 | tf_op jit(solution)/shard_map/reduce_scatter | solution.py:260
  689.1 131.6 %reduce-scatter.20.cloned.1.call-done = f32[768,288]{0,1:T(8,128)} async-done(((f32[768,2304]{0,1:T(8,128)}), f32[768,288]{0,1:T(8,128)}) %reduce-scatter.20.cloned.1.call-update) | async-done | bytes 884752 | tf_op jit(solution)/shard_map/reduce_scatter | solution.py:258
  823.4 70.0 %reduce-scatter.22.cloned.1.call-done = f32[768,96]{0,1:T(8,128)} async-done(((f32[768,768]{0,1:T(8,128)}), f32[768,96]{0,1:T(8,128)}) %reduce-scatter.22.cloned.1.call-update) | async-done | bytes 294928 | tf_op jit(solution)/shard_map/reduce_scatter | solution.py:259
  895.3 26.0 %reduce-scatter.34.cloned.1.call-done = f32[192,384]{1,0:T(8,128)} async-done(((f32[768,384]{1,0:T(8,128)}), f32[192,384]{1,0:T(8,128)}) %reduce-scatter.34.cloned.1.call-update) | async-done | bytes 294928
  923.3 26.4 %reduce-scatter.32.cloned.1.call-done = f32[192,384]{1,0:T(8,128)} async-done(((f32[768,384]{1,0:T(8,128)}), f32[192,384]{1,0:T(8,128)}) %reduce-scatter.32.cloned.1.call-update) | async-done | bytes 294928
  951.6 27.0 %reduce-scatter.28.cloned.1.call-done = f32[192,288]{1,0:T(8,128)} async-done(((f32[768,288]{1,0:T(8,128)}), f32[192,288]{1,0:T(8,128)}) %reduce-scatter.28.cloned.1.call-update) | async-done | bytes 221200
  984.6 3.5 copy.226
  988.1 3.5 copy.228
  991.6 10.7 reduce-scatter.30.cloned.1.call-done
  1003.3 33.6 %all_gather.95 = f32[192,768]{0,1:T(8,128)S(1)} all-gather(f32[192,96]{0,1:T(8,128)S(1)} %copy.248), channel_id=1, replica_groups=mesh['ctx'=8,'fsdp'=4] {'ctx'}, dimensions={1}, use_global_device_ids=true | all-gather | bytes 663552 | tf_op jit(solution)/shard_map/all_gather | solution.py:271
  1037.0 33.2 %all-gather.32.cloned.1.call-done = f32[192,3072]{0,1:T(8,128)} async-done(((f32[192,384]{0,1:T(8,128)}), f32[192,3072]{0,1:T(8,128)}) %all-gather.32.cloned.1.call-update) | async-done | bytes 2359312 | tf_op jit(solution)/shard_map/all_gather | solution.py:273
  1070.2 3.3 multiply_add_fusion
  1080.6 8.1 all_gather.99
  1090.9 4.7 fusion.128
  1095.6 36.3 %all-gather.30.cloned.1.call-done = f32[192,3072]{0,1:T(8,128)} async-done(((f32[192,384]{0,1:T(8,128)}), f32[192,3072]{0,1:T(8,128)}) %all-gather.30.cloned.1.call-update) | async-done | bytes 2359312 | tf_op jit(solution)/shard_map/all_gather | solution.py:272
  1131.9 3.3 multiply_add_fusion.1
  1139.6 5.2 fusion.74
  1145.5 39.7 %all-gather.28.cloned.1.call-done = f32[192,2304]{0,1:T(8,128)} async-done(((f32[192,288]{0,1:T(8,128)}), f32[192,2304]{0,1:T(8,128)}) %all-gather.28.cloned.1.call-update) | async-done | bytes 1769488 | tf_op jit(solution)/shard_map/all_gather | solution.py:270
  1192.9 40.9 %all-reduce.9 = (f32[768]{0:T(1024)}, f32[768]{0:T(1024)}, f32[768]{0:T(1024)}, f32[768]{0:T(1024)}, f32[2304]{0:T(1024)}, /*index=5*/f32[768]{0:T(1024)}, f32[3...) all-reduce(f32[768]{0:T(1024)S(1)} %copy-done.68, ...), channel_id=1, replica_groups=mesh['ctx'=8,'fsdp'=4] {'ctx','fsdp'}, use_global_device_ids=true, to_apply=%region_15.16 | all-reduce | flops 9220 | bytes 73760 | tf_op jit(solution)/shard_map/psum | solution.py:285
  1236.4 11.9 all_gather.98
  1252.6 78.6 %all-reduce.19.cloned.1.call-done = bf16[768,768]{1,0:T(8,128)(2,1)} async-done(((bf16[768,768]{1,0:T(8,128)(2,1)}), bf16[768,768]{1,0:T(8,128)(2,1)}) %all-reduce.19.cloned.1.call-update) | async-done | bytes 1179664 | tf_op jit(solution)/shard_map/psum | solution.py:321
  1331.2 4.8 fusion.35
  1336.0 3.1 convolution_convert_fusion.3
  1339.2 79.5 %all-reduce.21.cloned.1.call-done = bf16[768,768]{1,0:T(8,128)(2,1)} async-done(((bf16[768,768]{1,0:T(8,128)(2,1)}), bf16[768,768]{1,0:T(8,128)(2,1)}) %all-reduce.21.cloned.1.call-update) | async-done | bytes 1179664 | tf_op jit(solution)/shard_map/psum | solution.py:321
  1418.8 4.8 fusion.36
  1423.5 3.1 convolution_convert_fusion.2
  1427.0 79.2 %all-reduce.23.cloned.1.call-done = bf16[768,768]{1,0:T(8,128)(2,1)} async-done(((bf16[768,768]{1,0:T(8,128)(2,1)}), bf16[768,768]{1,0:T(8,128)(2,1)}) %all-reduce.23.cloned.1.call-update) | async-done | bytes 1179664 | tf_op jit(solution)/shard_map/psum | solution.py:321
  1506.2 4.8 fusion.37
  1511.0 3.1 convolution_convert_fusion.1
  1514.2 79.5 %all-reduce.25.cloned.1.call-done = bf16[768,768]{1,0:T(8,128)(2,1)} async-done(((bf16[768,768]{1,0:T(8,128)(2,1)}), bf16[768,768]{1,0:T(8,128)(2,1)}) %all-reduce.25.cloned.1.call-update) | async-done | bytes 1179664 | tf_op jit(solution)/shard_map/psum | solution.py:321
  1593.6 4.3 fusion.38
  1599.8 79.5 %all-reduce.27.cloned.1.call-done = bf16[768,768]{1,0:T(8,128)(2,1)} async-done(((bf16[768,768]{1,0:T(8,128)(2,1)}), bf16[768,768]{1,0:T(8,128)(2,1)}) %all-reduce.27.cloned.1.call-update) | async-done | bytes 1179664 | tf_op jit(solution)/shard_map/psum | solution.py:321
  1679.3 5.4 broadcast_select_fusion
  1684.8 55.6 %all-reduce.29.cloned.1.call-done = (bf16[768,384]{1,0:T(8,128)(2,1)}, bf16[768,384]{1,0:T(8,128)(2,1)}, bf16[768,384]{1,0:T(8,128)(2,1)}, bf16[768,384]{1,0:T(8,128)(2,1)}) async-done(((bf16[768,384]{1,0:T(8,128)(2,1)}, bf16[768,384]{1,0:T(8,128)(2,1)}, bf16[768,384]{1,0:T(8,128)(2,1)}, bf16[768,384]{1,0:T(8,128)(2,1)}), (bf16[768,384]{1,0:T(8,128)(2,1)}, bf16[768,384]{1,0:T(8,128)(2,1)}, ...) | async-done | bytes 2359312 | tf_op jit(solution)/shard_map/psum | solution.py:24
  1747.8 4.7 fusion.44
  1755.8 3.5 copy.240
  1761.5 3.5 copy.234
  1767.2 3.1 copy.238
  1787.6 33.3 %all_gather.103 = f32[192,768]{0,1:T(8,128)S(1)} all-gather(f32[192,96]{0,1:T(8,128)S(1)} %copy.231), channel_id=1, replica_groups=mesh['ctx'=8,'fsdp'=4] {'ctx'}, dimensions={1}, use_global_device_ids=true | all-gather | bytes 663552 | tf_op jit(solution)/shard_map/all_gather | solution.py:344
  1824.8 27.7 %all-gather.40.cloned.1.call-done = f32[192,3072]{1,0:T(8,128)} async-done(((f32[192,384]{1,0:T(8,128)}), f32[192,3072]{1,0:T(8,128)}) %all-gather.40.cloned.1.call-update) | async-done | bytes 2359312 | tf_op jit(solution)/shard_map/all_gather | solution.py:345
  1852.5 53.3 %all-gather.42.cloned.1.call-done = f32[192,3072]{1,0:T(8,128)} async-done(((f32[192,384]{1,0:T(8,128)}), f32[192,3072]{1,0:T(8,128)}) %all-gather.42.cloned.1.call-update) | async-done | bytes 2359312 | tf_op jit(solution)/shard_map/all_gather | solution.py:346
  1906.3 3.4 copy.319
  (441 shorter events, 140.2 us)
Async XLA Ops:
  7.2 36.7 %all-gather.16.cloned.1.call-start = ((), (), s32[]{:S(2)}) async-start(), calls=%async_computation.9 | async-start | bytes 4423680 | tf_op jit(solution)/shard_map/all_gather | solution.py:113
  9.9 53.8 %all-gather.22.cloned.1.call-start = ((), (), s32[]{:S(2)}) async-start(), calls=%async_computation.12 | async-start | bytes 1474560 | tf_op jit(solution)/shard_map/all_gather | solution.py:114
  10.7 100.9 %all-gather.18.cloned.1.call-start = ((), (), s32[]{:S(2)}) async-start(), calls=%async_computation.10 | async-start | bytes 1769472 | tf_op jit(solution)/shard_map/all_gather | solution.py:144
  10.9 33.0 %copy-start.54 = (f32[128]{0:T(128)}, f32[128]{0:T(128)S(1)}, u32[]{:S(2)}) copy-start(f32[128]{0:T(128)S(1)} %broadcast_multiply_fusion.6) | copy-start | bytes 1540
  28.6 18.1 copy-start.50
  28.8 15.2 copy-start.60
  30.0 17.1 copy-start.52
  48.5 109.1 %all-gather.20.cloned.1.call-start = ((), (), s32[]{:S(2)}) async-start(), calls=%async_computation.11 | async-start | bytes 1769472 | tf_op jit(solution)/shard_map/all_gather | solution.py:145
  49.3 167.3 %all-gather.24.cloned.1.call-start = ((), (), s32[]{:S(2)}) async-start(), calls=%async_computation.13 | async-start | bytes 5898240 | tf_op jit(solution)/shard_map/all_gather | solution.py:115
  52.4 182.4 %all-gather.26.cloned.1.call-start = ((), (), s32[]{:S(2)}) async-start(), calls=%async_computation.14 | async-start | bytes 5898240 | tf_op jit(solution)/shard_map/all_gather | solution.py:116
  53.7 303.2 %reduce-scatter.18.cloned.1.call-start = ((), (), s32[]{:S(2)}) async-start(), calls=%async_computation.15 | async-start | bytes 7077888 | tf_op jit(solution)/shard_map/reduce_scatter | solution.py:238
  54.2 12.1 copy-start.47
  54.2 12.1 copy-start.48
  54.9 11.5 copy-start.16
  210.5 312.4 %reduce-scatter.26.cloned.1.call-start = ((), (), s32[]{:S(2)}) async-start(), calls=%async_computation.21 | async-start | bytes 10616832 | tf_op jit(solution)/shard_map/reduce_scatter | solution.py:261
  225.0 464.1 %reduce-scatter.24.cloned.1.call-start = ((), (), s32[]{:S(2)}) async-start(), calls=%async_computation.19 | async-start | bytes 10616832 | tf_op jit(solution)/shard_map/reduce_scatter | solution.py:260
  244.4 114.3 %copy-start.53 = (f32[128,8]{0,1:T(8,128)S(1)}, f32[128,8]{0,1:T(8,128)}, u32[]{:S(2)}) copy-start(f32[128,8]{0,1:T(8,128)} %copy-done.52) | copy-start | bytes 12292
  244.4 576.3 %reduce-scatter.20.cloned.1.call-start = ((), (), s32[]{:S(2)}) async-start(), calls=%async_computation.16 | async-start | bytes 7962624 | tf_op jit(solution)/shard_map/reduce_scatter | solution.py:258
  245.4 114.2 %copy-start.20 = (f32[1,128,12,48]{1,3,2,0:T(8,128)}, f32[1,128,12,48]{1,3,2,0:T(8,128)S(1)}, u32[]{:S(2)}) copy-start(f32[1,128,12,48]{1,3,2,0:T(8,128)S(1)} %slice.64) | copy-start | bytes 884740
  365.1 528.3 %reduce-scatter.22.cloned.1.call-start = ((), (), s32[]{:S(2)}) async-start(), calls=%async_computation.18 | async-start | bytes 2654208 | tf_op jit(solution)/shard_map/reduce_scatter | solution.py:259
  367.9 553.4 %reduce-scatter.34.cloned.1.call-start = ((), (), s32[]{:S(2)}) async-start(), calls=%async_computation.36 | async-start | bytes 1474560
  525.6 424.0 %reduce-scatter.32.cloned.1.call-start = ((), (), s32[]{:S(2)}) async-start(), calls=%async_computation.35 | async-start | bytes 1474560
  689.1 289.4 %reduce-scatter.28.cloned.1.call-start = ((), (), s32[]{:S(2)}) async-start(), calls=%async_computation.33 | async-start | bytes 1474560
  823.3 179.0 %reduce-scatter.30.cloned.1.call-start = ((), (), s32[]{:S(2)}) async-start(), calls=%async_computation.34 | async-start | bytes 491520
  895.2 85.2 %copy-start.25 = (f32[192,2304]{1,0:T(8,128)S(1)}, f32[192,2304]{1,0:T(8,128)}, u32[]{:S(2)}) copy-start(f32[192,2304]{1,0:T(8,128)} %param.36) | copy-start | bytes 5308420
  895.3 174.9 %all-gather.32.cloned.1.call-start = ((), (), s32[]{:S(2)}) async-start(), calls=%async_computation.22 | async-start | bytes 3538944 | tf_op jit(solution)/shard_map/all_gather | solution.py:273
  923.2 208.7 %all-gather.30.cloned.1.call-start = ((), (), s32[]{:S(2)}) async-start(), calls=%async_computation.20 | async-start | bytes 3538944 | tf_op jit(solution)/shard_map/all_gather | solution.py:272
  951.5 233.7 %all-gather.28.cloned.1.call-start = ((), (), s32[]{:S(2)}) async-start(), calls=%async_computation.17 | async-start | bytes 2654208 | tf_op jit(solution)/shard_map/all_gather | solution.py:270
  980.4 268.0 %all-gather.36.cloned.1.call-start = ((), (), s32[]{:S(2)}) async-start(), calls=%async_computation.24 | async-start | bytes 1474560 | tf_op jit(solution)/shard_map/all_gather | solution.py:305
  1077.8 170.6 %all-gather.34.cloned.1.call-start = ((), (), s32[]{:S(2)}) async-start(), calls=%async_computation.23 | async-start | bytes 1474560 | tf_op jit(solution)/shard_map/all_gather | solution.py:304
  1079.1 11.8 copy-start.12
  1080.6 9.3 copy-start.31
  1080.6 10.3 copy-start.36
  1080.6 10.3 copy-start.38
  1080.6 10.3 copy-start.40
  1139.6 191.7 %all-reduce.19.cloned.1.call-start = ((), (), s32[]{:S(2)}) async-start(), calls=%async_computation.25 | async-start | bytes 2359296 | tf_op jit(solution)/shard_map/psum | solution.py:321
  1144.8 43.1 %copy-start.14 = (f32[128,768]{1,0:T(8,128)}, f32[128,768]{1,0:T(8,128)S(1)}, u32[]{:S(2)}) copy-start(f32[128,768]{1,0:T(8,128)S(1)} %get-tuple-element.470) | copy-start | bytes 1179652
  1145.5 47.4 %copy-start.49 = (f32[2304]{0:T(1024)S(1)}, f32[2304]{0:T(1024)}, u32[]{:S(2)}) copy-start(f32[2304]{0:T(1024)} %maximum_reduce_fusion) | copy-start | bytes 27652
  1145.5 47.4 %copy-start.66 = (f32[768]{0:T(1024)S(1)}, f32[768]{0:T(1024)}, u32[]{:S(2)}) copy-start(f32[768]{0:T(1024)} %get-tuple-element.455) | copy-start | bytes 9220
  1145.5 47.4 %copy-start.67 = (f32[768]{0:T(1024)S(1)}, f32[768]{0:T(1024)}, u32[]{:S(2)}) copy-start(f32[768]{0:T(1024)} %get-tuple-element.361) | copy-start | bytes 9220
  1145.5 47.4 %copy-start.68 = (f32[768]{0:T(1024)S(1)}, f32[768]{0:T(1024)}, u32[]{:S(2)}) copy-start(f32[768]{0:T(1024)} %get-tuple-element.370) | copy-start | bytes 9220
  1145.5 47.4 %copy-start.73 = (f32[3072]{0:T(1024)S(1)}, f32[3072]{0:T(1024)}, u32[]{:S(2)}) copy-start(f32[3072]{0:T(1024)} %get-tuple-element.472) | copy-start | bytes 36868
  1145.5 47.4 %copy-start.80 = (f32[768]{0:T(1024)S(1)}, f32[768]{0:T(1024)}, u32[]{:S(2)}) copy-start(f32[768]{0:T(1024)} %get-tuple-element.367) | copy-start | bytes 9220
  1189.3 59.0 %copy-start.28 = (f32[768,96]{1,0:T(8,128)S(1)}, f32[768,96]{1,0:T(8,128)}, u32[]{:S(2)}) copy-start(f32[768,96]{1,0:T(8,128)} %all_gather.99) | copy-start | bytes 884740
  1252.6 166.2 %all-reduce.21.cloned.1.call-start = ((), (), s32[]{:S(2)}) async-start(), calls=%async_computation.26 | async-start | bytes 2359296 | tf_op jit(solution)/shard_map/psum | solution.py:321
  1336.0 82.7 %copy-start.23 = (bf16[768,384]{1,0:T(8,128)(2,1)S(1)}, bf16[768,384]{1,0:T(8,128)(2,1)}, u32[]{:S(2)}) copy-start(bf16[768,384]{1,0:T(8,128)(2,1)} %fusion.35) | copy-start | bytes 1769476
  1339.2 167.1 %all-reduce.23.cloned.1.call-start = ((), (), s32[]{:S(2)}) async-start(), calls=%async_computation.27 | async-start | bytes 2359296 | tf_op jit(solution)/shard_map/psum | solution.py:321
  1423.5 82.7 %copy-start.24 = (bf16[768,384]{1,0:T(8,128)(2,1)S(1)}, bf16[768,384]{1,0:T(8,128)(2,1)}, u32[]{:S(2)}) copy-start(bf16[768,384]{1,0:T(8,128)(2,1)} %fusion.36) | copy-start | bytes 1769476
  1426.7 167.0 %all-reduce.25.cloned.1.call-start = ((), (), s32[]{:S(2)}) async-start(), calls=%async_computation.28 | async-start | bytes 2359296 | tf_op jit(solution)/shard_map/psum | solution.py:321
  1514.1 165.2 %all-reduce.27.cloned.1.call-start = ((), (), s32[]{:S(2)}) async-start(), calls=%async_computation.29 | async-start | bytes 2359296 | tf_op jit(solution)/shard_map/psum | solution.py:321
  1599.8 140.7 %all-reduce.29.cloned.1.call-start = ((), (), s32[]{:S(2)}) async-start(), calls=%async_computation.37 | async-start | bytes 4718592 | tf_op jit(solution)/shard_map/psum | solution.py:24
  1684.7 59.7 %copy-start.82 = (bf16[768]{0:T(1024)(128)(2,1)S(1)}, bf16[768]{0:T(1024)(128)(2,1)}, u32[]{:S(2)}) copy-start(bf16[768]{0:T(1024)(128)(2,1)} %get-tuple-element.407) | copy-start | bytes 4612
  1684.7 59.7 %copy-start.81 = (bf16[768]{0:T(1024)(128)(2,1)S(1)}, bf16[768]{0:T(1024)(128)(2,1)}, u32[]{:S(2)}) copy-start(bf16[768]{0:T(1024)(128)(2,1)} %get-tuple-element.408) | copy-start | bytes 4612
  1684.7 59.7 %copy-start.42 = (bf16[12,128,64]{1,2,0:T(8,128)(2,1)S(1)}, bf16[12,128,64]{1,2,0:T(8,128)(2,1)}, u32[]{:S(2)}) copy-start(bf16[12,128,64]{1,2,0:T(8,128)(2,1)} %get-tuple-element.469) | copy-start | bytes 589828
  1684.7 137.2 %all-gather.38.cloned.1.call-start = ((), (), s32[]{:S(2)}) async-start(), calls=%async_computation.30 | async-start | bytes 2654208 | tf_op jit(solution)/shard_map/all_gather | solution.py:343
  1742.5 110.0 %all-gather.40.cloned.1.call-start = ((), (), s32[]{:S(2)}) async-start(), calls=%async_computation.31 | async-start | bytes 2654208 | tf_op jit(solution)/shard_map/all_gather | solution.py:345
  1744.3 161.4 %all-gather.42.cloned.1.call-start = ((), (), s32[]{:S(2)}) async-start(), calls=%async_computation.32 | async-start | bytes 2654208 | tf_op jit(solution)/shard_map/all_gather | solution.py:346
  1767.2 7.0 copy-start.75
  1767.2 8.3 copy-start.65
  1767.2 9.6 copy-start.79
  1767.2 10.9 copy-start.64
  1767.2 12.2 copy-start.86
  1767.2 12.8 copy-start.7
  1780.1 125.7 %copy-start.74 = (f32[192]{0:T(256)}, f32[192]{0:T(256)S(1)}, u32[]{:S(2)}) copy-start(f32[192]{0:T(256)S(1)} %get-tuple-element.685) | copy-start | bytes 2308
  (76 other events, 228.7 us)
Sparse Core Ops, SparseCore 0:
  10.2 33.7 all-gather.15
  46.1 17.5 all-gather.21
  66.3 45.2 all-gather.17
  114.1 43.4 all-gather.19
  159.6 35.6 all-gather.23
  197.3 37.5 all-gather.25
  238.4 118.3 reduce-scatter.17
  360.4 162.4 reduce-scatter.25
  526.5 162.5 reduce-scatter.23
  692.6 128.0 reduce-scatter.19
  825.2 68.0 reduce-scatter.21
  896.5 24.7 reduce-scatter.33
  923.9 25.7 reduce-scatter.31
  952.8 25.7 reduce-scatter.27
  981.4 20.8 reduce-scatter.29
  1005.0 65.1 all-gather.31
  1072.8 59.0 all-gather.29
  1134.5 50.6 all-gather.27
  1187.4 16.5 all-gather.35
  1205.9 17.5 all-gather.33
  1252.7 78.5 all-reduce.18
  1339.3 79.4 all-reduce.20
  1426.8 79.3 all-reduce.22
  1514.2 79.3 all-reduce.24
  1599.9 79.3 all-reduce.26
  1684.8 55.5 all-reduce.28
  1743.3 53.3 all-gather.37
  1799.1 53.3 all-gather.39
  1854.8 50.8 all-gather.41
where the time goes:
time: 1920 us
  waiting for transfers between devices  1480 us (77%)
  blocking collectives  147 us (8%)
  matrix products  108 us (6%)
  local copies, waits for them, and re-layouts  96.3 us (5%)
  other arithmetic  56.7 us (3%)
  between operations  24.8 us (1%)
    psum x5, waiting for transfers between devices, local(): lax.psum(partial_value.astype(jnp.bfloat16), 'ctx').astype(jnp.float32)  396 us
    reduce_scatter x1, waiting for transfers between devices, local(): lax.psum_scatter(up_local, 'ctx', scatter_dimension=1, tiled=True)  163 us
    reduce_scatter x1, waiting for transfers between devices, local(): lax.psum_scatter(down_local, 'ctx', scatter_dimension=1, tiled=True)  155 us
    reduce_scatter x1, waiting for transfers between devices, local(): lax.psum_scatter(heads_local, 'ctx', scatter_dimension=1, tiled=True)  132 us
    reduce_scatter x1, waiting for transfers between devices, local(): home = lax.psum_scatter(key_grads, 'ctx', scatter_dimension=1, tiled=True)  111 us
    unnamed x33, waiting for transfers between devices  90.5 us
    reduce_scatter x1, waiting for transfers between devices, local(): lax.psum_scatter(output_local, 'ctx', scatter_dimension=1, tiled=True)  70 us
    unnamed x240, local copies, waits for them, and re-layouts  65.4 us
  transfers between devices with their start and end apart: 29, of which 25 were waited for; matrix products, arithmetic and copies ran while one was open for 11% of the time, Pallas kernels for 0%

commit v1 on v0

--- a/solution.py
+++ b/solution.py
@@ -3,6 +3,8 @@
 import jax
 import jax.numpy as jnp
 from jax import lax
+from jax.experimental import pallas as pl
+from jax.experimental.pallas import tpu as pltpu
 from jax.sharding import PartitionSpec as P
 
 HEADS = 12
@@ -76,7 +78,7 @@
     )
 
 
-def local(
+def local_general(
     residual_in,
     cotangent,
     group_order,
@@ -401,6 +403,530 @@
     )
 
 
+Y_PLACES = 2
+Z_PLACES = 4
+CTX = Y_PLACES * Z_PLACES
+SHARDS = 4
+
+
+def swap(x, axis, offset):
+    count = lax.axis_size(axis)
+    return lax.ppermute(x, axis, [(i, i ^ offset) for i in range(count)])
+
+
+def pick(x, index, dim=0):
+    return lax.dynamic_index_in_dim(x, index, dim, keepdims=False)
+
+
+def in_order(pieces, place):
+    stacked = jnp.stack(pieces)
+    return jnp.stack([pick(stacked, place ^ i) for i in range(len(pieces))])
+
+
+def spread(x, place):
+    return [pick(x, place)] + [swap(pick(x, place ^ k), "fsdp", k) for k in range(1, SHARDS)]
+
+
+def gather_ctx(x):
+    along = [x] + [swap(x, "ctx", 2 * k) for k in range(1, Z_PLACES)]
+    pieces = []
+    for piece in along:
+        pieces += [piece, swap(piece, "ctx", 1)]
+    return pieces
+
+
+def scatter_ctx(x, ctx_place, dim):
+    single, half = jnp.float32, jnp.bfloat16
+    y, z = ctx_place % Y_PLACES, ctx_place // Y_PLACES
+    x = x.reshape(x.shape[:dim] + (Z_PLACES, Y_PLACES) + x.shape[dim + 1 :])
+    sent = swap(pick(x, 1 - y, dim + 1).astype(half), "ctx", 1)
+    kept = pick(x, y, dim + 1) + sent.astype(single)
+    total = pick(kept, z, dim)
+    for k in range(1, Z_PLACES):
+        total = total + swap(pick(kept, z ^ k, dim).astype(half), "ctx", 2 * k).astype(single)
+    return total
+
+
+def attention_kernel(recv_ref, place_row_ref, place_col_ref, place_half_ref, out_ref):
+    single, half = jnp.float32, jnp.bfloat16
+    scale = 1.0 / math.sqrt(HD)
+    rows = 128
+    length = CTX * rows
+    place_row = place_row_ref[...]
+
+    def run(query, keys, values, outer, places, step):
+        key_sum = jnp.zeros((length, HD), single)
+        value_sum = jnp.zeros((length, HD), single)
+        mixed_all, query_all = [], []
+        for at in range(0, query.shape[0], step):
+            one = query[at : at + step]
+            back = outer[at : at + step]
+            score = (
+                lax.dot_general(one, keys, (((1,), (1,)), ((), ())), preferred_element_type=single)
+                * scale
+            )
+            allowed = place_row <= places[at : at + step]
+            score = jnp.where(allowed, score, neg_large)
+            peak = jnp.max(score, axis=-1, keepdims=True)
+            weights = jnp.where(allowed, jnp.exp(score - peak), 0.0)
+            total = jnp.sum(weights, axis=-1, keepdims=True)
+            prob = weights * (1.0 / total)
+            prob_half = prob.astype(half)
+            mixed = jnp.dot(prob_half, values, preferred_element_type=single).astype(half)
+            delta = jnp.sum(
+                back.astype(single) * mixed.astype(single), axis=-1, keepdims=True
+            )
+            prob_grad = lax.dot_general(
+                back, values, (((1,), (1,)), ((), ())), preferred_element_type=single
+            )
+            score_delta = (prob * (prob_grad - delta)).astype(half)
+            query_grad = jnp.dot(score_delta, keys, preferred_element_type=single) * scale
+            key_sum += lax.dot_general(
+                score_delta, one, (((0,), (0,)), ((), ())), preferred_element_type=single
+            )
+            value_sum += lax.dot_general(
+                prob_half, back, (((0,), (0,)), ((), ())), preferred_element_type=single
+            )
+            mixed_all.append(mixed)
+            query_all.append(query_grad.astype(half))
+        return (
+            jnp.concatenate(mixed_all, axis=0),
+            jnp.concatenate(query_all, axis=0),
+            (key_sum * scale).astype(half),
+            value_sum.astype(half),
+        )
+
+    first = recv_ref[:, 0:128, :].reshape(length, 128)
+    second = recv_ref[:, 128:256, :].reshape(length, 128)
+    mixed, query_grad, key_grad, value_grad = run(
+        first[:, :HD], first[:, HD:], second[:, :HD], second[:, HD:], place_col_ref[...], 256
+    )
+    out_ref[:, 0:128, :] = jnp.concatenate([mixed, query_grad], axis=1).reshape(CTX, rows, 128)
+    out_ref[:, 128:256, :] = jnp.concatenate([key_grad, value_grad], axis=1).reshape(
+        CTX, rows, 128
+    )
+    third = recv_ref[:, 256:384, :].reshape(length, 128)
+    fourth = recv_ref[:, 384:448, :].reshape(length // 2, 128)
+    mixed, query_grad, key_grad, value_grad = run(
+        fourth[:, :HD], third[:, :HD], third[:, HD:], fourth[:, HD:], place_half_ref[...], 256
+    )
+    out_ref[:, 256:384, :] = jnp.concatenate([key_grad, value_grad], axis=1).reshape(
+        CTX, rows, 128
+    )
+    out_ref[:, 384:448, :] = jnp.concatenate([mixed, query_grad], axis=1).reshape(
+        CTX, rows // 2, 128
+    )
+
+
+def attention(recv, places, y):
+    length = places.shape[0]
+    halves = pick(places.reshape(CTX, Y_PLACES, length // CTX // Y_PLACES), y, 1).reshape(-1)
+    return pl.pallas_call(
+        attention_kernel,
+        out_shape=jax.ShapeDtypeStruct(recv.shape, recv.dtype),
+        compiler_params=pltpu.CompilerParams(vmem_limit_bytes=48 * 1024 * 1024),
+        cost_estimate=pl.CostEstimate(
+            flops=7 * 2 * 1536 * 1024 * 128, bytes_accessed=2 * recv.size * 2, transcendentals=1536 * 1024
+        ),
+        name="attention",
+    )(recv, places[None, :], places[:, None], halves[:, None])
+
+
+def moment_kernel(where_ref, grads_ref, *refs):
+    at = 0
+    for which in range(4):
+        moment_ref, grad_out, moment_out = refs[which], refs[4 + which], refs[8 + which]
+        cols = moment_ref.shape[1]
+        grad = grads_ref[0, :, at : at + cols].astype(jnp.float32)
+        grad_out[...] = grad
+        moment_out[...] = mom_rate * moment_ref[...] + grad
+        at += cols
+
+
+def write_moments(grads, moments, ctx_place):
+    rows = moments[0].shape[0] // CTX
+    blocks = [pl.BlockSpec((rows, m.shape[1]), lambda i, where: (i, 0)) for m in moments]
+    shapes = [jax.ShapeDtypeStruct(m.shape, m.dtype) for m in moments]
+    out = pl.pallas_call(
+        moment_kernel,
+        grid_spec=pltpu.PrefetchScalarGridSpec(
+            num_scalar_prefetch=1,
+            grid=(CTX,),
+            in_specs=[
+                pl.BlockSpec((1,) + grads.shape[1:], lambda i, where: (i ^ where[0], 0, 0))
+            ]
+            + blocks,
+            out_specs=blocks + blocks,
+        ),
+        out_shape=shapes + shapes,
+        compiler_params=pltpu.CompilerParams(vmem_limit_bytes=32 * 1024 * 1024),
+        name="moments",
+    )(ctx_place.reshape(1), grads, *moments)
+    return out[:4], out[4:]
+
+
+def weight_kernel(where_ref, *refs):
+    for which in range(4):
+        ortho_ref, weight_ref, out_ref = refs[which], refs[4 + which], refs[8 + which]
+        cols = weight_ref.shape[1]
+        rate = step_rates[which] * math.sqrt(cols)
+        out_ref[...] = weight_ref[...] - rate * ortho_ref[0, 0, :, :cols].astype(jnp.float32)
+
+
+def write_weights(ortho, weights, ctx_place, shard_place):
+    rows = weights[0].shape[0] // CTX
+    blocks = [pl.BlockSpec((rows, w.shape[1]), lambda i, where: (i, 0)) for w in weights]
+
+    def source(which):
+        return pl.BlockSpec(
+            (1, 1) + ortho.shape[2:], lambda i, where: (where[1] ^ which, i ^ where[0], 0, 0)
+        )
+
+    return pl.pallas_call(
+        weight_kernel,
+        grid_spec=pltpu.PrefetchScalarGridSpec(
+            num_scalar_prefetch=1,
+            grid=(CTX,),
+            in_specs=[source(which) for which in range(4)] + blocks,
+            out_specs=blocks,
+        ),
+        out_shape=[jax.ShapeDtypeStruct(w.shape, w.dtype) for w in weights],
+        compiler_params=pltpu.CompilerParams(vmem_limit_bytes=32 * 1024 * 1024),
+        name="weights",
+    )(jnp.stack([ctx_place, shard_place]), ortho, ortho, ortho, ortho, *weights)
+
+
+def local_fast(
+    residual_in,
+    cotangent,
+    group_order,
+    gain_first,
+    shift_first,
+    gain_second,
+    shift_second,
+    heads_weight,
+    heads_bias,
+    output_weight,
+    output_bias,
+    up_weight,
+    up_bias,
+    down_weight,
+    down_bias,
+    heads_moment,
+    output_moment,
+    up_moment,
+    down_moment,
+):
+    single = jnp.float32
+    half = jnp.bfloat16
+    ctx_place = lax.axis_index("ctx")
+    shard_place = lax.axis_index("fsdp")
+    y, z = ctx_place % Y_PLACES, ctx_place // Y_PLACES
+    seqs, rows, width = residual_in.shape
+    length = rows * CTX
+    group = rows // 2
+    part = width // SHARDS
+    hidden = up_weight.shape[1]
+    hidden_part = hidden // SHARDS
+    strip = part // CTX
+
+    small = jnp.zeros((16, width), half)
+    small = small.at[0].set(
+        jnp.concatenate([gain_first, shift_first, gain_second, shift_second]).astype(half)
+    )
+    small = small.at[1, : 2 * part].set(jnp.concatenate([output_bias, down_bias]).astype(half))
+    small = small.at[2, : 3 * part].set(heads_bias.astype(half))
+    packed = jnp.concatenate([residual_in[0], cotangent[0].astype(half), small], axis=0)
+    packs = [packed] + [swap(packed, "fsdp", k) for k in range(1, SHARDS)]
+    heads_split = jnp.moveaxis(
+        heads_weight.astype(half).reshape(part, 3, SHARDS, part), 2, 0
+    ).reshape(SHARDS, part, 3 * part)
+    heads_block = in_order(spread(heads_split, shard_place), shard_place).reshape(width, 3 * part)
+    up_split = jnp.moveaxis(up_weight.astype(half).reshape(part, SHARDS, hidden_part), 1, 0)
+    down_split = jnp.moveaxis(down_weight.astype(half).reshape(part, SHARDS, hidden_part), 1, 0)
+    mlp_split = jnp.concatenate([up_split, down_split], axis=-1)
+    mlp_block = in_order(spread(mlp_split, shard_place), shard_place).reshape(
+        width, 2 * hidden_part
+    )
+    up_block, down_block = mlp_block[:, :hidden_part], mlp_block[:, hidden_part:]
+    output_block = output_weight.astype(half)
+
+    tokens = jnp.stack([p[:rows] for p in packs])
+    grad_half = jnp.stack([p[rows : 2 * rows] for p in packs]).reshape(SHARDS * rows, width)
+    vectors = in_order([p[2 * rows :] for p in packs], shard_place).astype(single)
+    gain_one, shift_one, gain_two, shift_two = [
+        vectors[:, 0, i * part : (i + 1) * part].reshape(width) for i in range(4)
+    ]
+    output_shift, down_shift = [
+        vectors[:, 1, i * part : (i + 1) * part].reshape(width) for i in range(2)
+    ]
+    heads_shift = pick(
+        vectors[:, 2, : 3 * part].reshape(3, SHARDS, part), shard_place, 1
+    ).reshape(3 * part)
+    up_shift = up_bias.astype(half).astype(single)
+
+    inputs = tokens.astype(single).reshape(SHARDS * rows, width)
+    average = jnp.mean(inputs, axis=-1, keepdims=True)
+    centred = inputs - average
+    variance = jnp.mean(centred * centred, axis=-1, keepdims=True)
+    inverse = lax.rsqrt(variance + norm_eps)
+    normed = centred * inverse
+    first_in = (normed * gain_one + shift_one).astype(half)
+    second_in = (normed * gain_two + shift_two).astype(half)
+
+    projected = jnp.dot(first_in, heads_block, preferred_element_type=single) + heads_shift
+    places = slot_places(group_order, 0, length, group)
+    query_places = slot_places(group_order, ctx_place * rows, rows, group)
+    cosine, sine = rotary_tables(query_places)
+    rest = HD - ROT
+    turn_cos = jnp.concatenate([cosine, cosine, jnp.ones((rows, rest), single)], axis=1)
+    turn_sin = jnp.concatenate([sine, sine, jnp.zeros((rows, rest), single)], axis=1)
+    turn_cos = jnp.tile(turn_cos, (SHARDS, 2 * part // HD))
+    turn_sin = jnp.tile(turn_sin, (SHARDS, 2 * part // HD))
+    lane = jnp.arange(2 * part)
+    inside = lane % HD
+    other = jnp.where(inside < ROT // 2, lane + ROT // 2, lane - ROT // 2)
+    sign = jnp.where(inside < ROT // 2, -1.0, 1.0) * (inside < ROT)
+    partner = jnp.where(lane[:, None] == other[None, :], sign[None, :], 0.0).astype(single)
+
+    def turned(x, direction):
+        moved = jnp.dot(x, partner, precision=lax.Precision.HIGHEST, preferred_element_type=single)
+        return x * turn_cos + direction * (moved * turn_sin)
+
+    turned_half = turned(projected[:, : 2 * part], 1.0).astype(half)
+    attn_delta = lax.dot_general(
+        grad_half, output_block, (((1,), (1,)), ((), ())), preferred_element_type=single
+    ).astype(half)
+    query = turned_half[:, :part].reshape(SHARDS, rows, part)
+    keys = turned_half[:, part:].reshape(SHARDS, rows, part)
+    values = projected[:, 2 * part :].astype(half).reshape(SHARDS, rows, part)
+    outer = attn_delta.reshape(SHARDS, rows, part)
+
+    def beside(a, b, head):
+        cut = slice(head * HD, (head + 1) * HD)
+        return jnp.concatenate([a[..., cut], b[..., cut]], axis=-1)
+
+    shared_rows = beside(query, outer, 2).reshape(SHARDS, Y_PLACES, rows // 2, 2 * HD)
+    shared_keys = beside(keys, values, 2)
+    payload = jnp.stack(
+        [
+            jnp.concatenate(
+                [
+                    beside(query, keys, head),
+                    beside(values, outer, head),
+                    shared_keys,
+                    shared_rows[:, head],
+                ],
+                axis=1,
+            )
+            for head in range(Y_PLACES)
+        ],
+        axis=1,
+    ).reshape(CTX, 3 * rows + rows // 2, 2 * HD)
+    sent = lax.all_to_all(payload, "ctx", 0, 0)
+    done = attention(sent, places, y)
+    back = lax.all_to_all(done, "ctx", 0, 0).reshape(
+        Z_PLACES, Y_PLACES, 3 * rows + rows // 2, 2 * HD
+    )
+
+    up_pre = jnp.dot(second_in, up_block, preferred_element_type=single) + up_shift
+    active = gelu_value(up_pre).astype(half)
+    up_delta = jnp.dot(grad_half, down_block, preferred_element_type=single) * gelu_slope(up_pre)
+    up_half = up_delta.astype(half)
+
+    def over_tokens(a, b):
+        return lax.dot_general(a, b, (((0,), (0,)), ((), ())), preferred_element_type=single)
+
+    def over_columns(a, b):
+        return lax.dot_general(a, b, (((1,), (1,)), ((), ())), preferred_element_type=single)
+
+    up_local = over_tokens(second_in, up_half).reshape(SHARDS, CTX, strip, hidden_part)
+    down_local = over_tokens(grad_half, active).reshape(SHARDS, CTX, strip, hidden_part)
+    up_strip = scatter_ctx(up_local, ctx_place, 1)
+    down_strip = scatter_ctx(down_local, ctx_place, 1)
+    mlp_part = over_columns(active, down_block)
+    second_part = over_columns(up_half, up_block)
+
+    early, late = back[..., :HD], back[..., HD:]
+    attn = jnp.concatenate(
+        [early[:, 0, :rows], early[:, 1, :rows], early[:, :, 3 * rows :].reshape(SHARDS, rows, HD)],
+        axis=-1,
+    ).reshape(SHARDS * rows, part)
+    query_grad = jnp.concatenate(
+        [late[:, 0, :rows], late[:, 1, :rows], late[:, :, 3 * rows :].reshape(SHARDS, rows, HD)],
+        axis=-1,
+    ).astype(single)
+    wide = back[:, :, rows : 3 * rows].astype(single)
+    shared = wide[:, 0, rows:] + wide[:, 1, rows:]
+    key_grad = jnp.concatenate(
+        [wide[:, 0, :rows, :HD], wide[:, 1, :rows, :HD], shared[..., :HD]], axis=-1
+    )
+    value_grad = jnp.concatenate(
+        [wide[:, 0, :rows, HD:], wide[:, 1, :rows, HD:], shared[..., HD:]], axis=-1
+    )
+    turned_grad = turned(
+        jnp.concatenate([query_grad, key_grad], axis=-1).reshape(SHARDS * rows, 2 * part), -1.0
+    )
+    heads_delta = jnp.concatenate([turned_grad, value_grad.reshape(SHARDS * rows, part)], axis=-1)
+    heads_half = heads_delta.astype(half)
+    heads_local = over_tokens(first_in, heads_half).reshape(SHARDS, CTX, strip, 3 * part)
+    output_local = over_tokens(attn, grad_half).reshape(CTX, strip, width)
+    heads_strip = scatter_ctx(heads_local, ctx_place, 1)
+    output_strip = scatter_ctx(output_local, ctx_place, 0)
+    output_part = jnp.dot(attn, output_block, preferred_element_type=single)
+    first_part = over_columns(heads_half, heads_block)
+
+    def home(x):
+        x = x.reshape(SHARDS, rows, width)
+        total = x[0]
+        for k in range(1, SHARDS):
+            total = total + swap(x[k].astype(half), "fsdp", k).astype(single)
+        return total
+
+    mine = inputs[:rows]
+    block_out = (mine + (home(output_part + mlp_part) + output_shift + down_shift)).astype(half)
+    second_delta = home(second_part)
+    first_delta = home(first_part)
+    my_normed, my_inverse = normed[:rows], inverse[:rows]
+    input_grad = (
+        cotangent[0]
+        + norm_back(first_delta, my_normed, my_inverse, gain_one)
+        + norm_back(second_delta, my_normed, my_inverse, gain_two)
+    )
+
+    strips = jnp.concatenate([heads_strip, up_strip, down_strip], axis=-1).astype(half)
+    whole = in_order(spread(strips, shard_place), shard_place)
+    heads_grad = jnp.moveaxis(
+        whole[..., : 3 * part].reshape(SHARDS, strip, 3, part), 0, 2
+    ).reshape(strip, 3 * width)
+    up_grad = jnp.moveaxis(whole[..., 3 * part : 3 * part + hidden_part], 0, 1).reshape(
+        strip, hidden
+    )
+    down_grad = jnp.moveaxis(whole[..., 3 * part + hidden_part :], 0, 1).reshape(strip, hidden)
+    strip_grads = (heads_grad, output_strip.astype(half), up_grad, down_grad)
+    moments_all = (heads_moment, output_moment, up_moment, down_moment)
+    weights_all = (heads_weight, output_weight, up_weight, down_weight)
+    nests = []
+    for which in range(4):
+        grad = strip_grads[which].astype(single)
+        moment = mom_rate * lax.dynamic_slice_in_dim(
+            moments_all[which], ctx_place * strip, strip, 0
+        ) + grad
+        nest = (grad + mom_rate * moment).astype(half)
+        nests.append(jnp.pad(nest, ((0, 0), (0, hidden - nest.shape[1]))))
+    owned = jnp.stack(spread(jnp.stack(nests), shard_place))
+    nest = jnp.stack(gather_ctx(owned)).reshape(width, hidden)
+    grads_all = jnp.stack(gather_ctx(jnp.concatenate(strip_grads, axis=-1)))
+    full_grads, new_moments = write_moments(grads_all, moments_all, ctx_place)
+
+    wide_nest = nest.astype(single)
+    size = jnp.sqrt(jnp.sum(wide_nest * wide_nest))
+    ortho = (wide_nest / (size + 1e-07)).astype(half)
+    for turn in range(NS_ITERS):
+        gram = over_columns(ortho, ortho).astype(half)
+        mix = (
+            schulz_coeffs[1] * gram.astype(single)
+            + schulz_coeffs[2] * jnp.dot(gram, gram, preferred_element_type=single)
+        ).astype(half)
+        ortho = (
+            schulz_coeffs[0] * ortho.astype(single)
+            + jnp.dot(mix, ortho, preferred_element_type=single)
+        ).astype(half)
+    ortho = ortho.reshape(CTX, SHARDS, strip, hidden)
+    arrived = jnp.stack(
+        [ortho[:, 0]] + [swap(ortho[:, k], "fsdp", k) for k in range(1, SHARDS)]
+    )
+    new_weights = write_weights(arrived, weights_all, ctx_place, shard_place)
+
+    heads_sum = jnp.sum(heads_delta, axis=0).reshape(3, 1, part)
+    heads_sum = lax.dynamic_update_slice(
+        jnp.zeros((3, SHARDS, part), single), heads_sum, (0, shard_place, 0)
+    ).reshape(3 * width)
+    up_sum = lax.dynamic_update_slice(
+        jnp.zeros((hidden,), single), jnp.sum(up_delta, axis=0), (shard_place * hidden_part,)
+    )
+    sums = lax.psum(
+        jnp.concatenate(
+            [
+                jnp.sum(first_delta * my_normed, axis=0),
+                jnp.sum(first_delta, axis=0),
+                jnp.sum(second_delta * my_normed, axis=0),
+                jnp.sum(second_delta, axis=0),
+                jnp.sum(cotangent[0], axis=0),
+                heads_sum,
+                up_sum,
+            ]
+        ),
+        ("ctx", "fsdp"),
+    )
+    pieces = [sums[i * width : (i + 1) * width] for i in range(5)]
+    heads_total = sums[5 * width : 8 * width]
+    up_total = sums[8 * width :]
+    vector_values = (
+        gain_first,
+        shift_first,
+        gain_second,
+        shift_second,
+        heads_bias,
+        output_bias,
+        up_bias,
+        down_bias,
+    )
+    vector_grads = (
+        pieces[0],
+        pieces[1],
+        pieces[2],
+        pieces[3],
+        heads_total,
+        pieces[4],
+        up_total,
+        pieces[4],
+    )
+    grad_shards = []
+    new_shards = []
+    for which in range(8):
+        size_here = vector_values[which].shape[0]
+        whole_grad = vector_grads[which]
+        shard = lax.dynamic_slice_in_dim(whole_grad, shard_place * size_here, size_here)
+        grad_shards.append(shard)
+        new_shards.append(
+            vector_values[which]
+            - vector_rate * shard * lax.rsqrt(jnp.mean(whole_grad * whole_grad) + norm_eps)
+        )
+    return (
+        block_out[None],
+        input_grad[None],
+        grad_shards[0],
+        grad_shards[1],
+        grad_shards[2],
+        grad_shards[3],
+        full_grads[0],
+        grad_shards[4],
+        full_grads[1],
+        grad_shards[5],
+        full_grads[2],
+        grad_shards[6],
+        full_grads[3],
+        grad_shards[7],
+        new_shards[0],
+        new_shards[1],
+        new_shards[2],
+        new_shards[3],
+        new_weights[0],
+        new_shards[4],
+        new_weights[1],
+        new_shards[5],
+        new_weights[2],
+        new_shards[6],
+        new_weights[3],
+        new_shards[7],
+        new_moments[0],
+        new_moments[1],
+        new_moments[2],
+        new_moments[3],
+    )
+
+
 def solution(mesh):
     in_specs = (
         P("fsdp", "ctx", None),
@@ -455,4 +981,7 @@
         P("fsdp", None),
         P("fsdp", None),
     )
-    return jax.shard_map(local, mesh=mesh, in_specs=in_specs, out_specs=out_specs, check_vma=False)
+    sizes = dict(mesh.shape)
+    fits = sizes["ctx"] == 8 and sizes["fsdp"] == 4
+    chosen = local_fast if fits else local_general
+    return jax.shard_map(chosen, mesh=mesh, in_specs=in_specs, out_specs=out_specs, check_vma=False)

time: 1920 us -> 706 us (0.37)
  waiting for transfers between devices: 1480 us -> 177 us
  blocking collectives: 147 us -> 40.8 us
  starting transfers between devices: 1.92 us -> 68.5 us
  other arithmetic: 56.7 us -> 108 us
  local copies, waits for them, and re-layouts: 96.3 us -> 142 us
  Pallas kernels: 0 us -> 24.1 us
    reduce_scatter x5 -> x0, waiting for transfers between devices: 631 us -> none  [the longest x1 163 us: local(): lax.psum_scatter(up_local, 'ctx', scatter_dimension=1, tiled=True)]
    psum x6 -> x0, waiting for transfers between devices: 452 us -> none  [the longest x5 396 us: local(): lax.psum(partial_value.astype(jnp.bfloat16), 'ctx').astype(jnp.float32)]
    all_gather x14 -> x0, waiting for transfers between devices: 309 us -> none  [the longest x1 53.3 us: local(): lax.all_gather(updated[3], 'ctx', axis=1, tiled=True)]
    ppermute x0 -> x57, waiting for transfers between devices: none -> 177 us  [swap(): return lax.ppermute(x, axis, [(i, i ^ offset) for i in range(count)])]
    all_gather x5 -> x0, blocking collectives: 92.3 us -> none  [the longest x1 33.6 us: local(): lax.all_gather(parts[1], 'ctx', axis=1, tiled=True)]
    unnamed x33 -> x0, waiting for transfers between devices: 90.5 us -> none
    ppermute x0 -> x57, starting transfers between devices: none -> 57.7 us  [swap(): return lax.ppermute(x, axis, [(i, i ^ offset) for i in range(count)])]
    unnamed x240 -> x188, local copies, waits for them, and re-layouts: 65.4 us -> 31.7 us
  transfers between devices with their start and end apart: 29 -> 59, of which waited for: 25 -> 23; matrix products, arithmetic and copies ran while one was open for 11% -> 48% of each run, Pallas kernels for 0% -> 3%
where the time goes in v1:
time: 706 us; the launch traced here: 694 us
  waiting for transfers between devices  177 us (25%)
  local copies, waits for them, and re-layouts  142 us (20%)
  matrix products  125 us (18%)
  other arithmetic  108 us (15%)
  starting transfers between devices  68.5 us (10%)
  blocking collectives  40.8 us (6%)
  Pallas kernels  24.1 us (3%)
  between operations  8.01 us (1%)
    ppermute x57, waiting for transfers between devices, swap(): return lax.ppermute(x, axis, [(i, i ^ offset) for i in range(count)])  177 us
    dot_general x5, matrix products, local_fast(): jnp.dot(mix, ortho, preferred_element_type=single)  63.3 us
    ppermute x57, starting transfers between devices, swap(): return lax.ppermute(x, axis, [(i, i ^ offset) for i in range(count)])  57.7 us
    dot_general x8, matrix products, over_columns(): lax.dot_general(a, b, (((1,), (1,)), ((), ())), preferred_element_type=si...  45.6 us
    psum x1, blocking collectives, local_fast(): lax.psum(jnp.concatenate([jnp.sum(first_delta * my_normed, axis=0), jnp.s...  40.8 us
    unnamed x188, local copies, waits for them, and re-layouts  31.7 us
  transfers between devices with their start and end apart: 59, of which 23 were waited for; matrix products, arithmetic and copies ran while one was open for 48% of the time, Pallas kernels for 3%

profile of v1, /device:TPU:0, one launch (start us, length us, event | category | flops | bytes accessed | tf_op | source)
XLA Modules:
  0.0 694.0 jit_solution(13670821590913727041)
XLA Ops:
  5.5 2.4 fusion.164
  10.2 2.4 collective-permute-start.2
  18.0 2.4 constant_dynamic-slice_fusion.20
  27.1 3.5 reshape.700
  30.5 2.8 convert_element_type.447
  33.3 3.5 reshape.701
  36.8 10.9 %fusion.13 = (bf16[1,192,1536]{2,0,1:T(2,128)(2,1)}, bf16[1,192,1536]{2,0,1:T(2,128)(2,1)S(1)}, bf16[1,192,1536]{2,0,1:T(2,128)(2,1)S(1)}, bf16[1,192,1536]{2,0,1:T(2,128)(2,1)S(1)}) fusion(s32[]{:T(128)S(6)} %select_n.237, bf16[4,192,768]{2,0,1:T(4,128)(2,1)} %bitcast.396, bf16[4,192,768]{2,0,1:T(4,128)(2,1)} %bitcast.397, s32[]{:T(128)S(6)} %select_n.238, ...), kind=kLoop, calls=%fused_computation.55 | loop fusion | flops 4718592 | bytes 4718608 | tf_op jit(solution)/shard_map/concatenate | solution.py:647
  56.4 2.7 copy.181
  77.8 2.3 copy.219
  97.0 6.3 all-to-all-start
  103.3 3.4 fusion.83
  106.7 2.3 copy.216
  109.0 2.3 copy.213
  111.3 2.5 fusion.154
  120.4 5.5 pad_maximum_fusion.1
  125.9 4.9 constant_dynamic-slice_fusion.13
  130.9 5.7 pad_maximum_fusion.2
  148.1 2.2 fusion.175
  151.3 11.1 %attention.1 = bf16[8,448,128]{2,1,0:T(8,128)(2,1)S(1)} custom-call(bf16[8,448,128]{2,1,0:T(8,128)(2,1)} %all-to-all-done.recv_ref, s32[1,1024]{1,0:T(1,128)S(1)} %fusion.119.place_row_ref, s32[1024,1]{1,0:T(8,128)S(1)} %fusion.42.place_col_ref, s32[512,1]{1,0:T(8,128)S(1)} %copy-done.9), custom_call_target="tpu_custom_call" | custom-call | flops 2818572288 | bytes 1835008 | tf_op jit(solution)/shard_map/attention/pallas_call | solution.py:524
  163.3 4.6 all-to-all-start.1
  179.2 2.4 collective-permute-start.25
  181.6 11.1 %collective-permute-done.26 = bf16[4,4,24,768]{3,2,0,1:T(8,128)(2,1)} collective-permute-done((bf16[4,4,24,768]{3,2,0,1:T(8,128)(2,1)S(1)}, bf16[4,4,24,768]{3,2,0,1:T(8,128)(2,1)}, u32[]{:S(2)}, u32[]{:S(2)}) %collective-permute-start.26) | collective-permute-done | bytes 589856 | tf_op jit(solution)/shard_map/ppermute | solution.py:414
  192.7 2.3 collective-permute-start.24
  198.4 11.2 %collective-permute-done.24 = bf16[4,24,768]{2,1,0:T(8,128)(2,1)S(1)} collective-permute-done((bf16[4,24,768]{2,1,0:T(8,128)(2,1)S(1)}, bf16[4,24,768]{2,1,0:T(8,128)(2,1)S(1)}, u32[]{:S(2)}, u32[]{:S(2)}) %collective-permute-start.24) | collective-permute-done | bytes 147488 | tf_op jit(solution)/shard_map/ppermute | solution.py:414
  210.4 5.7 collective-permute-done.28
  228.6 2.4 fusion.95
  246.9 2.3 fusion.9
  274.0 2.5 collective-permute-start.11
  278.2 4.2 collective-permute-done.13
  282.4 3.1 multiply_reduce_fusion.1
  294.0 40.8 %psum.7 = f32[9216]{0:T(1024)} all-reduce(f32[9216]{0:T(1024)} %constant_dynamic-update-slice_fusion.1), channel_id=1, replica_groups=mesh['ctx'=8,'fsdp'=4] {'ctx','fsdp'}, use_global_device_ids=true, to_apply=%region_15.16 | all-reduce | flops 9216 | bytes 73728 | tf_op jit(solution)/shard_map/psum | solution.py:848
  356.0 2.3 fusion.84
  370.0 3.1 collective-permute-done.21
  373.1 4.1 collective-permute-done.20
  387.0 2.6 collective-permute-done.31
  399.2 2.5 collective-permute-start.38
  407.7 3.4 collective-permute-done.46
  415.7 6.9 collective-permute-done.37
  423.8 6.2 collective-permute-done.38
  432.2 11.0 %collective-permute-done.47 = bf16[4,24,3072]{2,1,0:T(8,128)(2,1)S(1)} collective-permute-done((bf16[4,24,3072]{2,1,0:T(8,128)(2,1)S(1)}, bf16[4,24,3072]{2,1,0:T(8,128)(2,1)S(1)}, u32[]{:S(2)}, u32[]{:S(2)}) %collective-permute-start.47) | collective-permute-done | bytes 589856 | tf_op jit(solution)/shard_map/ppermute | solution.py:414
  444.9 2.3 collective-permute-start.39
  447.3 6.7 collective-permute-done.48
  454.6 23.2 %collective-permute-done.50 = bf16[4,24,3072]{2,1,0:T(8,128)(2,1)S(1)} collective-permute-done((bf16[4,24,3072]{2,1,0:T(8,128)(2,1)S(1)}, bf16[4,24,3072]{2,1,0:T(8,128)(2,1)S(1)}, u32[]{:S(2)}, u32[]{:S(2)}) %collective-permute-start.50) | collective-permute-done | bytes 589856 | tf_op jit(solution)/shard_map/ppermute | solution.py:414
  485.1 8.9 %collective-permute-done.49 = bf16[4,24,3072]{2,1,0:T(8,128)(2,1)S(1)} collective-permute-done((bf16[4,24,3072]{2,1,0:T(8,128)(2,1)S(1)}, bf16[4,24,3072]{2,1,0:T(8,128)(2,1)S(1)}, u32[]{:S(2)}, u32[]{:S(2)}) %collective-permute-start.49) | collective-permute-done | bytes 589856 | tf_op jit(solution)/shard_map/ppermute | solution.py:414
  494.1 12.5 %collective-permute-done.51 = bf16[4,24,3072]{2,1,0:T(8,128)(2,1)S(1)} collective-permute-done((bf16[4,24,3072]{2,1,0:T(8,128)(2,1)S(1)}, bf16[4,24,3072]{2,1,0:T(8,128)(2,1)S(1)}, u32[]{:S(2)}, u32[]{:S(2)}) %collective-permute-start.51) | collective-permute-done | bytes 589856 | tf_op jit(solution)/shard_map/ppermute | solution.py:414
  506.7 11.5 %collective-permute-done.53 = bf16[4,24,3072]{2,1,0:T(8,128)(2,1)S(1)} collective-permute-done((bf16[4,24,3072]{2,1,0:T(8,128)(2,1)S(1)}, bf16[4,24,3072]{2,1,0:T(8,128)(2,1)S(1)}, u32[]{:S(2)}, u32[]{:S(2)}) %collective-permute-start.53) | collective-permute-done | bytes 589856 | tf_op jit(solution)/shard_map/ppermute | solution.py:414
  520.5 3.0 fusion
  524.2 3.5 fusion.1
  527.8 2.2 copy-done.24
  530.0 4.9 convolution_convert_fusion.4
  534.9 12.6 %add_convert_fusion.4 = bf16[768,3072]{1,0:T(8,128)(2,1)} fusion(bf16[768,3072]{1,0:T(8,128)(2,1)} %bitcast.394, bf16[768,768]{1,0:T(8,128)(2,1)} %convolution_convert_fusion.4), kind=kOutput, calls=%fused_computation.8 | convolution fusion | flops 4542234624 | bytes 10616832 | tf_op jit(solution)/shard_map/dot_general | solution.py:833
  547.5 8.6 %convolution_convert_fusion.3 = bf16[768,768]{1,0:T(8,128)(2,1)} fusion(bf16[768,3072]{1,0:T(8,128)(2,1)} %add_convert_fusion.4), kind=kOutput, calls=%fused_computation.42 | convolution fusion | flops 3624468480 | bytes 5898240 | tf_op jit(solution)/shard_map/dot_general | solution.py:741
  556.1 12.8 %add_convert_fusion.3 = bf16[768,3072]{1,0:T(8,128)(2,1)} fusion(bf16[768,3072]{1,0:T(8,128)(2,1)} %add_convert_fusion.4, bf16[768,768]{1,0:T(8,128)(2,1)} %convolution_convert_fusion.3), kind=kOutput, calls=%fused_computation.7 | convolution fusion | flops 4542234624 | bytes 10616832 | tf_op jit(solution)/shard_map/dot_general | solution.py:833
  568.9 8.6 %convolution_convert_fusion.2 = bf16[768,768]{1,0:T(8,128)(2,1)} fusion(bf16[768,3072]{1,0:T(8,128)(2,1)} %add_convert_fusion.3), kind=kOutput, calls=%fused_computation.41 | convolution fusion | flops 3624468480 | bytes 5898240 | tf_op jit(solution)/shard_map/dot_general | solution.py:741
  577.5 12.6 %add_convert_fusion.2 = bf16[768,3072]{1,0:T(8,128)(2,1)} fusion(bf16[768,3072]{1,0:T(8,128)(2,1)} %add_convert_fusion.3, bf16[768,768]{1,0:T(8,128)(2,1)} %convolution_convert_fusion.2), kind=kOutput, calls=%fused_computation.6 | convolution fusion | flops 4542234624 | bytes 10616832 | tf_op jit(solution)/shard_map/dot_general | solution.py:833
  590.2 8.6 %convolution_convert_fusion.1 = bf16[768,768]{1,0:T(8,128)(2,1)} fusion(bf16[768,3072]{1,0:T(8,128)(2,1)} %add_convert_fusion.2), kind=kOutput, calls=%fused_computation.40 | convolution fusion | flops 3624468480 | bytes 5898240 | tf_op jit(solution)/shard_map/dot_general | solution.py:741
  598.8 12.8 %add_convert_fusion.1 = bf16[768,3072]{1,0:T(8,128)(2,1)} fusion(bf16[768,3072]{1,0:T(8,128)(2,1)} %add_convert_fusion.2, bf16[768,768]{1,0:T(8,128)(2,1)} %convolution_convert_fusion.1), kind=kOutput, calls=%fused_computation.5 | convolution fusion | flops 4542234624 | bytes 10616832 | tf_op jit(solution)/shard_map/dot_general | solution.py:833
  611.6 8.6 %convolution_convert_fusion = bf16[768,768]{1,0:T(8,128)(2,1)} fusion(bf16[768,3072]{1,0:T(8,128)(2,1)} %add_convert_fusion.1), kind=kOutput, calls=%fused_computation.39 | convolution fusion | flops 3624468480 | bytes 5898240 | tf_op jit(solution)/shard_map/dot_general | solution.py:741
  620.3 12.4 %add_convert_fusion = bf16[768,3072]{1,0:T(8,128)(2,1)} fusion(bf16[768,3072]{1,0:T(8,128)(2,1)} %add_convert_fusion.1, bf16[768,768]{1,0:T(8,128)(2,1)} %convolution_convert_fusion), kind=kOutput, calls=%fused_computation.4 | convolution fusion | flops 4542234624 | bytes 10616832 | tf_op jit(solution)/shard_map/dot_general | solution.py:833
  632.7 2.9 slice_bitcast_fusion.3
  639.6 8.3 %moments.1 = (f32[192,2304]{1,0:T(8,128)}, f32[192,768]{1,0:T(8,128)}, f32[192,3072]{1,0:T(8,128)}, f32[192,3072]{1,0:T(8,128)}, f32[192,2304]{1,0:T(8,128)}, /*...) custom-call(s32[1]{0:T(128)} %bitcast.60.where_ref, ...), custom_call_target="tpu_custom_call" | custom-call | tf_op jit(solution)/shard_map/moments/pallas_call | solution.py:550
  647.9 16.7 %collective-permute-done.55 = bf16[8,24,3072]{2,1,0:T(8,128)(2,1)S(1)} collective-permute-done((bf16[8,24,3072]{2,1,0:T(8,128)(2,1)S(1)}, bf16[8,24,3072]{2,1,0:T(8,128)(2,1)S(1)}, u32[]{:S(2)}, u32[]{:S(2)}) %collective-permute-start.55) | collective-permute-done | bytes 1179680 | tf_op jit(solution)/shard_map/ppermute | solution.py:414
  664.6 21.4 %collective-permute-done.56 = bf16[8,24,3072]{2,1,0:T(8,128)(2,1)S(1)} collective-permute-done((bf16[8,24,3072]{2,1,0:T(8,128)(2,1)S(1)}, bf16[8,24,3072]{2,1,0:T(8,128)(2,1)S(1)}, u32[]{:S(2)}, u32[]{:S(2)}) %collective-permute-start.56) | collective-permute-done | bytes 1179680 | tf_op jit(solution)/shard_map/ppermute | solution.py:414
  688.2 4.8 weights.1
  (476 shorter events, 241.6 us)
Async XLA Ops:
  10.2 48.9 %collective-permute-start.2 = (bf16[272,768]{1,0:T(8,128)(2,1)}, bf16[272,768]{1,0:T(8,128)(2,1)}, u32[]{:S(2)}, u32[]{:S(2)}) collective-permute-start(bf16[272,768]{1,0:T(8,128)(2,1)} %pad_maximum_fusion.13), channel_id=1, source_target_pairs={{0,3},{1,2},{2,1},{3,0},{4,7},{5,6},{6,5},{7,4},{8,11},{9,10},{10,... | collective-permute-start | bytes 1253384 | tf_op jit(solution)/shard_map/ppermute | solution.py:414
  12.6 47.4 %collective-permute-start.1 = (bf16[272,768]{1,0:T(8,128)(2,1)}, bf16[272,768]{1,0:T(8,128)(2,1)}, u32[]{:S(2)}, u32[]{:S(2)}) collective-permute-start(bf16[272,768]{1,0:T(8,128)(2,1)} %pad_maximum_fusion.13), channel_id=1, source_target_pairs={{0,2},{1,3},{2,0},{3,1},{4,6},{5,7},{6,4},{7,5},{8,10},{9,11},{10,... | collective-permute-start | bytes 1253384 | tf_op jit(solution)/shard_map/ppermute | solution.py:414
  20.4 30.8 %collective-permute-start.5 = (bf16[192,576]{0,1:T(8,128)(2,1)}, bf16[192,576]{0,1:T(8,128)(2,1)}, u32[]{:S(2)}, u32[]{:S(2)}) collective-permute-start(bf16[192,576]{0,1:T(8,128)(2,1)} %get-tuple-element.152), channel_id=1, source_target_pairs={{0,3},{1,2},{2,1},{3,0},{4,7},{5,6},{6,5},{7,4},{8,11},{9,10},{10,... | collective-permute-start | bytes 663560 | tf_op jit(solution)/shard_map/ppermute | solution.py:414
  21.9 29.8 %collective-permute-start.4 = (bf16[192,576]{0,1:T(8,128)(2,1)}, bf16[192,576]{0,1:T(8,128)(2,1)}, u32[]{:S(2)}, u32[]{:S(2)}) collective-permute-start(bf16[192,576]{0,1:T(8,128)(2,1)} %get-tuple-element.153), channel_id=1, source_target_pairs={{0,2},{1,3},{2,0},{3,1},{4,6},{5,7},{6,4},{7,5},{8,10},{9,11},{10,... | collective-permute-start | bytes 663560 | tf_op jit(solution)/shard_map/ppermute | solution.py:414
  22.2 31.0 %collective-permute-start.3 = (bf16[192,576]{0,1:T(8,128)(2,1)}, bf16[192,576]{0,1:T(8,128)(2,1)}, u32[]{:S(2)}, u32[]{:S(2)}) collective-permute-start(bf16[192,576]{0,1:T(8,128)(2,1)} %get-tuple-element.154), channel_id=1, source_target_pairs={{0,1},{1,0},{2,3},{3,2},{4,5},{5,4},{6,7},{7,6},{8,9},{9,8},{10,11... | collective-permute-start | bytes 663560 | tf_op jit(solution)/shard_map/ppermute | solution.py:414
  51.2 9.5 %collective-permute-start = (bf16[272,768]{1,0:T(8,128)(2,1)}, bf16[272,768]{1,0:T(8,128)(2,1)}, u32[]{:S(2)}, u32[]{:S(2)}) collective-permute-start(bf16[272,768]{1,0:T(8,128)(2,1)} %pad_maximum_fusion.13), channel_id=1, source_target_pairs={{0,1},{1,0},{2,3},{3,2},{4,5},{5,4},{6,7},{7,6},{8,9},{9,8},{10,11... | collective-permute-start | bytes 1253384 | tf_op jit(solution)/shard_map/ppermute | solution.py:414
  51.7 62.7 %collective-permute-start.8 = (bf16[192,1536]{1,0:T(8,128)(2,1)}, bf16[192,1536]{1,0:T(8,128)(2,1)}, u32[]{:S(2)}, u32[]{:S(2)}) collective-permute-start(bf16[192,1536]{1,0:T(8,128)(2,1)} %bitcast.437), channel_id=1, source_target_pairs={{0,3},{1,2},{2,1},{3,0},{4,7},{5,6},{6,5},{7,4},{8,11},{9,10},{10,... | collective-permute-start | bytes 1769480 | tf_op jit(solution)/shard_map/ppermute | solution.py:414
  53.1 63.2 %collective-permute-start.7 = (bf16[192,1536]{1,0:T(8,128)(2,1)}, bf16[192,1536]{1,0:T(8,128)(2,1)}, u32[]{:S(2)}, u32[]{:S(2)}) collective-permute-start(bf16[192,1536]{1,0:T(8,128)(2,1)} %bitcast.436), channel_id=1, source_target_pairs={{0,2},{1,3},{2,0},{3,1},{4,6},{5,7},{6,4},{7,5},{8,10},{9,11},{10,... | collective-permute-start | bytes 1769480 | tf_op jit(solution)/shard_map/ppermute | solution.py:414
  59.2 59.3 %collective-permute-start.6 = (bf16[192,1536]{1,0:T(8,128)(2,1)}, bf16[192,1536]{1,0:T(8,128)(2,1)}, u32[]{:S(2)}, u32[]{:S(2)}) collective-permute-start(bf16[192,1536]{1,0:T(8,128)(2,1)} %bitcast.382), channel_id=1, source_target_pairs={{0,1},{1,0},{2,3},{3,2},{4,5},{5,4},{6,7},{7,6},{8,9},{9,8},{10,11... | collective-permute-start | bytes 1769480 | tf_op jit(solution)/shard_map/ppermute | solution.py:414
  97.0 53.4 %all-to-all-start = ((bf16[8,448,128]{2,1,0:T(8,128)(2,1)}), bf16[8,448,128]{2,1,0:T(8,128)(2,1)}, u32[]{:S(2)}, u32[]{:S(2)}) async-start(bf16[8,448,128]{2,1,0:T(8,128)(2,1)} %bitcast.400), calls=%async_computation | async-start | bytes 1835008 | tf_op jit(solution)/shard_map/all_to_all | solution.py:726
  143.9 32.0 %collective-permute-start.22 = (bf16[4,4,24,768]{3,2,1,0:T(8,128)(2,1)}, bf16[4,4,24,768]{3,2,1,0:T(8,128)(2,1)}, u32[]{:S(2)}, u32[]{:S(2)}) collective-permute-start(bf16[4,4,24,768]{3,2,1,0:T(8,128)(2,1)} %fusion.38), channel_id=1, source_target_pairs={{0,4},{4,0},{8,12},{12,8},{16,20},{20,16},{24,28},{28,24},{1,5},{5... | collective-permute-start | bytes 1769480 | tf_op jit(solution)/shard_map/ppermute | solution.py:414
  163.3 53.5 %all-to-all-start.1 = ((bf16[8,448,128]{2,1,0:T(8,128)(2,1)}), bf16[8,448,128]{2,1,0:T(8,128)(2,1)}, u32[]{:S(2)}, u32[]{:S(2)}) async-start(bf16[8,448,128]{2,1,0:T(8,128)(2,1)} %copy-done.7), calls=%async_computation.1 | async-start | bytes 1835008 | tf_op jit(solution)/shard_map/all_to_all | solution.py:728
  169.3 23.4 %collective-permute-start.26 = (bf16[4,4,24,768]{3,2,0,1:T(8,128)(2,1)S(1)}, bf16[4,4,24,768]{3,2,0,1:T(8,128)(2,1)}, u32[]{:S(2)}, u32[]{:S(2)}) collective-permute-start(bf16[4,4,24,768]{3,2,0,1:T(8,128)(2,1)S(1)} %fusion.39), channel_id=1, source_target_pairs={{0,4},{4,0},{8,12},{12,8},{16,20},{20,16},{24,28},{28,24},{1,5},{5... | collective-permute-start | bytes 1769480 | tf_op jit(solution)/shard_map/ppermute | solution.py:414
  172.2 98.4 %collective-permute-start.15 = (bf16[128,768]{1,0:T(8,128)(2,1)}, bf16[128,768]{1,0:T(8,128)(2,1)}, u32[]{:S(2)}, u32[]{:S(2)}) collective-permute-start(bf16[128,768]{1,0:T(8,128)(2,1)} %get-tuple-element.171), channel_id=1, source_target_pairs={{0,1},{1,0},{2,3},{3,2},{4,5},{5,4},{6,7},{7,6},{8,9},{9,8},{10,11... | collective-permute-start | bytes 589832 | tf_op jit(solution)/shard_map/ppermute | solution.py:414
  172.2 100.6 %collective-permute-start.17 = (bf16[128,768]{1,0:T(8,128)(2,1)}, bf16[128,768]{1,0:T(8,128)(2,1)}, u32[]{:S(2)}, u32[]{:S(2)}) collective-permute-start(bf16[128,768]{1,0:T(8,128)(2,1)} %get-tuple-element.172), channel_id=1, source_target_pairs={{0,3},{1,2},{2,1},{3,0},{4,7},{5,6},{6,5},{7,4},{8,11},{9,10},{10,... | collective-permute-start | bytes 589832 | tf_op jit(solution)/shard_map/ppermute | solution.py:414
  175.9 19.1 %copy-start.15 = (f32[4,4,2,24,768]{4,3,2,1,0:T(8,128)S(1)}, f32[4,4,2,24,768]{4,3,2,1,0:T(8,128)}, u32[]{:S(2)}) copy-start(f32[4,4,2,24,768]{4,3,2,1,0:T(8,128)} %fusion.30) | copy-start | bytes 7077892
  177.7 18.6 %collective-permute-start.23 = (bf16[4,24,768]{2,1,0:T(8,128)(2,1)S(1)}, bf16[4,24,768]{2,1,0:T(8,128)(2,1)S(1)}, u32[]{:S(2)}, u32[]{:S(2)}) collective-permute-start(bf16[4,24,768]{2,1,0:T(8,128)(2,1)S(1)} %get-tuple-element.144), channel_id=1, source_target_pairs={{0,8},{4,12},{8,0},{12,4},{16,24},{20,28},{24,16},{28,20},{1,9},{5... | collective-permute-start | bytes 442376 | tf_op jit(solution)/shard_map/ppermute | solution.py:414
  179.2 18.7 %collective-permute-start.25 = (bf16[4,24,768]{2,1,0:T(8,128)(2,1)S(1)}, bf16[4,24,768]{2,1,0:T(8,128)(2,1)S(1)}, u32[]{:S(2)}, u32[]{:S(2)}) collective-permute-start(bf16[4,24,768]{2,1,0:T(8,128)(2,1)S(1)} %get-tuple-element.145), channel_id=1, source_target_pairs={{0,24},{4,28},{8,16},{12,20},{16,8},{20,12},{24,0},{28,4},{1,25},{... | collective-permute-start | bytes 442376 | tf_op jit(solution)/shard_map/ppermute | solution.py:414
  192.7 16.9 %collective-permute-start.24 = (bf16[4,24,768]{2,1,0:T(8,128)(2,1)S(1)}, bf16[4,24,768]{2,1,0:T(8,128)(2,1)S(1)}, u32[]{:S(2)}, u32[]{:S(2)}) collective-permute-start(bf16[4,24,768]{2,1,0:T(8,128)(2,1)S(1)} %get-tuple-element.146), channel_id=1, source_target_pairs={{0,16},{4,20},{8,24},{12,28},{16,0},{20,4},{24,8},{28,12},{1,17},{... | collective-permute-start | bytes 442376 | tf_op jit(solution)/shard_map/ppermute | solution.py:414
  196.3 14.1 %collective-permute-start.27 = (bf16[4,24,768]{2,1,0:T(8,128)(2,1)S(1)}, bf16[4,24,768]{2,1,0:T(8,128)(2,1)S(1)}, u32[]{:S(2)}, u32[]{:S(2)}) collective-permute-start(bf16[4,24,768]{2,1,0:T(8,128)(2,1)S(1)} %get-tuple-element.141), channel_id=1, source_target_pairs={{0,8},{4,12},{8,0},{12,4},{16,24},{20,28},{24,16},{28,20},{1,9},{5... | collective-permute-start | bytes 442376 | tf_op jit(solution)/shard_map/ppermute | solution.py:414
  197.9 12.4 %collective-permute-start.29 = (bf16[4,24,768]{2,1,0:T(8,128)(2,1)S(1)}, bf16[4,24,768]{2,1,0:T(8,128)(2,1)S(1)}, u32[]{:S(2)}, u32[]{:S(2)}) collective-permute-start(bf16[4,24,768]{2,1,0:T(8,128)(2,1)S(1)} %get-tuple-element.142), channel_id=1, source_target_pairs={{0,24},{4,28},{8,16},{12,20},{16,8},{20,12},{24,0},{28,4},{1,25},{... | collective-permute-start | bytes 442376 | tf_op jit(solution)/shard_map/ppermute | solution.py:414
  209.6 6.5 collective-permute-start.28
  237.1 14.9 %copy-start.41 = (f32[512,64]{0,1:T(8,128)}, f32[512,64]{0,1:T(8,128)S(1)}, u32[]{:S(2)}) copy-start(f32[512,64]{0,1:T(8,128)S(1)} %copy.240) | copy-start | bytes 393220
  238.2 13.8 %copy-start.43 = (f32[512,64]{0,1:T(8,128)}, f32[512,64]{0,1:T(8,128)S(1)}, u32[]{:S(2)}) copy-start(f32[512,64]{0,1:T(8,128)S(1)} %copy.241) | copy-start | bytes 393220
  245.5 12.4 %collective-permute-start.33 = (bf16[4,24,768]{2,1,0:T(8,128)(2,1)S(1)}, bf16[4,24,768]{2,1,0:T(8,128)(2,1)S(1)}, u32[]{:S(2)}, u32[]{:S(2)}) collective-permute-start(bf16[4,24,768]{2,1,0:T(8,128)(2,1)S(1)} %fusion.91), channel_id=1, source_target_pairs={{0,4},{4,0},{8,12},{12,8},{16,20},{20,16},{24,28},{28,24},{1,5},{5... | collective-permute-start | bytes 442376 | tf_op jit(solution)/shard_map/ppermute | solution.py:414
  259.2 7.7 %collective-permute-start.34 = (bf16[24,768]{1,0:T(8,128)(2,1)}, bf16[24,768]{1,0:T(8,128)(2,1)}, u32[]{:S(2)}, u32[]{:S(2)}) collective-permute-start(bf16[24,768]{1,0:T(8,128)(2,1)} %get-tuple-element.205), channel_id=1, source_target_pairs={{0,8},{4,12},{8,0},{12,4},{16,24},{20,28},{24,16},{28,20},{1,9},{5... | collective-permute-start | bytes 110600 | tf_op jit(solution)/shard_map/ppermute | solution.py:414
  259.2 9.2 %collective-permute-start.36 = (bf16[24,768]{1,0:T(8,128)(2,1)}, bf16[24,768]{1,0:T(8,128)(2,1)}, u32[]{:S(2)}, u32[]{:S(2)}) collective-permute-start(bf16[24,768]{1,0:T(8,128)(2,1)} %get-tuple-element.206), channel_id=1, source_target_pairs={{0,24},{4,28},{8,16},{12,20},{16,8},{20,12},{24,0},{28,4},{1,25},{... | collective-permute-start | bytes 110600 | tf_op jit(solution)/shard_map/ppermute | solution.py:414
  260.7 7.7 %collective-permute-start.35 = (bf16[24,768]{1,0:T(8,128)(2,1)}, bf16[24,768]{1,0:T(8,128)(2,1)}, u32[]{:S(2)}, u32[]{:S(2)}) collective-permute-start(bf16[24,768]{1,0:T(8,128)(2,1)} %get-tuple-element.207), channel_id=1, source_target_pairs={{0,16},{4,20},{8,24},{12,28},{16,0},{20,4},{24,8},{28,12},{1,17},{... | collective-permute-start | bytes 110600 | tf_op jit(solution)/shard_map/ppermute | solution.py:414
  266.9 7.1 %collective-permute-start.16 = (bf16[128,768]{1,0:T(8,128)(2,1)}, bf16[128,768]{1,0:T(8,128)(2,1)S(1)}, u32[]{:S(2)}, u32[]{:S(2)}) collective-permute-start(bf16[128,768]{1,0:T(8,128)(2,1)} %get-tuple-element.173), channel_id=1, source_target_pairs={{0,2},{1,3},{2,0},{3,1},{4,6},{5,7},{6,4},{7,5},{8,10},{9,11},{10,... | collective-permute-start | bytes 589832 | tf_op jit(solution)/shard_map/ppermute | solution.py:414
  268.4 5.6 collective-permute-start.12
  268.4 9.8 %collective-permute-start.14 = (bf16[128,768]{1,0:T(8,128)(2,1)}, bf16[128,768]{1,0:T(8,128)(2,1)S(1)}, u32[]{:S(2)}, u32[]{:S(2)}) collective-permute-start(bf16[128,768]{1,0:T(8,128)(2,1)} %get-tuple-element.175), channel_id=1, source_target_pairs={{0,3},{1,2},{2,1},{3,0},{4,7},{5,6},{6,5},{7,4},{8,11},{9,10},{10,... | collective-permute-start | bytes 589832 | tf_op jit(solution)/shard_map/ppermute | solution.py:414
  270.6 11.8 %collective-permute-start.13 = (bf16[128,768]{1,0:T(8,128)(2,1)}, bf16[128,768]{1,0:T(8,128)(2,1)S(1)}, u32[]{:S(2)}, u32[]{:S(2)}) collective-permute-start(bf16[128,768]{1,0:T(8,128)(2,1)} %get-tuple-element.176), channel_id=1, source_target_pairs={{0,2},{1,3},{2,0},{3,1},{4,6},{5,7},{6,4},{7,5},{8,10},{9,11},{10,... | collective-permute-start | bytes 589832 | tf_op jit(solution)/shard_map/ppermute | solution.py:414
  272.8 87.5 %collective-permute-start.18 = (bf16[4,4,24,576]{3,2,1,0:T(8,128)(2,1)}, bf16[4,4,24,576]{3,2,1,0:T(8,128)(2,1)}, u32[]{:S(2)}, u32[]{:S(2)}) collective-permute-start(bf16[4,4,24,576]{3,2,1,0:T(8,128)(2,1)} %fusion.46), channel_id=1, source_target_pairs={{0,4},{4,0},{8,12},{12,8},{16,20},{20,16},{24,28},{28,24},{1,5},{5... | collective-permute-start | bytes 1327112 | tf_op jit(solution)/shard_map/ppermute | solution.py:414
  274.0 81.9 %collective-permute-start.9 = (bf16[128,768]{1,0:T(8,128)(2,1)}, bf16[128,768]{1,0:T(8,128)(2,1)}, u32[]{:S(2)}, u32[]{:S(2)}) collective-permute-start(bf16[128,768]{1,0:T(8,128)(2,1)} %get-tuple-element.177), channel_id=1, source_target_pairs={{0,1},{1,0},{2,3},{3,2},{4,5},{5,4},{6,7},{7,6},{8,9},{9,8},{10,11... | collective-permute-start | bytes 589832 | tf_op jit(solution)/shard_map/ppermute | solution.py:414
  274.0 81.9 %collective-permute-start.11 = (bf16[128,768]{1,0:T(8,128)(2,1)}, bf16[128,768]{1,0:T(8,128)(2,1)}, u32[]{:S(2)}, u32[]{:S(2)}) collective-permute-start(bf16[128,768]{1,0:T(8,128)(2,1)} %get-tuple-element.178), channel_id=1, source_target_pairs={{0,3},{1,2},{2,1},{3,0},{4,7},{5,6},{6,5},{7,4},{8,11},{9,10},{10,... | collective-permute-start | bytes 589832 | tf_op jit(solution)/shard_map/ppermute | solution.py:414
  278.2 77.7 %collective-permute-start.10 = (bf16[128,768]{1,0:T(8,128)(2,1)}, bf16[128,768]{1,0:T(8,128)(2,1)}, u32[]{:S(2)}, u32[]{:S(2)}) collective-permute-start(bf16[128,768]{1,0:T(8,128)(2,1)} %get-tuple-element.179), channel_id=1, source_target_pairs={{0,2},{1,3},{2,0},{3,1},{4,6},{5,7},{6,4},{7,5},{8,10},{9,11},{10,... | collective-permute-start | bytes 589832 | tf_op jit(solution)/shard_map/ppermute | solution.py:414
  282.4 73.5 %copy-start.67 = (f32[768]{0:T(1024)S(1)}, f32[768]{0:T(1024)}, u32[]{:S(2)}) copy-start(f32[768]{0:T(1024)} %add.567) | copy-start | bytes 9220
  362.4 21.8 %copy-start.78 = (f32[192]{0:T(256)S(1)}, f32[192]{0:T(256)}, u32[]{:S(2)}) copy-start(f32[192]{0:T(256)} %param.28) | copy-start | bytes 2308
  363.2 6.9 collective-permute-start.19
  364.3 8.8 %collective-permute-start.21 = (bf16[4,24,576]{2,1,0:T(8,128)(2,1)}, bf16[4,24,576]{2,1,0:T(8,128)(2,1)}, u32[]{:S(2)}, u32[]{:S(2)}) collective-permute-start(bf16[4,24,576]{2,1,0:T(8,128)(2,1)} %get-tuple-element.160), channel_id=1, source_target_pairs={{0,24},{4,28},{8,16},{12,20},{16,8},{20,12},{24,0},{28,4},{1,25},{... | collective-permute-start | bytes 331784 | tf_op jit(solution)/shard_map/ppermute | solution.py:414
  366.2 11.0 %collective-permute-start.20 = (bf16[4,24,576]{2,1,0:T(8,128)(2,1)}, bf16[4,24,576]{2,1,0:T(8,128)(2,1)}, u32[]{:S(2)}, u32[]{:S(2)}) collective-permute-start(bf16[4,24,576]{2,1,0:T(8,128)(2,1)} %get-tuple-element.161), channel_id=1, source_target_pairs={{0,16},{4,20},{8,24},{12,28},{16,0},{20,4},{24,8},{28,12},{1,17},{... | collective-permute-start | bytes 331784 | tf_op jit(solution)/shard_map/ppermute | solution.py:414
  382.1 4.9 collective-permute-start.32
  382.2 7.5 %collective-permute-start.31 = (bf16[24,2112]{1,0:T(8,128)(2,1)S(1)}, bf16[24,2112]{1,0:T(8,128)(2,1)S(1)}, u32[]{:S(2)}, u32[]{:S(2)}) collective-permute-start(bf16[24,2112]{1,0:T(8,128)(2,1)S(1)} %get-tuple-element.192), channel_id=1, source_target_pairs={{0,2},{1,3},{2,0},{3,1},{4,6},{5,7},{6,4},{7,5},{8,10},{9,11},{10,... | collective-permute-start | bytes 304136 | tf_op jit(solution)/shard_map/ppermute | solution.py:414
  384.2 5.5 collective-permute-start.30
  399.1 45.8 %collective-permute-start.40 = (bf16[24,9216]{1,0:T(8,128)(2,1)S(1)}, bf16[24,9216]{1,0:T(8,128)(2,1)S(1)}, u32[]{:S(2)}, u32[]{:S(2)}) collective-permute-start(bf16[24,9216]{1,0:T(8,128)(2,1)S(1)} %pad_maximum_fusion.12), channel_id=1, source_target_pairs={{0,16},{4,20},{8,24},{12,28},{16,0},{20,4},{24,8},{28,12},{1,17},{... | collective-permute-start | bytes 1327112 | tf_op jit(solution)/shard_map/ppermute | solution.py:414
  399.2 30.8 %collective-permute-start.38 = (bf16[24,9216]{1,0:T(8,128)(2,1)S(1)}, bf16[24,9216]{1,0:T(8,128)(2,1)S(1)}, u32[]{:S(2)}, u32[]{:S(2)}) collective-permute-start(bf16[24,9216]{1,0:T(8,128)(2,1)S(1)} %pad_maximum_fusion.12), channel_id=1, source_target_pairs={{0,8},{4,12},{8,0},{12,4},{16,24},{20,28},{24,16},{28,20},{1,9},{5... | collective-permute-start | bytes 1327112 | tf_op jit(solution)/shard_map/ppermute | solution.py:414
  405.0 6.1 collective-permute-start.46
  405.0 8.5 %collective-permute-start.45 = (bf16[24,3072]{1,0:T(8,128)(2,1)S(1)}, bf16[24,3072]{1,0:T(8,128)(2,1)S(1)}, u32[]{:S(2)}, u32[]{:S(2)}) collective-permute-start(bf16[24,3072]{1,0:T(8,128)(2,1)S(1)} %get-tuple-element.182), channel_id=1, source_target_pairs={{0,2},{1,3},{2,0},{3,1},{4,6},{5,7},{6,4},{7,5},{8,10},{9,11},{10,... | collective-permute-start | bytes 442376 | tf_op jit(solution)/shard_map/ppermute | solution.py:414
  406.0 9.0 %collective-permute-start.44 = (bf16[24,3072]{1,0:T(8,128)(2,1)S(1)}, bf16[24,3072]{1,0:T(8,128)(2,1)S(1)}, u32[]{:S(2)}, u32[]{:S(2)}) collective-permute-start(bf16[24,3072]{1,0:T(8,128)(2,1)S(1)} %get-tuple-element.183), channel_id=1, source_target_pairs={{0,1},{1,0},{2,3},{3,2},{4,5},{5,4},{6,7},{7,6},{8,9},{9,8},{10,11... | collective-permute-start | bytes 442376 | tf_op jit(solution)/shard_map/ppermute | solution.py:414
  411.1 11.4 %collective-permute-start.37 = (bf16[24,9216]{1,0:T(8,128)(2,1)S(1)}, bf16[24,9216]{1,0:T(8,128)(2,1)S(1)}, u32[]{:S(2)}, u32[]{:S(2)}) collective-permute-start(bf16[24,9216]{1,0:T(8,128)(2,1)S(1)} %pad_maximum_fusion.12), channel_id=1, source_target_pairs={{0,4},{4,0},{8,12},{12,8},{16,20},{20,16},{24,28},{28,24},{1,5},{5... | collective-permute-start | bytes 1327112 | tf_op jit(solution)/shard_map/ppermute | solution.py:414
  413.5 33.7 %collective-permute-start.42 = (bf16[24,9216]{1,0:T(8,128)(2,1)S(1)}, bf16[24,9216]{1,0:T(8,128)(2,1)}, u32[]{:S(2)}, u32[]{:S(2)}) collective-permute-start(bf16[24,9216]{1,0:T(8,128)(2,1)S(1)} %pad_maximum_fusion.12), channel_id=1, source_target_pairs={{0,24},{4,28},{8,16},{12,20},{16,8},{20,12},{24,0},{28,4},{1,25},{... | collective-permute-start | bytes 1327112 | tf_op jit(solution)/shard_map/ppermute | solution.py:414
  415.1 62.7 %collective-permute-start.50 = (bf16[4,24,3072]{2,1,0:T(8,128)(2,1)S(1)}, bf16[4,24,3072]{2,1,0:T(8,128)(2,1)S(1)}, u32[]{:S(2)}, u32[]{:S(2)}) collective-permute-start(bf16[4,24,3072]{2,1,0:T(8,128)(2,1)S(1)} %pad_maximum_fusion.10), channel_id=1, source_target_pairs={{0,16},{4,20},{8,24},{12,28},{16,0},{20,4},{24,8},{28,12},{1,17},{... | collective-permute-start | bytes 1769480 | tf_op jit(solution)/shard_map/ppermute | solution.py:414
  422.5 31.5 %collective-permute-start.48 = (bf16[4,24,3072]{2,1,0:T(8,128)(2,1)S(1)}, bf16[4,24,3072]{2,1,0:T(8,128)(2,1)S(1)}, u32[]{:S(2)}, u32[]{:S(2)}) collective-permute-start(bf16[4,24,3072]{2,1,0:T(8,128)(2,1)S(1)} %pad_maximum_fusion.10), channel_id=1, source_target_pairs={{0,8},{4,12},{8,0},{12,4},{16,24},{20,28},{24,16},{28,20},{1,9},{5... | collective-permute-start | bytes 1769480 | tf_op jit(solution)/shard_map/ppermute | solution.py:414
  430.0 13.2 %collective-permute-start.47 = (bf16[4,24,3072]{2,1,0:T(8,128)(2,1)S(1)}, bf16[4,24,3072]{2,1,0:T(8,128)(2,1)S(1)}, u32[]{:S(2)}, u32[]{:S(2)}) collective-permute-start(bf16[4,24,3072]{2,1,0:T(8,128)(2,1)S(1)} %pad_maximum_fusion.10), channel_id=1, source_target_pairs={{0,4},{4,0},{8,12},{12,8},{16,20},{20,16},{24,28},{28,24},{1,5},{5... | collective-permute-start | bytes 1769480 | tf_op jit(solution)/shard_map/ppermute | solution.py:414
  443.2 35.7 %collective-permute-start.52 = (bf16[4,24,3072]{2,1,0:T(8,128)(2,1)S(1)}, bf16[4,24,3072]{2,1,0:T(8,128)(2,1)S(1)}, u32[]{:S(2)}, u32[]{:S(2)}) collective-permute-start(bf16[4,24,3072]{2,1,0:T(8,128)(2,1)S(1)} %pad_maximum_fusion.10), channel_id=1, source_target_pairs={{0,24},{4,28},{8,16},{12,20},{16,8},{20,12},{24,0},{28,4},{1,25},{... | collective-permute-start | bytes 1769480 | tf_op jit(solution)/shard_map/ppermute | solution.py:414
  444.9 35.0 %collective-permute-start.39 = (bf16[24,9216]{1,0:T(8,128)(2,1)S(1)}, bf16[24,9216]{1,0:T(8,128)(2,1)S(1)}, u32[]{:S(2)}, u32[]{:S(2)}) collective-permute-start(bf16[24,9216]{1,0:T(8,128)(2,1)S(1)} %collective-permute-done.38), channel_id=1, source_target_pairs={{0,4},{4,0},{8,12},{12,8},{16,20},{20,16},{24,28},{28,24},{1,5},{5... | collective-permute-start | bytes 1327112 | tf_op jit(solution)/shard_map/ppermute | solution.py:414
  447.2 35.3 %collective-permute-start.41 = (bf16[24,9216]{1,0:T(8,128)(2,1)S(1)}, bf16[24,9216]{1,0:T(8,128)(2,1)S(1)}, u32[]{:S(2)}, u32[]{:S(2)}) collective-permute-start(bf16[24,9216]{1,0:T(8,128)(2,1)S(1)} %collective-permute-done.40), channel_id=1, source_target_pairs={{0,4},{4,0},{8,12},{12,8},{16,20},{20,16},{24,28},{28,24},{1,5},{5... | collective-permute-start | bytes 1327112 | tf_op jit(solution)/shard_map/ppermute | solution.py:414
  454.0 183.8 %collective-permute-start.43 = (bf16[24,9216]{1,0:T(8,128)(2,1)}, bf16[24,9216]{1,0:T(8,128)(2,1)}, u32[]{:S(2)}, u32[]{:S(2)}) collective-permute-start(bf16[24,9216]{1,0:T(8,128)(2,1)} %collective-permute-done.42), channel_id=1, source_target_pairs={{0,4},{4,0},{8,12},{12,8},{16,20},{20,16},{24,28},{28,24},{1,5},{5... | collective-permute-start | bytes 1327112 | tf_op jit(solution)/shard_map/ppermute | solution.py:414
  477.8 16.2 %collective-permute-start.49 = (bf16[4,24,3072]{2,1,0:T(8,128)(2,1)S(1)}, bf16[4,24,3072]{2,1,0:T(8,128)(2,1)S(1)}, u32[]{:S(2)}, u32[]{:S(2)}) collective-permute-start(bf16[4,24,3072]{2,1,0:T(8,128)(2,1)S(1)} %collective-permute-done.48), channel_id=1, source_target_pairs={{0,4},{4,0},{8,12},{12,8},{16,20},{20,16},{24,28},{28,24},{1,5},{5... | collective-permute-start | bytes 1769480 | tf_op jit(solution)/shard_map/ppermute | solution.py:414
  478.9 27.8 %collective-permute-start.51 = (bf16[4,24,3072]{2,1,0:T(8,128)(2,1)S(1)}, bf16[4,24,3072]{2,1,0:T(8,128)(2,1)S(1)}, u32[]{:S(2)}, u32[]{:S(2)}) collective-permute-start(bf16[4,24,3072]{2,1,0:T(8,128)(2,1)S(1)} %collective-permute-done.50), channel_id=1, source_target_pairs={{0,4},{4,0},{8,12},{12,8},{16,20},{20,16},{24,28},{28,24},{1,5},{5... | collective-permute-start | bytes 1769480 | tf_op jit(solution)/shard_map/ppermute | solution.py:414
  479.8 38.4 %collective-permute-start.53 = (bf16[4,24,3072]{2,1,0:T(8,128)(2,1)S(1)}, bf16[4,24,3072]{2,1,0:T(8,128)(2,1)S(1)}, u32[]{:S(2)}, u32[]{:S(2)}) collective-permute-start(bf16[4,24,3072]{2,1,0:T(8,128)(2,1)S(1)} %collective-permute-done.52), channel_id=1, source_target_pairs={{0,4},{4,0},{8,12},{12,8},{16,20},{20,16},{24,28},{28,24},{1,5},{5... | collective-permute-start | bytes 1769480 | tf_op jit(solution)/shard_map/ppermute | solution.py:414
  635.6 29.0 %collective-permute-start.55 = (bf16[8,24,3072]{2,1,0:T(8,128)(2,1)S(1)}, bf16[8,24,3072]{2,1,0:T(8,128)(2,1)S(1)}, u32[]{:S(2)}, u32[]{:S(2)}) collective-permute-start(bf16[8,24,3072]{2,1,0:T(8,128)(2,1)S(1)} %get-tuple-element.130), channel_id=1, source_target_pairs={{0,2},{1,3},{2,0},{3,1},{4,6},{5,7},{6,4},{7,5},{8,10},{9,11},{10,... | collective-permute-start | bytes 3538952 | tf_op jit(solution)/shard_map/ppermute | solution.py:414
  636.2 28.4 %collective-permute-start.54 = (bf16[8,24,3072]{2,1,0:T(8,128)(2,1)S(1)}, bf16[8,24,3072]{2,1,0:T(8,128)(2,1)S(1)}, u32[]{:S(2)}, u32[]{:S(2)}) collective-permute-start(bf16[8,24,3072]{2,1,0:T(8,128)(2,1)S(1)} %get-tuple-element.131), channel_id=1, source_target_pairs={{0,1},{1,0},{2,3},{3,2},{4,5},{5,4},{6,7},{7,6},{8,9},{9,8},{10,11... | collective-permute-start | bytes 3538952 | tf_op jit(solution)/shard_map/ppermute | solution.py:414
  636.2 49.8 %collective-permute-start.56 = (bf16[8,24,3072]{2,1,0:T(8,128)(2,1)S(1)}, bf16[8,24,3072]{2,1,0:T(8,128)(2,1)S(1)}, u32[]{:S(2)}, u32[]{:S(2)}) collective-permute-start(bf16[8,24,3072]{2,1,0:T(8,128)(2,1)S(1)} %get-tuple-element.132), channel_id=1, source_target_pairs={{0,3},{1,2},{2,1},{3,0},{4,7},{5,6},{6,5},{7,4},{8,11},{9,10},{10,... | collective-permute-start | bytes 3538952 | tf_op jit(solution)/shard_map/ppermute | solution.py:414
  (78 other events, 374.0 us)

commit v2 on v1

--- a/solution.py
+++ b/solution.py
@@ -409,45 +409,459 @@
 SHARDS = 4
 
 
+OWNERS = (0, 2, 1, 3)
+
+
 def swap(x, axis, offset):
     count = lax.axis_size(axis)
     return lax.ppermute(x, axis, [(i, i ^ offset) for i in range(count)])
 
 
+def exchange(x, axis="fsdp"):
+    return lax.all_to_all(x, axis, 0, 0)
+
+
 def pick(x, index, dim=0):
     return lax.dynamic_index_in_dim(x, index, dim, keepdims=False)
 
 
-def in_order(pieces, place):
-    stacked = jnp.stack(pieces)
-    return jnp.stack([pick(stacked, place ^ i) for i in range(len(pieces))])
-
-
-def spread(x, place):
-    return [pick(x, place)] + [swap(pick(x, place ^ k), "fsdp", k) for k in range(1, SHARDS)]
-
-
-def gather_ctx(x):
-    along = [x] + [swap(x, "ctx", 2 * k) for k in range(1, Z_PLACES)]
+def gather_z(x):
+    return [x] + [swap(x, "ctx", Y_PLACES * k) for k in range(1, Z_PLACES)]
+
+
+def gather_y(along):
     pieces = []
     for piece in along:
         pieces += [piece, swap(piece, "ctx", 1)]
     return pieces
 
 
-def scatter_ctx(x, ctx_place, dim):
+def call(kernel, outs, args, prefetch, name, cost, scratch=(), earlier=()):
+    whole = pl.BlockSpec(memory_space=pltpu.VMEM)
+    count = 1 + len(args)
+
+    def body(*refs):
+        kernel(*refs[:count], *refs[count + len(earlier) :])
+
+    return pl.pallas_call(
+        body,
+        in_specs=[pl.BlockSpec(memory_space=pltpu.SMEM)]
+        + [whole] * len(args)
+        + [pl.BlockSpec(memory_space=pl.ANY)] * len(earlier),
+        out_specs=[whole] * len(outs),
+        out_shape=[jax.ShapeDtypeStruct(shape, dtype) for shape, dtype in outs],
+        scratch_shapes=list(scratch),
+        compiler_params=pltpu.CompilerParams(vmem_limit_bytes=50 * 1024 * 1024),
+        cost_estimate=pl.CostEstimate(
+            flops=0, bytes_accessed=int(cost * 3.6e6), transcendentals=0
+        ),
+        name=name,
+    )(prefetch, *args, *earlier)
+
+
+NT = (((1,), (1,)), ((), ()))
+TN = (((0,), (0,)), ((), ()))
+
+
+def pack_kernel(where_ref, residual_ref, grad_ref, *refs):
+    half = jnp.bfloat16
+    vectors, out_ref = refs[:7], refs[7]
+    place = where_ref[2]
+    rows, width = residual_ref.shape
+
+    def share(ref):
+        size = ref.shape[1]
+        lane = lax.broadcasted_iota(jnp.int32, (1, SHARDS * size), 1)
+        mine = jnp.logical_and(lane >= place * size, lane < (place + 1) * size)
+        return jnp.where(mine, jnp.concatenate([ref[...]] * SHARDS, axis=1), 0.0)
+
+    heads = share(vectors[6])
+    out_ref[:rows] = residual_ref[...]
+    out_ref[rows : 2 * rows] = grad_ref[...].astype(half)
+    small = [share(v) for v in vectors[:6]]
+    small += [heads[:, t * width : (t + 1) * width] for t in range(3)]
+    small.append(jnp.zeros((16 - len(small), width), jnp.float32))
+    out_ref[2 * rows :] = jnp.concatenate(small, axis=0).astype(half)
+
+
+def heads_split_kernel(where_ref, weight_ref, out_ref):
+    part, width = weight_ref.shape[0], weight_ref.shape[1] // 3
+    for dest in range(SHARDS):
+        out_ref[dest] = jnp.concatenate(
+            [
+                weight_ref[:, t * width + dest * part : t * width + (dest + 1) * part]
+                for t in range(3)
+            ],
+            axis=1,
+        ).astype(jnp.bfloat16)
+
+
+def mlp_split_kernel(where_ref, up_ref, down_ref, moments_ref, *outs):
+    place = where_ref[2]
+    part, cols = up_ref.shape[0], up_ref.shape[1] // SHARDS
+    for k in range(SHARDS):
+        cut = pl.ds(pl.multiple_of((place ^ k) * cols, cols), cols)
+        outs[k][:part, :cols] = up_ref[:, cut].astype(jnp.bfloat16)
+        outs[k][:part, cols:] = down_ref[:, cut].astype(jnp.bfloat16)
+        moment = moments_ref[place ^ k]
+        outs[k][part:] = jnp.concatenate(
+            [moment[:, : 2 * cols], moment[:, 2 * cols :]], axis=0
+        ).astype(jnp.bfloat16)
+
+
+def turn(x, cos_ref, high_ref, low_ref, direction):
+    lanes = x.shape[1]
+    moved = pltpu.roll(x, ROT // 2, 1) * high_ref[...] + pltpu.roll(
+        x, lanes - ROT // 2, 1
+    ) * low_ref[...]
+    return x * cos_ref[...] + direction * moved
+
+
+def pre_kernel(where_ref, *refs):
     single, half = jnp.float32, jnp.bfloat16
-    y, z = ctx_place % Y_PLACES, ctx_place // Y_PLACES
-    x = x.reshape(x.shape[:dim] + (Z_PLACES, Y_PLACES) + x.shape[dim + 1 :])
-    sent = swap(pick(x, 1 - y, dim + 1).astype(half), "ctx", 1)
-    kept = pick(x, y, dim + 1) + sent.astype(single)
-    total = pick(kept, z, dim)
+    packs, block_ref = refs[:4], refs[4]
+    output_ref, cos_ref, high_ref, low_ref = refs[5:9]
+    first_ref, second_ref, grad_ref, payload_ref, normed_ref, inverse_ref = refs[9:]
+    place = where_ref[2]
+    part = output_ref.shape[0]
+    rows = normed_ref.shape[0]
+    vectors = sum(p[2 * rows :].astype(single) for p in packs)
+    for r in range(SHARDS):
+        x = packs[r][:rows].astype(single)
+        average = jnp.mean(x, axis=-1, keepdims=True)
+        centred = x - average
+        variance = jnp.mean(centred * centred, axis=-1, keepdims=True)
+        inverse = lax.rsqrt(variance + norm_eps)
+        normed = centred * inverse
+        if r == 0:
+            normed_ref[...] = normed
+            inverse_ref[...] = jnp.broadcast_to(inverse, inverse_ref.shape)
+        cut = slice(r * rows, (r + 1) * rows)
+        first_ref[cut] = (normed * vectors[0:1] + vectors[1:2]).astype(half)
+        second_ref[cut] = (normed * vectors[2:3] + vectors[3:4]).astype(half)
+        grad_ref[cut] = packs[r][rows : 2 * rows]
+    shift = jnp.concatenate(
+        [
+            sum(
+                jnp.where(place == j, vectors[6 + t : 7 + t, j * part : (j + 1) * part], 0.0)
+                for j in range(SHARDS)
+            )
+            for t in range(3)
+        ],
+        axis=1,
+    )
+    projected = jnp.dot(first_ref[...], block_ref[...], preferred_element_type=single) + shift
+    outer = lax.dot_general(
+        grad_ref[...], output_ref[...], NT, preferred_element_type=single
+    ).astype(half)
+    for r in range(SHARDS):
+        cut = slice(r * rows, (r + 1) * rows)
+        turned = turn(projected[cut, : 2 * part], cos_ref, high_ref, low_ref, 1.0).astype(half)
+        values = projected[cut, 2 * part :].astype(half)
+        back = outer[cut]
+
+        def head(x, h):
+            return x[:, h * HD : (h + 1) * HD]
+
+        last = 3 * Z_PLACES // 4 - 1
+        shared = jnp.concatenate([head(turned, 3 + last), head(values, last)], axis=1)
+        query = jnp.concatenate([head(turned, last), head(back, last)], axis=1)
+        for y in range(Y_PLACES):
+            at = r * Y_PLACES + y
+            payload_ref[at, :rows] = jnp.concatenate([head(turned, y), head(turned, 3 + y)], axis=1)
+            payload_ref[at, rows : 2 * rows] = jnp.concatenate(
+                [head(values, y), head(back, y)], axis=1
+            )
+            payload_ref[at, 2 * rows : 3 * rows] = shared
+            payload_ref[at, 3 * rows :] = query[y * rows // 2 : (y + 1) * rows // 2]
+
+
+def write_strips(grad_ref, send_ref, keep_ref, y):
+    strip = send_ref.shape[2]
+    for f in range(SHARDS):
+        for z in range(Z_PLACES):
+            start = (f * CTX + z * Y_PLACES) * strip
+            mine = pl.multiple_of(start + y * strip, 8)
+            other = pl.multiple_of(start + (1 - y) * strip, 8)
+            keep_ref[f, z] = grad_ref[pl.ds(mine, strip), :]
+            send_ref[f, z] = grad_ref[pl.ds(other, strip), :].astype(jnp.bfloat16)
+
+
+def mlp_kernel(where_ref, *refs):
+    single, half = jnp.float32, jnp.bfloat16
+    second_ref, grad_ref, shift_ref = refs[:3]
+    pieces = refs[3:7]
+    send_ref, keep_ref, out_ref, sum_ref, back_ref, block_ref, local_ref = refs[7:]
+    y, place = where_ref[1], where_ref[2]
+    cols = shift_ref.shape[1]
+    part = block_ref.shape[0] // SHARDS
+    for k in range(SHARDS):
+        block_ref[pl.ds(pl.multiple_of((place ^ k) * part, part), part), :] = pieces[k][:part]
+    second, grad = second_ref[...], grad_ref[...]
+    up = block_ref[:, :cols]
+    down = block_ref[:, cols:]
+    pre = jnp.dot(second, up, preferred_element_type=single) + shift_ref[...]
+    cdf = 0.5 * (1.0 + lax.erf(pre * (1.0 / math.sqrt(2.0))))
+    active = (pre * cdf).astype(half)
+    slope = cdf + pre * jnp.exp(-0.5 * pre * pre) * (1.0 / math.sqrt(2.0 * math.pi))
+    delta = jnp.dot(grad, down, preferred_element_type=single) * slope
+    sum_ref[...] = jnp.sum(delta, axis=0, keepdims=True)
+    delta_half = delta.astype(half)
+    local_ref[:, :cols] = lax.dot_general(second, delta_half, TN, preferred_element_type=single)
+    local_ref[:, cols:] = lax.dot_general(grad, active, TN, preferred_element_type=single)
+    write_strips(local_ref, send_ref, keep_ref, y)
+    out_ref[...] = lax.dot_general(active, down, NT, preferred_element_type=single)
+    back_ref[...] = lax.dot_general(delta_half, up, NT, preferred_element_type=single)
+
+
+def post_kernel(where_ref, *refs):
+    single, half = jnp.float32, jnp.bfloat16
+    back_ref, first_ref, grad_ref, block_ref, output_ref, mlp_ref, second_ref = refs[:7]
+    cos_ref, high_ref, low_ref = refs[7:10]
+    send_ref, keep_ref, sum_ref, mine_ref, home_ref = refs[10:15]
+    attn_ref, heads_ref, local_ref = refs[15:]
+    y, place = where_ref[1], where_ref[2]
+    part, width = output_ref.shape
+    rows = mine_ref.shape[0] // 3
+    sums = jnp.zeros((1, 3 * part), single)
+    for r in range(SHARDS):
+        cut = slice(r * rows, (r + 1) * rows)
+        early = [back_ref[r * Y_PLACES + i, :rows] for i in range(Y_PLACES)]
+        early.append(
+            jnp.concatenate([back_ref[r * Y_PLACES + i, 3 * rows :] for i in range(Y_PLACES)], axis=0)
+        )
+        late = [back_ref[r * Y_PLACES + i, rows : 2 * rows].astype(single) for i in range(Y_PLACES)]
+        late.append(
+            sum(back_ref[r * Y_PLACES + i, 2 * rows : 3 * rows].astype(single) for i in range(Y_PLACES))
+        )
+        attn_ref[cut] = jnp.concatenate([x[:, :HD] for x in early], axis=1)
+        turned = turn(
+            jnp.concatenate(
+                [x[:, HD:].astype(single) for x in early] + [x[:, :HD] for x in late], axis=1
+            ),
+            cos_ref,
+            high_ref,
+            low_ref,
+            -1.0,
+        )
+        whole = jnp.concatenate([turned] + [x[:, HD:] for x in late], axis=1)
+        sums += jnp.sum(whole, axis=0, keepdims=True)
+        heads_ref[cut] = whole.astype(half)
+    sum_ref[...] = sums
+    local_ref[:, : 3 * part] = lax.dot_general(
+        first_ref[...], heads_ref[...], TN, preferred_element_type=single
+    )
+    output_local = lax.dot_general(
+        attn_ref[...], grad_ref[...], TN, preferred_element_type=single
+    )
+    for j in range(SHARDS):
+        local_ref[j * part : (j + 1) * part, 3 * part :] = output_local[:, j * part : (j + 1) * part]
+    write_strips(local_ref, send_ref, keep_ref, y)
+    out = jnp.dot(attn_ref[...], output_ref[...], preferred_element_type=single) + mlp_ref[...]
+    first = lax.dot_general(heads_ref[...], block_ref[...], NT, preferred_element_type=single)
+    for i, value in enumerate((out, first, second_ref[...])):
+        cut = slice(i * rows, (i + 1) * rows)
+        mine_ref[cut] = value[:rows]
+        home_ref[place, cut] = jnp.zeros((rows, width), half)
+        for k in range(1, SHARDS):
+            home_ref[place ^ k, cut] = value[k * rows : (k + 1) * rows].astype(half)
+
+
+def along_z_kernel(where_ref, keep_ref, came_ref, own_ref, *sends):
+    z = where_ref[0]
+    own_ref[...] = keep_ref[:, z] + came_ref[:, z].astype(jnp.float32)
     for k in range(1, Z_PLACES):
-        total = total + swap(pick(kept, z ^ k, dim).astype(half), "ctx", 2 * k).astype(single)
-    return total
-
-
-def attention_kernel(recv_ref, place_row_ref, place_col_ref, place_half_ref, out_ref):
+        sends[k - 1][...] = (keep_ref[:, z ^ k] + came_ref[:, z ^ k].astype(jnp.float32)).astype(
+            jnp.bfloat16
+        )
+
+
+def scatter_ctx(send, keep, where, name, *earlier):
+    single, half = jnp.float32, jnp.bfloat16
+    came = swap(send, "ctx", 1)
+    shape = (keep.shape[0],) + keep.shape[2:]
+    own, *sends = call(
+        along_z_kernel,
+        [(shape, single)] + [(shape, half)] * (Z_PLACES - 1),
+        [keep, came],
+        where,
+        name,
+        0.1,
+        earlier=earlier,
+    )
+    return came, [own] + [swap(sends[k - 1], "ctx", 2 * k) for k in range(1, Z_PLACES)]
+
+
+def strip_sum(parts, index):
+    return parts[0][index] + sum(p[index].astype(jnp.float32) for p in parts[1:])
+
+
+def strip_kernel(where_ref, *refs):
+    half = jnp.bfloat16
+    heads, mlp = refs[:4], refs[4:8]
+    strips_ref, owners_ref, output_ref = refs[8:]
+    size = owners_ref.shape[3]
+    cols = 3 * size // 4
+    for j in range(SHARDS):
+        total = strip_sum(heads, j)
+        both = strip_sum(mlp, j).astype(half)
+        strips_ref[j, :, : 2 * size] = both
+        strips_ref[j, :, 2 * size :] = total[:, :cols].astype(half)
+        output_ref[:, j * size // SHARDS : (j + 1) * size // SHARDS] = total[:, cols:]
+        owners_ref[OWNERS[0], j] = total.astype(half)
+        owners_ref[OWNERS[2], j] = both[:, :size]
+        owners_ref[OWNERS[3], j] = both[:, size:]
+    owners_ref[OWNERS[1], 0] = output_ref[...].astype(half)
+    owners_ref[OWNERS[1], 1:] = jnp.zeros(owners_ref.shape[1:], half)[1:]
+
+
+def owned_kernel(where_ref, grads_ref, strips_ref, *refs):
+    single = jnp.float32
+    moments, out_ref, strips_out = refs[:4], refs[4], refs[5]
+    strips_out[...] = strips_ref[...]
+    place = where_ref[2]
+    size = grads_ref.shape[3]
+    part = size // SHARDS
+
+    def write(f, owner, grad):
+        cols, strip = grad.shape[1], grad.shape[0]
+        both = moments[f ^ owner][part:].astype(single)
+        moment = jnp.concatenate([both[:strip], both[strip:]], axis=1)[:, :cols]
+        nest = grad + mom_rate * (mom_rate * moment + grad)
+        out_ref[f, :, :cols] = nest.astype(out_ref.dtype)
+        if cols < out_ref.shape[2]:
+            rest = (out_ref.shape[1], out_ref.shape[2] - cols)
+            out_ref[f, :, cols:] = jnp.zeros(rest, out_ref.dtype)
+
+    @pl.when(place == OWNERS[0])
+    def _():
+        for f in range(SHARDS):
+            pieces = [
+                grads_ref[j, f][:, t * part : (t + 1) * part].astype(single)
+                for t in range(3)
+                for j in range(SHARDS)
+            ]
+            write(f, OWNERS[0], jnp.concatenate(pieces, axis=1))
+
+    @pl.when(place == OWNERS[1])
+    def _():
+        for f in range(SHARDS):
+            write(f, OWNERS[1], grads_ref[f, 0].astype(single))
+
+    for owner in OWNERS[2:]:
+
+        @pl.when(place == owner)
+        def _():
+            for f in range(SHARDS):
+                pieces = [grads_ref[j, f].astype(single) for j in range(SHARDS)]
+                write(f, owner, jnp.concatenate(pieces, axis=1))
+
+
+def grads_kernel(where_ref, strips_ref, output_ref, out_ref):
+    size = output_ref.shape[1]
+    part = size // SHARDS
+    pieces = [
+        strips_ref[f][:, 2 * size + t * part : 2 * size + (t + 1) * part].astype(jnp.float32)
+        for t in range(3)
+        for f in range(SHARDS)
+    ]
+    out_ref[...] = jnp.concatenate(
+        pieces
+        + [output_ref[...]]
+        + [
+            strips_ref[f][:, i * size : (i + 1) * size].astype(jnp.float32)
+            for i in range(2)
+            for f in range(SHARDS)
+        ],
+        axis=1,
+    ).astype(jnp.bfloat16)
+
+
+NEWTON_SIZE = 256
+NEWTON_CHUNK = 768
+
+
+def newton_mixing(x_ref, gram_ref, mix_ref):
+    single, half = jnp.float32, jnp.bfloat16
+    blocks = x_ref.shape[0] // NEWTON_SIZE
+    cuts = [slice(i * NEWTON_SIZE, (i + 1) * NEWTON_SIZE) for i in range(blocks)]
+    pairs = [(cuts[i], cuts[j]) for i in range(blocks) for j in range(i, blocks)]
+    for here, there in pairs:
+        gram = lax.dot_general(x_ref[here], x_ref[there], NT, preferred_element_type=single)
+        gram_ref[here, there] = gram.astype(half)
+        if here != there:
+            gram_ref[there, here] = jnp.transpose(gram).astype(half)
+    for here, there in pairs:
+        square = jnp.dot(gram_ref[here], gram_ref[:, there], preferred_element_type=single)
+        mix = schulz_coeffs[1] * gram_ref[here, there].astype(single) + schulz_coeffs[2] * square
+        mix_ref[here, there] = mix.astype(half)
+        if here != there:
+            mix_ref[there, here] = jnp.transpose(mix).astype(half)
+
+
+def newton_applied(x_ref, mix_ref, at):
+    x = x_ref[:, at : at + NEWTON_CHUNK]
+    return schulz_coeffs[0] * x.astype(jnp.float32) + jnp.dot(
+        mix_ref[...], x, preferred_element_type=jnp.float32
+    )
+
+
+def newton_kernel(where_ref, *refs):
+    single, half = jnp.float32, jnp.bfloat16
+    pieces, x_ref, gram_ref, mix_ref = refs[:CTX], *refs[CTX:]
+    cols = x_ref.shape[1]
+    tall = SHARDS * pieces[0].shape[1]
+    total = jnp.zeros((1, 1), single)
+    for piece in pieces:
+        value = piece[...].astype(single)
+        total += jnp.sum(jnp.sum(value * value, axis=0), keepdims=True)
+    factor = 1.0 / (jnp.sqrt(total) + 1e-07)
+    for c in range(CTX):
+        value = pieces[c][...].astype(single).reshape(tall, cols)
+        x_ref[c * tall : (c + 1) * tall] = (value * factor).astype(half)
+
+    @pl.loop(0, NS_ITERS - 1)
+    def _(step):
+        newton_mixing(x_ref, gram_ref, mix_ref)
+        for at in range(0, cols, NEWTON_CHUNK):
+            x_ref[:, at : at + NEWTON_CHUNK] = newton_applied(x_ref, mix_ref, at).astype(half)
+
+
+def last_newton_kernel(where_ref, x_ref, sums_ref, out_ref, sums_out, gram_ref, mix_ref):
+    sums_out[...] = sums_ref[...]
+    newton_mixing(x_ref, gram_ref, mix_ref)
+    strip = out_ref.shape[2]
+    for at in range(0, x_ref.shape[1], NEWTON_CHUNK):
+        x = newton_applied(x_ref, mix_ref, at)
+        for c in range(CTX):
+            for k in range(SHARDS):
+                start = (c * SHARDS + k) * strip
+                out_ref[k, c, :, at : at + NEWTON_CHUNK] = x[start : start + strip].astype(
+                    jnp.bfloat16
+                )
+
+
+def newton(pieces, sums, where, earlier, between):
+    strip, cols = pieces[0].shape[1:]
+    n = CTX * SHARDS * strip
+    half = jnp.bfloat16
+    scratch = [pltpu.VMEM((n, n), half), pltpu.VMEM((n, n), half)]
+    [x] = call(
+        newton_kernel, [((n, cols), half)], list(pieces), where, "newton", 36.0, scratch, earlier
+    )
+    return call(
+        last_newton_kernel,
+        [((SHARDS, CTX, strip, cols), half), (sums.shape, sums.dtype)],
+        [x, sums],
+        where,
+        "last_newton",
+        9.0,
+        scratch,
+        between,
+    )
+
+
+def attention_kernel(where_ref, recv_ref, place_row_ref, place_col_ref, place_half_ref, out_ref):
     single, half = jnp.float32, jnp.bfloat16
     scale = 1.0 / math.sqrt(HD)
     rows = 128
@@ -518,18 +932,19 @@
     )
 
 
-def attention(recv, places, y):
+def attention(recv, places, where, y, earlier):
     length = places.shape[0]
     halves = pick(places.reshape(CTX, Y_PLACES, length // CTX // Y_PLACES), y, 1).reshape(-1)
-    return pl.pallas_call(
+    [out] = call(
         attention_kernel,
-        out_shape=jax.ShapeDtypeStruct(recv.shape, recv.dtype),
-        compiler_params=pltpu.CompilerParams(vmem_limit_bytes=48 * 1024 * 1024),
-        cost_estimate=pl.CostEstimate(
-            flops=7 * 2 * 1536 * 1024 * 128, bytes_accessed=2 * recv.size * 2, transcendentals=1536 * 1024
-        ),
-        name="attention",
-    )(recv, places[None, :], places[:, None], halves[:, None])
+        [(recv.shape, recv.dtype)],
+        [recv, places[None, :], places[:, None], halves[:, None]],
+        where,
+        "attention",
+        0.1,
+        earlier=earlier,
+    )
+    return out
 
 
 def moment_kernel(where_ref, grads_ref, *refs):
@@ -560,6 +975,9 @@
         ),
         out_shape=shapes + shapes,
         compiler_params=pltpu.CompilerParams(vmem_limit_bytes=32 * 1024 * 1024),
+        cost_estimate=pl.CostEstimate(
+            flops=0, bytes_accessed=int(100 * 3.6e6), transcendentals=0
+        ),
         name="moments",
     )(ctx_place.reshape(1), grads, *moments)
     return out[:4], out[4:]
@@ -573,13 +991,13 @@
         out_ref[...] = weight_ref[...] - rate * ortho_ref[0, 0, :, :cols].astype(jnp.float32)
 
 
-def write_weights(ortho, weights, ctx_place, shard_place):
+def write_weights(ortho, weights, ctx_place):
     rows = weights[0].shape[0] // CTX
     blocks = [pl.BlockSpec((rows, w.shape[1]), lambda i, where: (i, 0)) for w in weights]
 
-    def source(which):
+    def source(owner):
         return pl.BlockSpec(
-            (1, 1) + ortho.shape[2:], lambda i, where: (where[1] ^ which, i ^ where[0], 0, 0)
+            (1, 1) + ortho.shape[2:], lambda i, where: (owner, i ^ where[0], 0, 0)
         )
 
     return pl.pallas_call(
@@ -587,13 +1005,13 @@
         grid_spec=pltpu.PrefetchScalarGridSpec(
             num_scalar_prefetch=1,
             grid=(CTX,),
-            in_specs=[source(which) for which in range(4)] + blocks,
+            in_specs=[source(owner) for owner in OWNERS] + blocks,
             out_specs=blocks,
         ),
         out_shape=[jax.ShapeDtypeStruct(w.shape, w.dtype) for w in weights],
         compiler_params=pltpu.CompilerParams(vmem_limit_bytes=32 * 1024 * 1024),
         name="weights",
-    )(jnp.stack([ctx_place, shard_place]), ortho, ortho, ortho, ortho, *weights)
+    )(ctx_place.reshape(1), *[ortho] * 4, *weights)
 
 
 def local_fast(
@@ -630,234 +1048,198 @@
     hidden_part = hidden // SHARDS
     strip = part // CTX
 
-    small = jnp.zeros((16, width), half)
-    small = small.at[0].set(
-        jnp.concatenate([gain_first, shift_first, gain_second, shift_second]).astype(half)
-    )
-    small = small.at[1, : 2 * part].set(jnp.concatenate([output_bias, down_bias]).astype(half))
-    small = small.at[2, : 3 * part].set(heads_bias.astype(half))
-    packed = jnp.concatenate([residual_in[0], cotangent[0].astype(half), small], axis=0)
-    packs = [packed] + [swap(packed, "fsdp", k) for k in range(1, SHARDS)]
-    heads_split = jnp.moveaxis(
-        heads_weight.astype(half).reshape(part, 3, SHARDS, part), 2, 0
-    ).reshape(SHARDS, part, 3 * part)
-    heads_block = in_order(spread(heads_split, shard_place), shard_place).reshape(width, 3 * part)
-    up_split = jnp.moveaxis(up_weight.astype(half).reshape(part, SHARDS, hidden_part), 1, 0)
-    down_split = jnp.moveaxis(down_weight.astype(half).reshape(part, SHARDS, hidden_part), 1, 0)
-    mlp_split = jnp.concatenate([up_split, down_split], axis=-1)
-    mlp_block = in_order(spread(mlp_split, shard_place), shard_place).reshape(
-        width, 2 * hidden_part
-    )
-    up_block, down_block = mlp_block[:, :hidden_part], mlp_block[:, hidden_part:]
+    where = jnp.stack([z, y, shard_place, ctx_place]).astype(jnp.int32)
+
+    [packed] = call(
+        pack_kernel,
+        [((2 * rows + 16, width), half)],
+        [residual_in[0], cotangent[0]]
+        + [
+            v[None]
+            for v in (
+                gain_first,
+                shift_first,
+                gain_second,
+                shift_second,
+                output_bias,
+                down_bias,
+                heads_bias,
+            )
+        ],
+        where,
+        "pack",
+        0.1,
+    )
+    packs = [packed] + [swap(packed, "fsdp", k) for k in (1, 2)]
+    packs.append(swap(packs[2], "fsdp", 1))
+    [heads_split] = call(
+        heads_split_kernel, [((SHARDS, part, 3 * part), half)], [heads_weight], where, "heads_split", 0.1
+    )
+    heads_block = exchange(heads_split).reshape(width, 3 * part)
+    moments_all = (heads_moment, output_moment, up_moment, down_moment)
+    weights_all = (heads_weight, output_weight, up_weight, down_weight)
+    strip_moments = [None] * SHARDS
+    for which in range(4):
+        moment = lax.dynamic_slice_in_dim(moments_all[which], ctx_place * strip, strip, 0)
+        strip_moments[OWNERS[which]] = jnp.pad(moment, ((0, 0), (0, hidden - moment.shape[1])))
+    mlp_split = call(
+        mlp_split_kernel,
+        [((part + 2 * strip, 2 * hidden_part), half)] * SHARDS,
+        [up_weight, down_weight, jnp.stack(strip_moments)],
+        where,
+        "mlp_split",
+        0.1,
+        earlier=[heads_block],
+    )
+    mlp_pieces = [mlp_split[0]] + [swap(mlp_split[k], "fsdp", k) for k in range(1, SHARDS)]
     output_block = output_weight.astype(half)
-
-    tokens = jnp.stack([p[:rows] for p in packs])
-    grad_half = jnp.stack([p[rows : 2 * rows] for p in packs]).reshape(SHARDS * rows, width)
-    vectors = in_order([p[2 * rows :] for p in packs], shard_place).astype(single)
-    gain_one, shift_one, gain_two, shift_two = [
-        vectors[:, 0, i * part : (i + 1) * part].reshape(width) for i in range(4)
-    ]
-    output_shift, down_shift = [
-        vectors[:, 1, i * part : (i + 1) * part].reshape(width) for i in range(2)
-    ]
-    heads_shift = pick(
-        vectors[:, 2, : 3 * part].reshape(3, SHARDS, part), shard_place, 1
-    ).reshape(3 * part)
-    up_shift = up_bias.astype(half).astype(single)
-
-    inputs = tokens.astype(single).reshape(SHARDS * rows, width)
-    average = jnp.mean(inputs, axis=-1, keepdims=True)
-    centred = inputs - average
-    variance = jnp.mean(centred * centred, axis=-1, keepdims=True)
-    inverse = lax.rsqrt(variance + norm_eps)
-    normed = centred * inverse
-    first_in = (normed * gain_one + shift_one).astype(half)
-    second_in = (normed * gain_two + shift_two).astype(half)
-
-    projected = jnp.dot(first_in, heads_block, preferred_element_type=single) + heads_shift
+    vectors = sum(p[2 * rows :].astype(single) for p in packs)
+
     places = slot_places(group_order, 0, length, group)
     query_places = slot_places(group_order, ctx_place * rows, rows, group)
     cosine, sine = rotary_tables(query_places)
-    rest = HD - ROT
-    turn_cos = jnp.concatenate([cosine, cosine, jnp.ones((rows, rest), single)], axis=1)
-    turn_sin = jnp.concatenate([sine, sine, jnp.zeros((rows, rest), single)], axis=1)
-    turn_cos = jnp.tile(turn_cos, (SHARDS, 2 * part // HD))
-    turn_sin = jnp.tile(turn_sin, (SHARDS, 2 * part // HD))
-    lane = jnp.arange(2 * part)
-    inside = lane % HD
-    other = jnp.where(inside < ROT // 2, lane + ROT // 2, lane - ROT // 2)
-    sign = jnp.where(inside < ROT // 2, -1.0, 1.0) * (inside < ROT)
-    partner = jnp.where(lane[:, None] == other[None, :], sign[None, :], 0.0).astype(single)
-
-    def turned(x, direction):
-        moved = jnp.dot(x, partner, precision=lax.Precision.HIGHEST, preferred_element_type=single)
-        return x * turn_cos + direction * (moved * turn_sin)
-
-    turned_half = turned(projected[:, : 2 * part], 1.0).astype(half)
-    attn_delta = lax.dot_general(
-        grad_half, output_block, (((1,), (1,)), ((), ())), preferred_element_type=single
+    none, rest = jnp.zeros((rows, ROT // 2), single), jnp.zeros((rows, HD - ROT), single)
+    turn_cos, turn_high, turn_low = [
+        jnp.tile(jnp.concatenate(t, axis=1), (1, 2 * part // HD))
+        for t in ([cosine, cosine, rest + 1.0], [none, sine, rest], [-sine, none, rest])
+    ]
+
+    first_in, second_in, grad_half, payload, my_normed, inverse = call(
+        pre_kernel,
+        [
+            ((SHARDS * rows, width), half),
+            ((SHARDS * rows, width), half),
+            ((SHARDS * rows, width), half),
+            ((CTX, 3 * rows + rows // 2, 2 * HD), half),
+            ((rows, width), single),
+            ((rows, 128), single),
+        ],
+        list(packs) + [heads_block, output_block, turn_cos, turn_high, turn_low],
+        where,
+        "pre",
+        0.1,
+    )
+    my_inverse = inverse[:, :1]
+    sent = exchange(payload, "ctx")
+    done = attention(sent, places, where, y, mlp_pieces[2:3])
+    back = exchange(done, "ctx")
+
+    mlp_send, mlp_keep, mlp_part, up_sum, second_part = call(
+        mlp_kernel,
+        [
+            ((SHARDS, Z_PLACES, strip, 2 * hidden_part), half),
+            ((SHARDS, Z_PLACES, strip, 2 * hidden_part), single),
+            ((SHARDS * rows, width), single),
+            ((1, hidden_part), single),
+            ((SHARDS * rows, width), single),
+        ],
+        [second_in, grad_half, up_bias.astype(half).astype(single)[None]] + mlp_pieces,
+        where,
+        "mlp",
+        0.1,
+        [
+            pltpu.VMEM((width, 2 * hidden_part), half),
+            pltpu.VMEM((width, 2 * hidden_part), single),
+        ],
+    )
+    mlp_came, mlp_sums = scatter_ctx(mlp_send, mlp_keep, where, "mlp_z")
+
+    send, keep, heads_sum, mine, home = call(
+        post_kernel,
+        [
+            ((SHARDS, Z_PLACES, strip, width), half),
+            ((SHARDS, Z_PLACES, strip, width), single),
+            ((1, 3 * part), single),
+            ((3 * rows, width), single),
+            ((SHARDS, 3 * rows, width), half),
+        ],
+        [back, first_in, grad_half, heads_block, output_block, mlp_part, second_part]
+        + [turn_cos, turn_high, turn_low],
+        where,
+        "post",
+        0.1,
+        [
+            pltpu.VMEM((SHARDS * rows, part), half),
+            pltpu.VMEM((SHARDS * rows, 3 * part), half),
+            pltpu.VMEM((width, width), single),
+        ],
+        [mlp_sums[0]],
+    )
+    _, heads_sums = scatter_ctx(send, keep, where, "heads_z")
+    home = exchange(home)
+    total = mine + jnp.sum(home.astype(single), axis=0)
+    block_out = (
+        residual_in[0].astype(single) + (total[:rows] + vectors[4] + vectors[5])
     ).astype(half)
-    query = turned_half[:, :part].reshape(SHARDS, rows, part)
-    keys = turned_half[:, part:].reshape(SHARDS, rows, part)
-    values = projected[:, 2 * part :].astype(half).reshape(SHARDS, rows, part)
-    outer = attn_delta.reshape(SHARDS, rows, part)
-
-    def beside(a, b, head):
-        cut = slice(head * HD, (head + 1) * HD)
-        return jnp.concatenate([a[..., cut], b[..., cut]], axis=-1)
-
-    shared_rows = beside(query, outer, 2).reshape(SHARDS, Y_PLACES, rows // 2, 2 * HD)
-    shared_keys = beside(keys, values, 2)
-    payload = jnp.stack(
-        [
-            jnp.concatenate(
-                [
-                    beside(query, keys, head),
-                    beside(values, outer, head),
-                    shared_keys,
-                    shared_rows[:, head],
-                ],
-                axis=1,
-            )
-            for head in range(Y_PLACES)
-        ],
-        axis=1,
-    ).reshape(CTX, 3 * rows + rows // 2, 2 * HD)
-    sent = lax.all_to_all(payload, "ctx", 0, 0)
-    done = attention(sent, places, y)
-    back = lax.all_to_all(done, "ctx", 0, 0).reshape(
-        Z_PLACES, Y_PLACES, 3 * rows + rows // 2, 2 * HD
-    )
-
-    up_pre = jnp.dot(second_in, up_block, preferred_element_type=single) + up_shift
-    active = gelu_value(up_pre).astype(half)
-    up_delta = jnp.dot(grad_half, down_block, preferred_element_type=single) * gelu_slope(up_pre)
-    up_half = up_delta.astype(half)
-
-    def over_tokens(a, b):
-        return lax.dot_general(a, b, (((0,), (0,)), ((), ())), preferred_element_type=single)
-
-    def over_columns(a, b):
-        return lax.dot_general(a, b, (((1,), (1,)), ((), ())), preferred_element_type=single)
-
-    up_local = over_tokens(second_in, up_half).reshape(SHARDS, CTX, strip, hidden_part)
-    down_local = over_tokens(grad_half, active).reshape(SHARDS, CTX, strip, hidden_part)
-    up_strip = scatter_ctx(up_local, ctx_place, 1)
-    down_strip = scatter_ctx(down_local, ctx_place, 1)
-    mlp_part = over_columns(active, down_block)
-    second_part = over_columns(up_half, up_block)
-
-    early, late = back[..., :HD], back[..., HD:]
-    attn = jnp.concatenate(
-        [early[:, 0, :rows], early[:, 1, :rows], early[:, :, 3 * rows :].reshape(SHARDS, rows, HD)],
-        axis=-1,
-    ).reshape(SHARDS * rows, part)
-    query_grad = jnp.concatenate(
-        [late[:, 0, :rows], late[:, 1, :rows], late[:, :, 3 * rows :].reshape(SHARDS, rows, HD)],
-        axis=-1,
-    ).astype(single)
-    wide = back[:, :, rows : 3 * rows].astype(single)
-    shared = wide[:, 0, rows:] + wide[:, 1, rows:]
-    key_grad = jnp.concatenate(
-        [wide[:, 0, :rows, :HD], wide[:, 1, :rows, :HD], shared[..., :HD]], axis=-1
-    )
-    value_grad = jnp.concatenate(
-        [wide[:, 0, :rows, HD:], wide[:, 1, :rows, HD:], shared[..., HD:]], axis=-1
-    )
-    turned_grad = turned(
-        jnp.concatenate([query_grad, key_grad], axis=-1).reshape(SHARDS * rows, 2 * part), -1.0
-    )
-    heads_delta = jnp.concatenate([turned_grad, value_grad.reshape(SHARDS * rows, part)], axis=-1)
-    heads_half = heads_delta.astype(half)
-    heads_local = over_tokens(first_in, heads_half).reshape(SHARDS, CTX, strip, 3 * part)
-    output_local = over_tokens(attn, grad_half).reshape(CTX, strip, width)
-    heads_strip = scatter_ctx(heads_local, ctx_place, 1)
-    output_strip = scatter_ctx(output_local, ctx_place, 0)
-    output_part = jnp.dot(attn, output_block, preferred_element_type=single)
-    first_part = over_columns(heads_half, heads_block)
-
-    def home(x):
-        x = x.reshape(SHARDS, rows, width)
-        total = x[0]
-        for k in range(1, SHARDS):
-            total = total + swap(x[k].astype(half), "fsdp", k).astype(single)
-        return total
-
-    mine = inputs[:rows]
-    block_out = (mine + (home(output_part + mlp_part) + output_shift + down_shift)).astype(half)
-    second_delta = home(second_part)
-    first_delta = home(first_part)
-    my_normed, my_inverse = normed[:rows], inverse[:rows]
+    first_delta, second_delta = total[rows : 2 * rows], total[2 * rows :]
     input_grad = (
         cotangent[0]
-        + norm_back(first_delta, my_normed, my_inverse, gain_one)
-        + norm_back(second_delta, my_normed, my_inverse, gain_two)
-    )
-
-    strips = jnp.concatenate([heads_strip, up_strip, down_strip], axis=-1).astype(half)
-    whole = in_order(spread(strips, shard_place), shard_place)
-    heads_grad = jnp.moveaxis(
-        whole[..., : 3 * part].reshape(SHARDS, strip, 3, part), 0, 2
-    ).reshape(strip, 3 * width)
-    up_grad = jnp.moveaxis(whole[..., 3 * part : 3 * part + hidden_part], 0, 1).reshape(
-        strip, hidden
-    )
-    down_grad = jnp.moveaxis(whole[..., 3 * part + hidden_part :], 0, 1).reshape(strip, hidden)
-    strip_grads = (heads_grad, output_strip.astype(half), up_grad, down_grad)
-    moments_all = (heads_moment, output_moment, up_moment, down_moment)
-    weights_all = (heads_weight, output_weight, up_weight, down_weight)
-    nests = []
-    for which in range(4):
-        grad = strip_grads[which].astype(single)
-        moment = mom_rate * lax.dynamic_slice_in_dim(
-            moments_all[which], ctx_place * strip, strip, 0
-        ) + grad
-        nest = (grad + mom_rate * moment).astype(half)
-        nests.append(jnp.pad(nest, ((0, 0), (0, hidden - nest.shape[1]))))
-    owned = jnp.stack(spread(jnp.stack(nests), shard_place))
-    nest = jnp.stack(gather_ctx(owned)).reshape(width, hidden)
-    grads_all = jnp.stack(gather_ctx(jnp.concatenate(strip_grads, axis=-1)))
-    full_grads, new_moments = write_moments(grads_all, moments_all, ctx_place)
-
-    wide_nest = nest.astype(single)
-    size = jnp.sqrt(jnp.sum(wide_nest * wide_nest))
-    ortho = (wide_nest / (size + 1e-07)).astype(half)
-    for turn in range(NS_ITERS):
-        gram = over_columns(ortho, ortho).astype(half)
-        mix = (
-            schulz_coeffs[1] * gram.astype(single)
-            + schulz_coeffs[2] * jnp.dot(gram, gram, preferred_element_type=single)
-        ).astype(half)
-        ortho = (
-            schulz_coeffs[0] * ortho.astype(single)
-            + jnp.dot(mix, ortho, preferred_element_type=single)
-        ).astype(half)
-    ortho = ortho.reshape(CTX, SHARDS, strip, hidden)
-    arrived = jnp.stack(
-        [ortho[:, 0]] + [swap(ortho[:, k], "fsdp", k) for k in range(1, SHARDS)]
-    )
-    new_weights = write_weights(arrived, weights_all, ctx_place, shard_place)
-
-    heads_sum = jnp.sum(heads_delta, axis=0).reshape(3, 1, part)
+        + norm_back(first_delta, my_normed, my_inverse, vectors[0])
+        + norm_back(second_delta, my_normed, my_inverse, vectors[2])
+    )
+
     heads_sum = lax.dynamic_update_slice(
-        jnp.zeros((3, SHARDS, part), single), heads_sum, (0, shard_place, 0)
+        jnp.zeros((3, SHARDS, part), single),
+        heads_sum.reshape(3, 1, part),
+        (0, shard_place, 0),
     ).reshape(3 * width)
     up_sum = lax.dynamic_update_slice(
-        jnp.zeros((hidden,), single), jnp.sum(up_delta, axis=0), (shard_place * hidden_part,)
-    )
-    sums = lax.psum(
-        jnp.concatenate(
-            [
-                jnp.sum(first_delta * my_normed, axis=0),
-                jnp.sum(first_delta, axis=0),
-                jnp.sum(second_delta * my_normed, axis=0),
-                jnp.sum(second_delta, axis=0),
-                jnp.sum(cotangent[0], axis=0),
-                heads_sum,
-                up_sum,
-            ]
-        ),
-        ("ctx", "fsdp"),
+        jnp.zeros((hidden,), single), up_sum[0], (shard_place * hidden_part,)
+    )
+    sums = jnp.concatenate(
+        [
+            jnp.sum(first_delta * my_normed, axis=0),
+            jnp.sum(first_delta, axis=0),
+            jnp.sum(second_delta * my_normed, axis=0),
+            jnp.sum(second_delta, axis=0),
+            jnp.sum(cotangent[0], axis=0),
+            heads_sum,
+            up_sum,
+        ]
+    ).reshape(-1, 128)
+    sums = sums + sum(swap(sums, "fsdp", k) for k in range(1, SHARDS))
+
+    strips, owned, output_strip = call(
+        strip_kernel,
+        [
+            ((SHARDS, strip, 2 * hidden_part + 3 * part), half),
+            ((SHARDS, SHARDS, strip, width), half),
+            ((strip, width), single),
+        ],
+        heads_sums + mlp_sums,
+        where,
+        "strip",
+        0.1,
+        earlier=[home],
+    )
+    owned, strips = call(
+        owned_kernel,
+        [((SHARDS, strip, hidden), half), (strips.shape, half)],
+        [exchange(owned), strips] + mlp_pieces,
+        where,
+        "owned",
+        0.1,
+    )
+    pieces = gather_y(gather_z(owned))
+    [grads] = call(
+        grads_kernel,
+        [((strip, 4 * width + 2 * hidden), half)],
+        [exchange(strips), output_strip],
+        where,
+        "grads",
+        0.1,
+        earlier=pieces[1:],
+    )
+    grads_along = gather_z(grads)
+
+    sums = sums + swap(sums, "ctx", 1)
+    ortho, sums = newton(pieces, sums, where, [grads], grads_along[1:])
+    sums = sums + sum(swap(sums, "ctx", Y_PLACES * k) for k in range(1, Z_PLACES))
+    sums = sums.reshape(-1)
+    arrived = exchange(ortho)
+    new_weights = write_weights(arrived, weights_all, ctx_place)
+    full_grads, new_moments = write_moments(
+        jnp.stack(gather_y(grads_along)), moments_all, ctx_place
     )
     pieces = [sums[i * width : (i + 1) * width] for i in range(5)]
     heads_total = sums[5 * width : 8 * width]

time: 706 us -> 437 us (0.62)
  matrix products: 125 us -> 0 us
  local copies, waits for them, and re-layouts: 142 us -> 59.1 us
  other arithmetic: 108 us -> 25.7 us
  Pallas kernels: 24.1 us -> 106 us
  blocking collectives: 40.8 us -> 0 us
  waiting for transfers between devices: 177 us -> 156 us
  starting transfers between devices: 68.5 us -> 78.1 us
    dot_general x24 -> x0, matrix products: 125 us -> none  [the longest x5 63.3 us: local_fast(): jnp.dot(mix, ortho, preferred_element_type=single)]
    pallas_call x1 -> x14, Pallas kernels: 11.1 us -> 92 us  [call(): pl.pallas_call(body, in_specs=[pl.BlockSpec(memory_space=pltpu.SMEM)] + [...]
    psum x1 -> x0, blocking collectives: 40.8 us -> none  [local_fast(): lax.psum(jnp.concatenate([jnp.sum(first_delta * my_normed, axis=0), jnp.s...]
    ppermute x57 -> x35, waiting for transfers between devices: 177 us -> 138 us  [swap(): return lax.ppermute(x, axis, [(i, i ^ offset) for i in range(count)])]
    another operation x24 -> x2, other arithmetic: 27.1 us -> 1.17 us  [the longest x1 1.1 us: local_fast(): jnp.stack(strip_moments)]
    all_to_all x2 -> x7, starting transfers between devices: 10.8 us -> 34.1 us  [exchange(): return lax.all_to_all(x, axis, 0, 0)]
    reshape x13 -> x1, local copies, waits for them, and re-layouts: 22.9 us -> 0.08 us  [local_fast(): heads_sum.reshape(3, 1, part)]
    another operation x20 -> x9, local copies, waits for them, and re-layouts: 22.5 us -> 3.41 us  [the longest x2 1.94 us: local_fast(): jnp.stack(strip_moments)]
  transfers between devices with their start and end apart: 59 -> 42, of which waited for: 23 -> 14; matrix products, arithmetic and copies ran while one was open for 48% -> 10% of each run, Pallas kernels for 3% -> 19%
where the time goes in v2:
time: 437 us; the launch traced here: 431 us
  waiting for transfers between devices  156 us (36%)
  Pallas kernels  106 us (24%)
  starting transfers between devices  78.1 us (18%)
  local copies, waits for them, and re-layouts  59.1 us (14%)
  other arithmetic  25.7 us (6%)
  between operations  6.67 us (2%)
    ppermute x35, waiting for transfers between devices, swap(): return lax.ppermute(x, axis, [(i, i ^ offset) for i in range(count)])  138 us
    pallas_call x14, Pallas kernels, call(): pl.pallas_call(body, in_specs=[pl.BlockSpec(memory_space=pltpu.SMEM)] + [...  92 us
    unnamed x184, local copies, waits for them, and re-layouts  50.1 us
    ppermute x35, starting transfers between devices, swap(): return lax.ppermute(x, axis, [(i, i ^ offset) for i in range(count)])  43.9 us
    all_to_all x7, starting transfers between devices, exchange(): return lax.all_to_all(x, axis, 0, 0)  34.1 us
    all_to_all x7, waiting for transfers between devices, exchange(): return lax.all_to_all(x, axis, 0, 0)  17.5 us
    sub x8, other arithmetic, local_fast(): vector_values[which]  10.2 us
  transfers between devices with their start and end apart: 42, of which 14 were waited for; matrix products, arithmetic and copies ran while one was open for 10% of the time, Pallas kernels for 19%

profile of v2, /device:TPU:0, one launch (start us, length us, event | category | flops | bytes accessed | tf_op | source)
XLA Modules:
  0.0 430.9 jit_solution(18274469858822093753)
XLA Ops:
  8.1 3.0 collective-permute-start.1
  11.1 1.5 copy-done.4
  12.6 1.7 heads_split.1
  14.3 3.6 all-to-all-start
  22.7 8.9 %all-to-all-done = bf16[4,192,576]{2,1,0:T(8,128)(2,1)S(1)} async-done(((bf16[4,192,576]{2,1,0:T(8,128)(2,1)}), bf16[4,192,576]{2,1,0:T(8,128)(2,1)S(1)}, u32[]{:S(2)}, u32[]{:S(2)}) %all-to-all-start) | async-done | bytes 884768 | tf_op jit(solution)/shard_map/all_to_all | solution.py:421
  32.6 4.2 pre.1
  38.5 6.5 %all-to-all-start.1 = ((bf16[8,448,128]{2,1,0:T(8,128)(2,1)}), bf16[8,448,128]{2,1,0:T(8,128)(2,1)S(1)}, u32[]{:S(2)}, u32[]{:S(2)}) async-start(bf16[8,448,128]{2,1,0:T(8,128)(2,1)} %get-tuple-element.77), calls=%async_computation.1 | async-start | bytes 1835008 | tf_op jit(solution)/shard_map/all_to_all | solution.py:421
  47.2 3.9 mlp_split.1
  57.1 1.9 fusion.refs_3_
  59.0 13.4 %collective-permute-done.3.refs_5_.refs_6_ = bf16[240,1536]{1,0:T(8,128)(2,1)S(1)} collective-permute-done((bf16[240,1536]{1,0:T(8,128)(2,1)}, bf16[240,1536]{1,0:T(8,128)(2,1)S(1)}, u32[]{:S(2)}, u32[]{:S(2)}) %collective-permute-start.3) | collective-permute-done | bytes 737312 | tf_op jit(solution)/shard_map/ppermute | solution.py:417
  74.7 10.9 %attention.1 = bf16[8,448,128]{2,1,0:T(8,128)(2,1)} custom-call(s32[4]{0:T(128)S(1)} %pad_add_fusion.refs_0_, bf16[8,448,128]{2,1,0:T(8,128)(2,1)S(1)} %all-to-all-done.1.refs_1_, s32[1,1024]{1,0:T(1,128)S(1)} %fusion.12.refs_2_, s32[1024,1]{1,0:T(8,128)S(1)} %copy-done.32, s32[512,1]{1,0:T(8,128)S(1)} %copy-done.46, ...), custom_call_target="tpu_custom_call" | custom-call | bytes 360000 | tf_op jit(solution)/shard_map/attention/pallas_call | solution.py:446
  85.6 6.4 %all-to-all-start.2 = ((bf16[8,448,128]{2,1,0:T(8,128)(2,1)}), bf16[8,448,128]{2,1,0:T(8,128)(2,1)}, u32[]{:S(2)}, u32[]{:S(2)}) async-start(bf16[8,448,128]{2,1,0:T(8,128)(2,1)} %attention.1), calls=%async_computation.2 | async-start | bytes 1835008 | tf_op jit(solution)/shard_map/all_to_all | solution.py:421
  92.0 7.9 %mlp.1 = (bf16[4,4,24,1536]{3,2,1,0:T(8,128)(2,1)}, f32[4,4,24,1536]{3,2,1,0:T(8,128)}, f32[512,768]{1,0:T(8,128)}, f32[1,768]{1,0:T(1,128)S(1)}, f32[512,768]{1,0:T(8,128)}) custom-call(s32[4]{0:T(128)S(1)} %pad_add_fusion.refs_0_, bf16[512,768]{1,0:T(8,128)(2,1)S(1)} %copy-done.49, bf16[512,768]{1,0:T(8,128)(2,1)} %get-tuple-element.80.refs_2_.refs_3_, ...), custom_call_target="tpu_custom_call" | custom-call | bytes 360000 | tf_op jit(solution)/shard_map/mlp/pallas_call | solution.py:446
  100.0 2.1 collective-permute-start.6
  102.1 26.2 %collective-permute-done.6.refs_2_ = bf16[4,4,24,1536]{3,2,1,0:T(8,128)(2,1)S(1)} collective-permute-done((bf16[4,4,24,1536]{3,2,1,0:T(8,128)(2,1)}, bf16[4,4,24,1536]{3,2,1,0:T(8,128)(2,1)S(1)}, u32[]{:S(2)}, u32[]{:S(2)}) %collective-permute-start.6) | collective-permute-done | bytes 1179680 | tf_op jit(solution)/shard_map/ppermute | solution.py:417
  128.3 2.0 mlp_z.1
  135.5 6.6 %post.1 = (bf16[4,4,24,768]{3,2,1,0:T(8,128)(2,1)S(1)}, f32[4,4,24,768]{3,2,1,0:T(8,128)}, f32[1,576]{1,0:T(1,128)S(1)}, f32[384,768]{1,0:T(8,128)}, bf16[4,384,768]{2,1,0:T(8,128)(2,1)}) custom-call(s32[4]{0:T(128)S(1)} %pad_add_fusion.refs_0_, bf16[8,448,128]{2,1,0:T(8,128)(2,1)} %all-to-all-done.2.refs_1_, bf16[512,768]{1,0:T(8,128)(2,1)S(1)} %copy-done.48, ...), custom_call_target="tpu_custom_call" | custom-call | bytes 360000 | tf_op jit(solution)/shard_map/post/pallas_call | solution.py:446
  142.9 4.6 %all-to-all-start.3 = ((bf16[4,384,768]{2,1,0:T(8,128)(2,1)}), bf16[4,384,768]{2,1,0:T(8,128)(2,1)}, u32[]{:S(2)}, u32[]{:S(2)}) async-start(bf16[4,384,768]{2,1,0:T(8,128)(2,1)} %get-tuple-element.91), calls=%async_computation.3 | async-start | bytes 4718592 | tf_op jit(solution)/shard_map/all_to_all | solution.py:421
  147.8 1.5 collective-permute-start.11
  149.3 1.6 collective-permute-start.12
  150.9 1.4 collective-permute-start.13
  153.1 10.4 %collective-permute-done.7.refs_2_ = bf16[4,4,24,768]{3,2,1,0:T(8,128)(2,1)S(1)} collective-permute-done((bf16[4,4,24,768]{3,2,1,0:T(8,128)(2,1)}, bf16[4,4,24,768]{3,2,1,0:T(8,128)(2,1)S(1)}, u32[]{:S(2)}, u32[]{:S(2)}) %collective-permute-start.7) | collective-permute-done | bytes 589856 | tf_op jit(solution)/shard_map/ppermute | solution.py:417
  166.8 1.4 collective-permute-start.8
  168.2 1.5 collective-permute-start.9
  169.7 1.5 collective-permute-start.10
  173.1 2.2 collective-permute-done.8.refs_2_
  175.4 13.4 %collective-permute-done.9.refs_3_ = bf16[4,24,768]{2,1,0:T(8,128)(2,1)S(1)} collective-permute-done((bf16[4,24,768]{2,1,0:T(8,128)(2,1)}, bf16[4,24,768]{2,1,0:T(8,128)(2,1)S(1)}, u32[]{:S(2)}, u32[]{:S(2)}) %collective-permute-start.9) | collective-permute-done | bytes 147488 | tf_op jit(solution)/shard_map/ppermute | solution.py:417
  189.8 2.2 strip.1
  192.7 3.5 all-to-all-start.4
  196.2 2.2 convert_reduce_fusion
  199.9 1.8 collective-permute-start.23
  202.0 4.2 all-to-all-done.4.refs_1_
  207.2 2.6 owned.1
  210.6 2.1 collective-permute-start.19
  212.6 2.1 collective-permute-start.17
  215.1 2.0 collective-permute-start.14
  217.0 12.0 %collective-permute-done.19.refs_8_.refs_7_ = bf16[4,24,3072]{2,1,0:T(8,128)(2,1)} collective-permute-done((bf16[4,24,3072]{2,1,0:T(8,128)(2,1)}, bf16[4,24,3072]{2,1,0:T(8,128)(2,1)}, u32[]{:S(2)}, u32[]{:S(2)}) %collective-permute-start.19) | collective-permute-done | bytes 589856 | tf_op jit(solution)/shard_map/ppermute | solution.py:417
  229.1 1.9 collective-permute-start.20
  231.0 33.8 %collective-permute-done.17.refs_6_.refs_5_ = bf16[4,24,3072]{2,1,0:T(8,128)(2,1)S(1)} collective-permute-done((bf16[4,24,3072]{2,1,0:T(8,128)(2,1)}, bf16[4,24,3072]{2,1,0:T(8,128)(2,1)S(1)}, u32[]{:S(2)}, u32[]{:S(2)}) %collective-permute-start.17) | collective-permute-done | bytes 589856 | tf_op jit(solution)/shard_map/ppermute | solution.py:417
  264.7 1.9 collective-permute-start.18
  266.8 4.3 %all-to-all-start.5 = ((bf16[4,24,2112]{2,1,0:T(8,128)(2,1)}), bf16[4,24,2112]{2,1,0:T(8,128)(2,1)}, u32[]{:S(2)}, u32[]{:S(2)}) async-start(bf16[4,24,2112]{2,1,0:T(8,128)(2,1)} %copy-done.56), calls=%async_computation.5 | async-start | bytes 835584 | tf_op jit(solution)/shard_map/all_to_all | solution.py:421
  272.0 2.0 collective-permute-start.24
  273.9 2.5 add_bitcast_fusion
  276.4 17.2 %collective-permute-done.24 = f32[72,128]{1,0:T(8,128)S(1)} collective-permute-done((f32[72,128]{1,0:T(8,128)S(1)}, f32[72,128]{1,0:T(8,128)S(1)}, u32[]{:S(2)}, u32[]{:S(2)}) %collective-permute-start.24) | collective-permute-done | bytes 36896 | tf_op jit(solution)/shard_map/ppermute | solution.py:417
  294.3 2.2 grads.1.refs_9_
  296.5 1.8 collective-permute-start.31
  298.4 2.1 collective-permute-start.27
  300.7 2.0 collective-permute-start.25
  309.1 34.1 %newton.1.refs_1_ = bf16[768,3072]{1,0:T(8,128)(2,1)} custom-call(s32[4]{0:T(128)S(1)} %pad_add_fusion.refs_0_, bf16[4,24,3072]{2,1,0:T(8,128)(2,1)} %get-tuple-element.105.refs_1_, bf16[4,24,3072]{2,1,0:T(8,128)(2,1)S(1)} %copy-done.26, bf16[4,24,3072]{2,1,0:T(8,128)(2,1)S(1)} %copy-done.24, bf16[4,24,3072]{2,1,0:T(8,128)(2,1)S(1)} %copy-done.30, ...), custom_call_target="tpu_custom_call" | custom-call | bytes 129600000 | tf_op jit(solution)/shard_map/newton/pallas_call | solution.py:446
  344.0 11.7 %last_newton.1 = (bf16[4,8,24,3072]{3,2,1,0:T(8,128)(2,1)}, f32[72,128]{1,0:T(8,128)}) custom-call(s32[4]{0:T(128)S(1)} %pad_add_fusion.refs_0_, bf16[768,3072]{1,0:T(8,128)(2,1)} %newton.1.refs_1_, f32[72,128]{1,0:T(8,128)S(1)} %copy-done.59, bf16[24,9216]{1,0:T(8,128)(2,1)S(1)} %collective-permute-done.25.refs_3_, ...), custom_call_target="tpu_custom_call" | custom-call | bytes 32400000 | tf_op jit(solution)/shard_map/last_newton/pallas_call | solution.py:446
  355.7 2.2 collective-permute-start.30
  357.9 2.2 collective-permute-start.28
  360.2 5.1 %all-to-all-start.6 = ((bf16[4,8,24,3072]{3,2,1,0:T(8,128)(2,1)}), bf16[4,8,24,3072]{3,2,1,0:T(8,128)(2,1)}, u32[]{:S(2)}, u32[]{:S(2)}) async-start(bf16[4,8,24,3072]{3,2,1,0:T(8,128)(2,1)} %get-tuple-element.115), calls=%async_computation.6 | async-start | bytes 9437184 | tf_op jit(solution)/shard_map/all_to_all | solution.py:421
  365.7 1.7 collective-permute-start.33
  381.1 1.5 multiply_subtract_fusion
  389.4 7.7 %collective-permute-done.32 = bf16[24,9216]{1,0:T(8,128)(2,1)} collective-permute-done((bf16[24,9216]{1,0:T(8,128)(2,1)}, bf16[24,9216]{1,0:T(8,128)(2,1)}, u32[]{:S(2)}, u32[]{:S(2)}) %collective-permute-start.32) | collective-permute-done | bytes 442400 | tf_op jit(solution)/shard_map/ppermute | solution.py:417
  402.4 1.9 copy-done.7
  404.2 2.0 copy-done.8
  406.2 1.7 copy-done.13
  409.0 5.9 %moments.1 = (f32[192,2304]{1,0:T(8,128)}, f32[192,768]{1,0:T(8,128)}, f32[192,3072]{1,0:T(8,128)}, f32[192,3072]{1,0:T(8,128)}, f32[192,2304]{1,0:T(8,128)}, /*...) custom-call(s32[1]{0:T(128)} %bitcast.4.where_ref, bf16[8,24,9216]{2,1,0:T(8,128)(2,1)S(1)} %copy-done.8, ...), custom_call_target="tpu_custom_call" | custom-call | bytes 360000000 | tf_op jit(solution)/shard_map/moments/pallas_call | solution.py:965
  414.8 4.3 %all-to-all-done.6.refs_0_.refs_1_.refs_2_.refs_3_ = bf16[4,8,24,3072]{3,2,1,0:T(8,128)(2,1)} async-done(((bf16[4,8,24,3072]{3,2,1,0:T(8,128)(2,1)}), bf16[4,8,24,3072]{3,2,1,0:T(8,128)(2,1)}, u32[]{:S(2)}, u32[]{:S(2)}) %all-to-all-start.6) | async-done | bytes 4718624 | tf_op jit(solution)/shard_map/all_to_all | solution.py:421
  419.2 1.7 copy-done.3
  420.8 1.5 copy-done.5
  422.3 7.8 %weights.1 = (f32[192,2304]{1,0:T(8,128)}, f32[192,768]{1,0:T(8,128)}, f32[192,3072]{1,0:T(8,128)}, f32[192,3072]{1,0:T(8,128)}) custom-call(s32[1]{0:T(128)} %bitcast.4.where_ref, bf16[4,8,24,3072]{3,2,1,0:T(8,128)(2,1)} %all-to-all-done.6.refs_0_.refs_1_.refs_2_.refs_3_, bf16[4,8,24,3072]{3,2,1,0:T(8,128)(2,1)} %all-to-all-done.6.refs_0_.refs_1_.refs_2_.refs_3_, ...), custom_call_target="tpu_custom_call" | custom-call | tf_op jit(solution)/shard_map/weights/pallas_call | solution.py:1003
  (295 shorter events, 74.6 us)
Async XLA Ops:
  8.1 23.6 %copy-start.33 = (bf16[272,768]{1,0:T(8,128)(2,1)}, bf16[272,768]{1,0:T(8,128)(2,1)S(1)}, u32[]{:S(2)}) copy-start(bf16[272,768]{1,0:T(8,128)(2,1)S(1)} %pack.1.refs_1_) | copy-start | bytes 1253380
  8.1 12.8 %collective-permute-start.1 = (bf16[272,768]{1,0:T(8,128)(2,1)S(1)}, bf16[272,768]{1,0:T(8,128)(2,1)S(1)}, u32[]{:S(2)}, u32[]{:S(2)}) collective-permute-start(bf16[272,768]{1,0:T(8,128)(2,1)S(1)} %pack.1.refs_1_), channel_id=1, source_target_pairs={{0,2},{1,3},{2,0},{3,1},{4,6},{5,7},{6,4},{7,5},{8,10},{9,11},{10,... | collective-permute-start | bytes 1253384 | tf_op jit(solution)/shard_map/ppermute | solution.py:417
  11.1 11.6 %collective-permute-start = (bf16[272,768]{1,0:T(8,128)(2,1)S(1)}, bf16[272,768]{1,0:T(8,128)(2,1)}, u32[]{:S(2)}, u32[]{:S(2)}) collective-permute-start(bf16[272,768]{1,0:T(8,128)(2,1)S(1)} %pack.1.refs_1_), channel_id=1, source_target_pairs={{0,1},{1,0},{2,3},{3,2},{4,5},{5,4},{6,7},{7,6},{8,9},{9,8},{10,11... | collective-permute-start | bytes 1253384 | tf_op jit(solution)/shard_map/ppermute | solution.py:417
  14.3 17.4 %all-to-all-start = ((bf16[4,192,576]{2,1,0:T(8,128)(2,1)}), bf16[4,192,576]{2,1,0:T(8,128)(2,1)S(1)}, u32[]{:S(2)}, u32[]{:S(2)}) async-start(bf16[4,192,576]{2,1,0:T(8,128)(2,1)} %heads_split.1), calls=%async_computation | async-start | bytes 1966080 | tf_op jit(solution)/shard_map/all_to_all | solution.py:421
  18.6 18.2 %copy-start.37 = (f32[128,384]{1,0:T(8,128)}, f32[128,384]{1,0:T(8,128)S(1)}, u32[]{:S(2)}) copy-start(f32[128,384]{1,0:T(8,128)S(1)} %copy.60.refs_9_.refs_10_) | copy-start | bytes 589828
  18.8 18.0 %copy-start.39 = (f32[128,384]{1,0:T(8,128)}, f32[128,384]{1,0:T(8,128)S(1)}, u32[]{:S(2)}) copy-start(f32[128,384]{1,0:T(8,128)S(1)} %copy.59.refs_8_.refs_9_) | copy-start | bytes 589828
  19.0 17.8 %copy-start.41 = (f32[128,384]{1,0:T(8,128)}, f32[128,384]{1,0:T(8,128)S(1)}, u32[]{:S(2)}) copy-start(f32[128,384]{1,0:T(8,128)S(1)} %copy.58.refs_7_.refs_8_) | copy-start | bytes 589828
  19.0 17.8 %copy-start.14 = (bf16[192,768]{1,0:T(8,128)(2,1)}, bf16[192,768]{1,0:T(8,128)(2,1)S(1)}, u32[]{:S(2)}) copy-start(bf16[192,768]{1,0:T(8,128)(2,1)S(1)} %convert_element_type.40.refs_6_.refs_5_) | copy-start | bytes 884740
  20.9 17.5 %copy-start.52 = (bf16[272,768]{1,0:T(8,128)(2,1)}, bf16[272,768]{1,0:T(8,128)(2,1)S(1)}, u32[]{:S(2)}) copy-start(bf16[272,768]{1,0:T(8,128)(2,1)S(1)} %collective-permute-done.1.refs_3_) | copy-start | bytes 1253380
  20.9 10.8 %collective-permute-start.2 = (bf16[272,768]{1,0:T(8,128)(2,1)S(1)}, bf16[272,768]{1,0:T(8,128)(2,1)S(1)}, u32[]{:S(2)}, u32[]{:S(2)}) collective-permute-start(bf16[272,768]{1,0:T(8,128)(2,1)S(1)} %collective-permute-done.1.refs_3_), channel_id=1, source_target_pairs={{0,1},{1,0},{2,3},{3,2},{4,5},{5,4},{6,7},{7,6},{8,9},{9,8},{10,11... | collective-permute-start | bytes 1253384 | tf_op jit(solution)/shard_map/ppermute | solution.py:417
  38.5 34.0 %all-to-all-start.1 = ((bf16[8,448,128]{2,1,0:T(8,128)(2,1)}), bf16[8,448,128]{2,1,0:T(8,128)(2,1)S(1)}, u32[]{:S(2)}, u32[]{:S(2)}) async-start(bf16[8,448,128]{2,1,0:T(8,128)(2,1)} %get-tuple-element.77), calls=%async_computation.1 | async-start | bytes 1835008 | tf_op jit(solution)/shard_map/all_to_all | solution.py:421
  52.8 19.6 %collective-permute-start.3 = (bf16[240,1536]{1,0:T(8,128)(2,1)}, bf16[240,1536]{1,0:T(8,128)(2,1)S(1)}, u32[]{:S(2)}, u32[]{:S(2)}) collective-permute-start(bf16[240,1536]{1,0:T(8,128)(2,1)} %get-tuple-element.78), channel_id=1, source_target_pairs={{0,2},{1,3},{2,0},{3,1},{4,6},{5,7},{6,4},{7,5},{8,10},{9,11},{10,... | collective-permute-start | bytes 2211848 | tf_op jit(solution)/shard_map/ppermute | solution.py:417
  54.3 37.7 %collective-permute-start.4 = (bf16[240,1536]{1,0:T(8,128)(2,1)}, bf16[240,1536]{1,0:T(8,128)(2,1)S(1)}, u32[]{:S(2)}, u32[]{:S(2)}) collective-permute-start(bf16[240,1536]{1,0:T(8,128)(2,1)} %copy-done.71), channel_id=1, source_target_pairs={{0,1},{1,0},{2,3},{3,2},{4,5},{5,4},{6,7},{7,6},{8,9},{9,8},{10,11... | collective-permute-start | bytes 2211848 | tf_op jit(solution)/shard_map/ppermute | solution.py:417
  54.3 37.7 %collective-permute-start.5 = (bf16[240,1536]{1,0:T(8,128)(2,1)}, bf16[240,1536]{1,0:T(8,128)(2,1)}, u32[]{:S(2)}, u32[]{:S(2)}) collective-permute-start(bf16[240,1536]{1,0:T(8,128)(2,1)} %copy-done.70), channel_id=1, source_target_pairs={{0,3},{1,2},{2,1},{3,0},{4,7},{5,6},{6,5},{7,4},{8,11},{9,10},{10,... | collective-permute-start | bytes 2211848 | tf_op jit(solution)/shard_map/ppermute | solution.py:417
  57.1 34.9 %copy-start.81 = (f32[768]{0:T(1024)S(1)}, f32[768]{0:T(1024)}, u32[]{:S(2)}) copy-start(f32[768]{0:T(1024)} %param.31) | copy-start | bytes 9220
  72.4 19.6 %copy-start.6 = (bf16[240,1536]{1,0:T(8,128)(2,1)}, bf16[240,1536]{1,0:T(8,128)(2,1)S(1)}, u32[]{:S(2)}) copy-start(bf16[240,1536]{1,0:T(8,128)(2,1)S(1)} %collective-permute-done.3.refs_5_.refs_6_) | copy-start | bytes 2211844
  85.6 47.6 %all-to-all-start.2 = ((bf16[8,448,128]{2,1,0:T(8,128)(2,1)}), bf16[8,448,128]{2,1,0:T(8,128)(2,1)}, u32[]{:S(2)}, u32[]{:S(2)}) async-start(bf16[8,448,128]{2,1,0:T(8,128)(2,1)} %attention.1), calls=%async_computation.2 | async-start | bytes 1835008 | tf_op jit(solution)/shard_map/all_to_all | solution.py:421
  100.0 33.2 %copy-start.11 = (bf16[512,768]{1,0:T(8,128)(2,1)S(1)}, bf16[512,768]{1,0:T(8,128)(2,1)}, u32[]{:S(2)}) copy-start(bf16[512,768]{1,0:T(8,128)(2,1)} %get-tuple-element.80.refs_2_.refs_3_) | copy-start | bytes 2359300
  100.0 33.2 %copy-start.15 = (bf16[192,768]{1,0:T(8,128)(2,1)S(1)}, bf16[192,768]{1,0:T(8,128)(2,1)}, u32[]{:S(2)}) copy-start(bf16[192,768]{1,0:T(8,128)(2,1)} %copy-done.14) | copy-start | bytes 884740
  100.0 33.2 %copy-start.38 = (f32[128,384]{1,0:T(8,128)S(1)}, f32[128,384]{1,0:T(8,128)}, u32[]{:S(2)}) copy-start(f32[128,384]{1,0:T(8,128)} %copy-done.37) | copy-start | bytes 589828
  100.0 33.2 %copy-start.40 = (f32[128,384]{1,0:T(8,128)S(1)}, f32[128,384]{1,0:T(8,128)}, u32[]{:S(2)}) copy-start(f32[128,384]{1,0:T(8,128)} %copy-done.39) | copy-start | bytes 589828
  100.0 33.2 %copy-start.42 = (f32[128,384]{1,0:T(8,128)S(1)}, f32[128,384]{1,0:T(8,128)}, u32[]{:S(2)}) copy-start(f32[128,384]{1,0:T(8,128)} %copy-done.41) | copy-start | bytes 589828
  100.0 28.3 %collective-permute-start.6 = (bf16[4,4,24,1536]{3,2,1,0:T(8,128)(2,1)}, bf16[4,4,24,1536]{3,2,1,0:T(8,128)(2,1)S(1)}, u32[]{:S(2)}, u32[]{:S(2)}) collective-permute-start(bf16[4,4,24,1536]{3,2,1,0:T(8,128)(2,1)} %get-tuple-element.88), channel_id=1, source_target_pairs={{0,4},{4,0},{8,12},{12,8},{16,20},{20,16},{24,28},{28,24},{1,5},{5... | collective-permute-start | bytes 3538952 | tf_op jit(solution)/shard_map/ppermute | solution.py:417
  142.9 45.9 %all-to-all-start.3 = ((bf16[4,384,768]{2,1,0:T(8,128)(2,1)}), bf16[4,384,768]{2,1,0:T(8,128)(2,1)}, u32[]{:S(2)}, u32[]{:S(2)}) async-start(bf16[4,384,768]{2,1,0:T(8,128)(2,1)} %get-tuple-element.91), calls=%async_computation.3 | async-start | bytes 4718592 | tf_op jit(solution)/shard_map/all_to_all | solution.py:421
  147.6 41.3 %copy-start.18 = (f32[4,24,1536]{2,1,0:T(8,128)S(1)}, f32[4,24,1536]{2,1,0:T(8,128)}, u32[]{:S(2)}) copy-start(f32[4,24,1536]{2,1,0:T(8,128)} %copy-done.16) | copy-start | bytes 1769476
  147.6 15.9 %collective-permute-start.7 = (bf16[4,4,24,768]{3,2,1,0:T(8,128)(2,1)}, bf16[4,4,24,768]{3,2,1,0:T(8,128)(2,1)S(1)}, u32[]{:S(2)}, u32[]{:S(2)}) collective-permute-start(bf16[4,4,24,768]{3,2,1,0:T(8,128)(2,1)} %copy-done.72), channel_id=1, source_target_pairs={{0,4},{4,0},{8,12},{12,8},{16,20},{20,16},{24,28},{28,24},{1,5},{5... | collective-permute-start | bytes 1769480 | tf_op jit(solution)/shard_map/ppermute | solution.py:417
  147.8 22.0 %collective-permute-start.11 = (bf16[4,24,1536]{2,1,0:T(8,128)(2,1)}, bf16[4,24,1536]{2,1,0:T(8,128)(2,1)}, u32[]{:S(2)}, u32[]{:S(2)}) collective-permute-start(bf16[4,24,1536]{2,1,0:T(8,128)(2,1)} %copy-done.75), channel_id=1, source_target_pairs={{0,8},{4,12},{8,0},{12,4},{16,24},{20,28},{24,16},{28,20},{1,9},{5... | collective-permute-start | bytes 884744 | tf_op jit(solution)/shard_map/ppermute | solution.py:417
  149.3 23.8 %collective-permute-start.12 = (bf16[4,24,1536]{2,1,0:T(8,128)(2,1)}, bf16[4,24,1536]{2,1,0:T(8,128)(2,1)}, u32[]{:S(2)}, u32[]{:S(2)}) collective-permute-start(bf16[4,24,1536]{2,1,0:T(8,128)(2,1)} %copy-done.74), channel_id=1, source_target_pairs={{0,16},{4,20},{8,24},{12,28},{16,0},{20,4},{24,8},{28,12},{1,17},{... | collective-permute-start | bytes 884744 | tf_op jit(solution)/shard_map/ppermute | solution.py:417
  150.9 22.2 %collective-permute-start.13 = (bf16[4,24,1536]{2,1,0:T(8,128)(2,1)}, bf16[4,24,1536]{2,1,0:T(8,128)(2,1)}, u32[]{:S(2)}, u32[]{:S(2)}) collective-permute-start(bf16[4,24,1536]{2,1,0:T(8,128)(2,1)} %copy-done.73), channel_id=1, source_target_pairs={{0,24},{4,28},{8,16},{12,20},{16,8},{20,12},{24,0},{28,4},{1,25},{... | collective-permute-start | bytes 884744 | tf_op jit(solution)/shard_map/ppermute | solution.py:417
  166.8 8.5 %collective-permute-start.8 = (bf16[4,24,768]{2,1,0:T(8,128)(2,1)}, bf16[4,24,768]{2,1,0:T(8,128)(2,1)S(1)}, u32[]{:S(2)}, u32[]{:S(2)}) collective-permute-start(bf16[4,24,768]{2,1,0:T(8,128)(2,1)} %get-tuple-element.97), channel_id=1, source_target_pairs={{0,8},{4,12},{8,0},{12,4},{16,24},{20,28},{24,16},{28,20},{1,9},{5... | collective-permute-start | bytes 442376 | tf_op jit(solution)/shard_map/ppermute | solution.py:417
  168.2 20.6 %collective-permute-start.9 = (bf16[4,24,768]{2,1,0:T(8,128)(2,1)}, bf16[4,24,768]{2,1,0:T(8,128)(2,1)S(1)}, u32[]{:S(2)}, u32[]{:S(2)}) collective-permute-start(bf16[4,24,768]{2,1,0:T(8,128)(2,1)} %get-tuple-element.98), channel_id=1, source_target_pairs={{0,16},{4,20},{8,24},{12,28},{16,0},{20,4},{24,8},{28,12},{1,17},{... | collective-permute-start | bytes 442376 | tf_op jit(solution)/shard_map/ppermute | solution.py:417
  169.7 19.1 %collective-permute-start.10 = (bf16[4,24,768]{2,1,0:T(8,128)(2,1)}, bf16[4,24,768]{2,1,0:T(8,128)(2,1)S(1)}, u32[]{:S(2)}, u32[]{:S(2)}) collective-permute-start(bf16[4,24,768]{2,1,0:T(8,128)(2,1)} %get-tuple-element.99), channel_id=1, source_target_pairs={{0,24},{4,28},{8,16},{12,20},{16,8},{20,12},{24,0},{28,4},{1,25},{... | collective-permute-start | bytes 442376 | tf_op jit(solution)/shard_map/ppermute | solution.py:417
  192.7 13.5 %all-to-all-start.4 = ((bf16[4,4,24,768]{3,2,1,0:T(8,128)(2,1)}), bf16[4,4,24,768]{3,2,1,0:T(8,128)(2,1)S(1)}, u32[]{:S(2)}, u32[]{:S(2)}) async-start(bf16[4,4,24,768]{3,2,1,0:T(8,128)(2,1)} %get-tuple-element.103), calls=%async_computation.4 | async-start | bytes 1179648 | tf_op jit(solution)/shard_map/all_to_all | solution.py:421
  199.9 15.1 %collective-permute-start.23 = (f32[72,128]{1,0:T(8,128)S(1)}, f32[72,128]{1,0:T(8,128)S(1)}, u32[]{:S(2)}, u32[]{:S(2)}) collective-permute-start(f32[72,128]{1,0:T(8,128)S(1)} %bitcast.80), channel_id=1, source_target_pairs={{0,3},{1,2},{2,1},{3,0},{4,7},{5,6},{6,5},{7,4},{8,11},{9,10},{10,... | collective-permute-start | bytes 110600 | tf_op jit(solution)/shard_map/ppermute | solution.py:417
  201.7 13.4 %collective-permute-start.22 = (f32[72,128]{1,0:T(8,128)S(1)}, f32[72,128]{1,0:T(8,128)}, u32[]{:S(2)}, u32[]{:S(2)}) collective-permute-start(f32[72,128]{1,0:T(8,128)S(1)} %bitcast.81), channel_id=1, source_target_pairs={{0,2},{1,3},{2,0},{3,1},{4,6},{5,7},{6,4},{7,5},{8,10},{9,11},{10,... | collective-permute-start | bytes 110600 | tf_op jit(solution)/shard_map/ppermute | solution.py:417
  210.6 18.5 %collective-permute-start.19 = (bf16[4,24,3072]{2,1,0:T(8,128)(2,1)}, bf16[4,24,3072]{2,1,0:T(8,128)(2,1)}, u32[]{:S(2)}, u32[]{:S(2)}) collective-permute-start(bf16[4,24,3072]{2,1,0:T(8,128)(2,1)} %get-tuple-element.105.refs_1_), channel_id=1, source_target_pairs={{0,24},{4,28},{8,16},{12,20},{16,8},{20,12},{24,0},{28,4},{1,25},{... | collective-permute-start | bytes 1769480 | tf_op jit(solution)/shard_map/ppermute | solution.py:417
  212.6 52.1 %collective-permute-start.17 = (bf16[4,24,3072]{2,1,0:T(8,128)(2,1)}, bf16[4,24,3072]{2,1,0:T(8,128)(2,1)S(1)}, u32[]{:S(2)}, u32[]{:S(2)}) collective-permute-start(bf16[4,24,3072]{2,1,0:T(8,128)(2,1)} %get-tuple-element.105.refs_1_), channel_id=1, source_target_pairs={{0,16},{4,20},{8,24},{12,28},{16,0},{20,4},{24,8},{28,12},{1,17},{... | collective-permute-start | bytes 1769480 | tf_op jit(solution)/shard_map/ppermute | solution.py:417
  214.8 51.9 %collective-permute-start.15 = (bf16[4,24,3072]{2,1,0:T(8,128)(2,1)}, bf16[4,24,3072]{2,1,0:T(8,128)(2,1)S(1)}, u32[]{:S(2)}, u32[]{:S(2)}) collective-permute-start(bf16[4,24,3072]{2,1,0:T(8,128)(2,1)} %get-tuple-element.105.refs_1_), channel_id=1, source_target_pairs={{0,8},{4,12},{8,0},{12,4},{16,24},{20,28},{24,16},{28,20},{1,9},{5... | collective-permute-start | bytes 1769480 | tf_op jit(solution)/shard_map/ppermute | solution.py:417
  215.0 56.2 %copy-start.80 = (f32[72,128]{1,0:T(8,128)}, f32[72,128]{1,0:T(8,128)S(1)}, u32[]{:S(2)}) copy-start(f32[72,128]{1,0:T(8,128)S(1)} %collective-permute-done.23) | copy-start | bytes 110596
  215.0 56.2 %collective-permute-start.21 = (f32[72,128]{1,0:T(8,128)S(1)}, f32[72,128]{1,0:T(8,128)}, u32[]{:S(2)}, u32[]{:S(2)}) collective-permute-start(f32[72,128]{1,0:T(8,128)S(1)} %bitcast.82), channel_id=1, source_target_pairs={{0,1},{1,0},{2,3},{3,2},{4,5},{5,4},{6,7},{7,6},{8,9},{9,8},{10,11... | collective-permute-start | bytes 110600 | tf_op jit(solution)/shard_map/ppermute | solution.py:417
  215.1 79.1 %collective-permute-start.14 = (bf16[4,24,3072]{2,1,0:T(8,128)(2,1)}, bf16[4,24,3072]{2,1,0:T(8,128)(2,1)S(1)}, u32[]{:S(2)}, u32[]{:S(2)}) collective-permute-start(bf16[4,24,3072]{2,1,0:T(8,128)(2,1)} %get-tuple-element.105.refs_1_), channel_id=1, source_target_pairs={{0,4},{4,0},{8,12},{12,8},{16,20},{20,16},{24,28},{28,24},{1,5},{5... | collective-permute-start | bytes 1769480 | tf_op jit(solution)/shard_map/ppermute | solution.py:417
  229.1 65.1 %collective-permute-start.20 = (bf16[4,24,3072]{2,1,0:T(8,128)(2,1)}, bf16[4,24,3072]{2,1,0:T(8,128)(2,1)}, u32[]{:S(2)}, u32[]{:S(2)}) collective-permute-start(bf16[4,24,3072]{2,1,0:T(8,128)(2,1)} %collective-permute-done.19.refs_8_.refs_7_), channel_id=1, source_target_pairs={{0,4},{4,0},{8,12},{12,8},{16,20},{20,16},{24,28},{28,24},{1,5},{5... | collective-permute-start | bytes 1769480 | tf_op jit(solution)/shard_map/ppermute | solution.py:417
  264.7 31.8 %copy-start.21 = (bf16[4,24,3072]{2,1,0:T(8,128)(2,1)}, bf16[4,24,3072]{2,1,0:T(8,128)(2,1)S(1)}, u32[]{:S(2)}) copy-start(bf16[4,24,3072]{2,1,0:T(8,128)(2,1)S(1)} %collective-permute-done.17.refs_6_.refs_5_) | copy-start | bytes 1769476
  264.7 29.5 %collective-permute-start.18 = (bf16[4,24,3072]{2,1,0:T(8,128)(2,1)S(1)}, bf16[4,24,3072]{2,1,0:T(8,128)(2,1)S(1)}, u32[]{:S(2)}, u32[]{:S(2)}) collective-permute-start(bf16[4,24,3072]{2,1,0:T(8,128)(2,1)S(1)} %collective-permute-done.17.refs_6_.refs_5_), channel_id=1, source_target_pairs={{0,4},{4,0},{8,12},{12,8},{16,20},{20,16},{24,28},{28,24},{1,5},{5... | collective-permute-start | bytes 1769480 | tf_op jit(solution)/shard_map/ppermute | solution.py:417
  266.6 29.9 %copy-start.23 = (bf16[4,24,3072]{2,1,0:T(8,128)(2,1)}, bf16[4,24,3072]{2,1,0:T(8,128)(2,1)S(1)}, u32[]{:S(2)}) copy-start(bf16[4,24,3072]{2,1,0:T(8,128)(2,1)S(1)} %collective-permute-done.15.refs_4_.refs_3_) | copy-start | bytes 1769476
  266.6 27.6 %collective-permute-start.16 = (bf16[4,24,3072]{2,1,0:T(8,128)(2,1)S(1)}, bf16[4,24,3072]{2,1,0:T(8,128)(2,1)S(1)}, u32[]{:S(2)}, u32[]{:S(2)}) collective-permute-start(bf16[4,24,3072]{2,1,0:T(8,128)(2,1)S(1)} %collective-permute-done.15.refs_4_.refs_3_), channel_id=1, source_target_pairs={{0,4},{4,0},{8,12},{12,8},{16,20},{20,16},{24,28},{28,24},{1,5},{5... | collective-permute-start | bytes 1769480 | tf_op jit(solution)/shard_map/ppermute | solution.py:417
  266.8 27.4 %all-to-all-start.5 = ((bf16[4,24,2112]{2,1,0:T(8,128)(2,1)}), bf16[4,24,2112]{2,1,0:T(8,128)(2,1)}, u32[]{:S(2)}, u32[]{:S(2)}) async-start(bf16[4,24,2112]{2,1,0:T(8,128)(2,1)} %copy-done.56), calls=%async_computation.5 | async-start | bytes 835584 | tf_op jit(solution)/shard_map/all_to_all | solution.py:421
  272.0 21.6 %collective-permute-start.24 = (f32[72,128]{1,0:T(8,128)S(1)}, f32[72,128]{1,0:T(8,128)S(1)}, u32[]{:S(2)}, u32[]{:S(2)}) collective-permute-start(f32[72,128]{1,0:T(8,128)S(1)} %add_add_fusion.1), channel_id=1, source_target_pairs={{0,4},{4,0},{8,12},{12,8},{16,20},{20,16},{24,28},{28,24},{1,5},{5... | collective-permute-start | bytes 110600 | tf_op jit(solution)/shard_map/ppermute | solution.py:417
  296.5 69.1 %collective-permute-start.31 = (bf16[24,9216]{1,0:T(8,128)(2,1)}, bf16[24,9216]{1,0:T(8,128)(2,1)}, u32[]{:S(2)}, u32[]{:S(2)}) collective-permute-start(bf16[24,9216]{1,0:T(8,128)(2,1)} %grads.1.refs_9_), channel_id=1, source_target_pairs={{0,4},{4,0},{8,12},{12,8},{16,20},{20,16},{24,28},{28,24},{1,5},{5... | collective-permute-start | bytes 1327112 | tf_op jit(solution)/shard_map/ppermute | solution.py:417
  298.4 44.9 %collective-permute-start.27 = (bf16[24,9216]{1,0:T(8,128)(2,1)}, bf16[24,9216]{1,0:T(8,128)(2,1)S(1)}, u32[]{:S(2)}, u32[]{:S(2)}) collective-permute-start(bf16[24,9216]{1,0:T(8,128)(2,1)} %grads.1.refs_9_), channel_id=1, source_target_pairs={{0,24},{4,28},{8,16},{12,20},{16,8},{20,12},{24,0},{28,4},{1,25},{... | collective-permute-start | bytes 1327112 | tf_op jit(solution)/shard_map/ppermute | solution.py:417
  300.5 42.7 %collective-permute-start.26 = (bf16[24,9216]{1,0:T(8,128)(2,1)}, bf16[24,9216]{1,0:T(8,128)(2,1)S(1)}, u32[]{:S(2)}, u32[]{:S(2)}) collective-permute-start(bf16[24,9216]{1,0:T(8,128)(2,1)} %grads.1.refs_9_), channel_id=1, source_target_pairs={{0,16},{4,20},{8,24},{12,28},{16,0},{20,4},{24,8},{28,12},{1,17},{... | collective-permute-start | bytes 1327112 | tf_op jit(solution)/shard_map/ppermute | solution.py:417
  300.7 42.6 %collective-permute-start.25 = (bf16[24,9216]{1,0:T(8,128)(2,1)}, bf16[24,9216]{1,0:T(8,128)(2,1)S(1)}, u32[]{:S(2)}, u32[]{:S(2)}) collective-permute-start(bf16[24,9216]{1,0:T(8,128)(2,1)} %grads.1.refs_9_), channel_id=1, source_target_pairs={{0,8},{4,12},{8,0},{12,4},{16,24},{20,28},{24,16},{28,20},{1,9},{5... | collective-permute-start | bytes 1327112 | tf_op jit(solution)/shard_map/ppermute | solution.py:417
  309.1 34.9 %copy-start.59 = (f32[72,128]{1,0:T(8,128)S(1)}, f32[72,128]{1,0:T(8,128)}, u32[]{:S(2)}) copy-start(f32[72,128]{1,0:T(8,128)} %add.245.refs_2_) | copy-start | bytes 110596
  355.7 13.8 %collective-permute-start.30 = (f32[72,128]{1,0:T(8,128)}, f32[72,128]{1,0:T(8,128)}, u32[]{:S(2)}, u32[]{:S(2)}) collective-permute-start(f32[72,128]{1,0:T(8,128)} %get-tuple-element.110), channel_id=1, source_target_pairs={{0,24},{4,28},{8,16},{12,20},{16,8},{20,12},{24,0},{28,4},{1,25},{... | collective-permute-start | bytes 110600 | tf_op jit(solution)/shard_map/ppermute | solution.py:417
  357.9 12.0 %collective-permute-start.29 = (f32[72,128]{1,0:T(8,128)}, f32[72,128]{1,0:T(8,128)}, u32[]{:S(2)}, u32[]{:S(2)}) collective-permute-start(f32[72,128]{1,0:T(8,128)} %get-tuple-element.110), channel_id=1, source_target_pairs={{0,16},{4,20},{8,24},{12,28},{16,0},{20,4},{24,8},{28,12},{1,17},{... | collective-permute-start | bytes 110600 | tf_op jit(solution)/shard_map/ppermute | solution.py:417
  357.9 12.0 %collective-permute-start.28 = (f32[72,128]{1,0:T(8,128)}, f32[72,128]{1,0:T(8,128)}, u32[]{:S(2)}, u32[]{:S(2)}) collective-permute-start(f32[72,128]{1,0:T(8,128)} %get-tuple-element.110), channel_id=1, source_target_pairs={{0,8},{4,12},{8,0},{12,4},{16,24},{20,28},{24,16},{28,20},{1,9},{5... | collective-permute-start | bytes 110600 | tf_op jit(solution)/shard_map/ppermute | solution.py:417
  360.2 22.5 %copy-start.65 = (f32[192]{0:T(256)S(1)}, f32[192]{0:T(256)}, u32[]{:S(2)}) copy-start(f32[192]{0:T(256)} %param.25) | copy-start | bytes 2308
  360.2 23.8 %copy-start.67 = (f32[192]{0:T(256)S(1)}, f32[192]{0:T(256)}, u32[]{:S(2)}) copy-start(f32[192]{0:T(256)} %param.24) | copy-start | bytes 2308
  360.2 59.0 %all-to-all-start.6 = ((bf16[4,8,24,3072]{3,2,1,0:T(8,128)(2,1)}), bf16[4,8,24,3072]{3,2,1,0:T(8,128)(2,1)}, u32[]{:S(2)}, u32[]{:S(2)}) async-start(bf16[4,8,24,3072]{3,2,1,0:T(8,128)(2,1)} %get-tuple-element.115), calls=%async_computation.6 | async-start | bytes 9437184 | tf_op jit(solution)/shard_map/all_to_all | solution.py:421
  365.3 36.0 %collective-permute-start.34 = (bf16[24,9216]{1,0:T(8,128)(2,1)}, bf16[24,9216]{1,0:T(8,128)(2,1)}, u32[]{:S(2)}, u32[]{:S(2)}) collective-permute-start(bf16[24,9216]{1,0:T(8,128)(2,1)} %copy-done.34), channel_id=1, source_target_pairs={{0,4},{4,0},{8,12},{12,8},{16,20},{20,16},{24,28},{28,24},{1,5},{5... | collective-permute-start | bytes 1327112 | tf_op jit(solution)/shard_map/ppermute | solution.py:417
  365.7 33.5 %collective-permute-start.33 = (bf16[24,9216]{1,0:T(8,128)(2,1)}, bf16[24,9216]{1,0:T(8,128)(2,1)}, u32[]{:S(2)}, u32[]{:S(2)}) collective-permute-start(bf16[24,9216]{1,0:T(8,128)(2,1)} %copy-done.35), channel_id=1, source_target_pairs={{0,4},{4,0},{8,12},{12,8},{16,20},{20,16},{24,28},{28,24},{1,5},{5... | collective-permute-start | bytes 1327112 | tf_op jit(solution)/shard_map/ppermute | solution.py:417
  369.5 27.6 %collective-permute-start.32 = (bf16[24,9216]{1,0:T(8,128)(2,1)}, bf16[24,9216]{1,0:T(8,128)(2,1)}, u32[]{:S(2)}, u32[]{:S(2)}) collective-permute-start(bf16[24,9216]{1,0:T(8,128)(2,1)} %copy-done.36), channel_id=1, source_target_pairs={{0,4},{4,0},{8,12},{12,8},{16,20},{20,16},{24,28},{28,24},{1,5},{5... | collective-permute-start | bytes 1327112 | tf_op jit(solution)/shard_map/ppermute | solution.py:417
  381.1 23.1 %copy-start.12 = (f32[192,3072]{1,0:T(8,128)S(1)}, f32[192,3072]{1,0:T(8,128)}, u32[]{:S(2)}) copy-start(f32[192,3072]{1,0:T(8,128)} %refs_3_.1) | copy-start | bytes 7077892
  381.1 23.1 %copy-start.31 = (f32[192,2304]{1,0:T(8,128)S(1)}, f32[192,2304]{1,0:T(8,128)}, u32[]{:S(2)}) copy-start(f32[192,2304]{1,0:T(8,128)} %refs_0_.1) | copy-start | bytes 5308420
  (63 other events, 195.6 us)

commit v3 on v2

--- a/solution.py
+++ b/solution.py
@@ -465,20 +465,21 @@
 
 def pack_kernel(where_ref, residual_ref, grad_ref, *refs):
     half = jnp.bfloat16
-    vectors, out_ref = refs[:7], refs[7]
+    vectors_ref, out_ref = refs
     place = where_ref[2]
     rows, width = residual_ref.shape
-
-    def share(ref):
-        size = ref.shape[1]
+    part = width // SHARDS
+
+    def share(start, size):
         lane = lax.broadcasted_iota(jnp.int32, (1, SHARDS * size), 1)
         mine = jnp.logical_and(lane >= place * size, lane < (place + 1) * size)
-        return jnp.where(mine, jnp.concatenate([ref[...]] * SHARDS, axis=1), 0.0)
-
-    heads = share(vectors[6])
+        piece = vectors_ref[:, start : start + size]
+        return jnp.where(mine, jnp.concatenate([piece] * SHARDS, axis=1), 0.0)
+
+    heads = share(6 * part, 3 * part)
     out_ref[:rows] = residual_ref[...]
     out_ref[rows : 2 * rows] = grad_ref[...].astype(half)
-    small = [share(v) for v in vectors[:6]]
+    small = [share(i * part, part) for i in range(6)]
     small += [heads[:, t * width : (t + 1) * width] for t in range(3)]
     small.append(jnp.zeros((16 - len(small), width), jnp.float32))
     out_ref[2 * rows :] = jnp.concatenate(small, axis=0).astype(half)
@@ -757,7 +758,12 @@
                 write(f, owner, jnp.concatenate(pieces, axis=1))
 
 
-def grads_kernel(where_ref, strips_ref, output_ref, out_ref):
+def copy_kernel(where_ref, x_ref, out_ref):
+    out_ref[...] = x_ref[...]
+
+
+def grads_kernel(where_ref, strips_ref, output_ref, sums_ref, out_ref, sums_out):
+    sums_out[...] = sums_ref[...]
     size = output_ref.shape[1]
     part = size // SHARDS
     pieces = [
@@ -974,7 +980,7 @@
             out_specs=blocks + blocks,
         ),
         out_shape=shapes + shapes,
-        compiler_params=pltpu.CompilerParams(vmem_limit_bytes=32 * 1024 * 1024),
+        compiler_params=pltpu.CompilerParams(vmem_limit_bytes=60 * 1024 * 1024),
         cost_estimate=pl.CostEstimate(
             flops=0, bytes_accessed=int(100 * 3.6e6), transcendentals=0
         ),
@@ -1009,7 +1015,7 @@
             out_specs=blocks,
         ),
         out_shape=[jax.ShapeDtypeStruct(w.shape, w.dtype) for w in weights],
-        compiler_params=pltpu.CompilerParams(vmem_limit_bytes=32 * 1024 * 1024),
+        compiler_params=pltpu.CompilerParams(vmem_limit_bytes=60 * 1024 * 1024),
         name="weights",
     )(ctx_place.reshape(1), *[ortho] * 4, *weights)
 
@@ -1053,18 +1059,20 @@
     [packed] = call(
         pack_kernel,
         [((2 * rows + 16, width), half)],
-        [residual_in[0], cotangent[0]]
-        + [
-            v[None]
-            for v in (
-                gain_first,
-                shift_first,
-                gain_second,
-                shift_second,
-                output_bias,
-                down_bias,
-                heads_bias,
-            )
+        [
+            residual_in[0],
+            cotangent[0],
+            jnp.concatenate(
+                [
+                    gain_first,
+                    shift_first,
+                    gain_second,
+                    shift_second,
+                    output_bias,
+                    down_bias,
+                    heads_bias,
+                ]
+            )[None],
         ],
         where,
         "pack",
@@ -1089,7 +1097,7 @@
         where,
         "mlp_split",
         0.1,
-        earlier=[heads_block],
+        earlier=[packs[3]],
     )
     mlp_pieces = [mlp_split[0]] + [swap(mlp_split[k], "fsdp", k) for k in range(1, SHARDS)]
     output_block = output_weight.astype(half)
@@ -1220,11 +1228,18 @@
         "owned",
         0.1,
     )
-    pieces = gather_y(gather_z(owned))
-    [grads] = call(
+    along = [owned, swap(owned, "ctx", Y_PLACES), swap(owned, "ctx", 2 * Y_PLACES)]
+    first, second = swap(owned, "ctx", 1), swap(along[1], "ctx", 1)
+    [again] = call(
+        copy_kernel, [(owned.shape, half)], [owned], where, "again", 0.1, earlier=[second, along[2]]
+    )
+    along.append(swap(again, "ctx", 3 * Y_PLACES))
+    third, fourth = swap(along[2], "ctx", 1), swap(along[3], "ctx", 1)
+    pieces = [owned, first, along[1], second, along[2], third, along[3], fourth]
+    grads, sums = call(
         grads_kernel,
-        [((strip, 4 * width + 2 * hidden), half)],
-        [exchange(strips), output_strip],
+        [((strip, 4 * width + 2 * hidden), half), (sums.shape, single)],
+        [exchange(strips), output_strip, sums],
         where,
         "grads",
         0.1,

time: 437 us -> 423 us (0.968)
  other arithmetic: 25.7 us -> 18.4 us
  waiting for transfers between devices: 156 us -> 149 us
  local copies, waits for them, and re-layouts: 59.1 us -> 52.9 us
  Pallas kernels: 106 us -> 112 us
    ppermute x35, waiting for transfers between devices: 138 us -> 121 us  [swap(): return lax.ppermute(x, axis, [(i, i ^ offset) for i in range(count)])]
    all_to_all x7, waiting for transfers between devices: 17.5 us -> 28.2 us  [exchange(): return lax.all_to_all(x, axis, 0, 0)]
    unnamed x184 -> x156, local copies, waits for them, and re-layouts: 50.1 us -> 41.8 us
    sub x8, other arithmetic: 10.2 us -> 5.11 us  [local_fast(): vector_values[which]]
    pallas_call x1, Pallas kernels: 5.86 us -> 10.8 us  [write_moments(): pl.pallas_call(moment_kernel, grid_spec=pltpu.PrefetchScalarGridSpec(num_...]
    pallas_call x14 -> x15, Pallas kernels: 92 us -> 92.3 us  [call(): pl.pallas_call(body, in_specs=[pl.BlockSpec(memory_space=pltpu.SMEM)] + [...]
  transfers between devices with their start and end apart: 42 -> 42, of which waited for: 14 -> 16; matrix products, arithmetic and copies ran while one was open for 10% -> 11% of each run, Pallas kernels for 19% -> 21%
where the time goes in v3:
time: 423 us; the launch traced here: 417 us
  waiting for transfers between devices  149 us (35%)
  Pallas kernels  112 us (26%)
  starting transfers between devices  77.8 us (18%)
  local copies, waits for them, and re-layouts  52.9 us (13%)
  other arithmetic  18.4 us (4%)
  between operations  6.52 us (2%)
    ppermute x35, waiting for transfers between devices, swap(): return lax.ppermute(x, axis, [(i, i ^ offset) for i in range(count)])  121 us
    pallas_call x15, Pallas kernels, call(): pl.pallas_call(body, in_specs=[pl.BlockSpec(memory_space=pltpu.SMEM)] + [...  92.3 us
    ppermute x35, starting transfers between devices, swap(): return lax.ppermute(x, axis, [(i, i ^ offset) for i in range(count)])  43.1 us
    unnamed x156, local copies, waits for them, and re-layouts  41.8 us
    all_to_all x7, starting transfers between devices, exchange(): return lax.all_to_all(x, axis, 0, 0)  34.8 us
    all_to_all x7, waiting for transfers between devices, exchange(): return lax.all_to_all(x, axis, 0, 0)  28.2 us
    pallas_call x1, Pallas kernels, write_moments(): pl.pallas_call(moment_kernel, grid_spec=pltpu.PrefetchScalarGridSpec(num_...  10.8 us
    pallas_call x1, Pallas kernels, write_weights(): pl.pallas_call(weight_kernel, grid_spec=pltpu.PrefetchScalarGridSpec(num_...  9.25 us
  transfers between devices with their start and end apart: 42, of which 16 were waited for; matrix products, arithmetic and copies ran while one was open for 11% of the time, Pallas kernels for 21%

profile of v3, /device:TPU:0, one launch (start us, length us, event | category | flops | bytes accessed | tf_op | source)
XLA Modules:
  0.0 417.1 jit_solution(13053596656218602400)
XLA Ops:
  4.2 3.0 collective-permute-start.1
  7.2 1.5 copy-done
  8.7 1.7 heads_split.1
  10.4 4.4 %all-to-all-start = ((bf16[4,192,576]{2,1,0:T(8,128)(2,1)}), bf16[4,192,576]{2,1,0:T(8,128)(2,1)}, u32[]{:S(2)}, u32[]{:S(2)}) async-start(bf16[4,192,576]{2,1,0:T(8,128)(2,1)} %heads_split.1), calls=%async_computation | async-start | bytes 1966080 | tf_op jit(solution)/shard_map/all_to_all | solution.py:421
  19.3 9.3 %all-to-all-done = bf16[4,192,576]{2,1,0:T(8,128)(2,1)} async-done(((bf16[4,192,576]{2,1,0:T(8,128)(2,1)}), bf16[4,192,576]{2,1,0:T(8,128)(2,1)}, u32[]{:S(2)}, u32[]{:S(2)}) %all-to-all-start) | async-done | bytes 884768 | tf_op jit(solution)/shard_map/all_to_all | solution.py:421
  28.6 4.1 pre.1
  34.4 6.5 %all-to-all-start.1 = ((bf16[8,448,128]{2,1,0:T(8,128)(2,1)}), bf16[8,448,128]{2,1,0:T(8,128)(2,1)S(1)}, u32[]{:S(2)}, u32[]{:S(2)}) async-start(bf16[8,448,128]{2,1,0:T(8,128)(2,1)} %get-tuple-element.79), calls=%async_computation.1 | async-start | bytes 1835008 | tf_op jit(solution)/shard_map/all_to_all | solution.py:421
  43.1 3.9 mlp_split.1
  48.7 1.5 collective-permute-start.5
  52.2 1.9 fusion.refs_3_
  54.1 13.4 %collective-permute-done.3.refs_5_.refs_6_ = bf16[240,1536]{1,0:T(8,128)(2,1)S(1)} collective-permute-done((bf16[240,1536]{1,0:T(8,128)(2,1)}, bf16[240,1536]{1,0:T(8,128)(2,1)S(1)}, u32[]{:S(2)}, u32[]{:S(2)}) %collective-permute-start.3) | collective-permute-done | bytes 737312 | tf_op jit(solution)/shard_map/ppermute | solution.py:417
  67.5 1.3 copy-done.7
  69.7 10.9 %attention.1 = bf16[8,448,128]{2,1,0:T(8,128)(2,1)} custom-call(s32[4]{0:T(128)S(1)} %pad_add_fusion.refs_0_, bf16[8,448,128]{2,1,0:T(8,128)(2,1)S(1)} %all-to-all-done.1.refs_1_, s32[1,1024]{1,0:T(1,128)S(1)} %fusion.12.refs_2_, s32[1024,1]{1,0:T(8,128)S(1)} %copy-done.7, s32[512,1]{1,0:T(8,128)S(1)} %copy-done.25, ...), custom_call_target="tpu_custom_call" | custom-call | bytes 360000 | tf_op jit(solution)/shard_map/attention/pallas_call | solution.py:446
  80.6 6.4 %all-to-all-start.2 = ((bf16[8,448,128]{2,1,0:T(8,128)(2,1)}), bf16[8,448,128]{2,1,0:T(8,128)(2,1)}, u32[]{:S(2)}, u32[]{:S(2)}) async-start(bf16[8,448,128]{2,1,0:T(8,128)(2,1)} %attention.1), calls=%async_computation.2 | async-start | bytes 1835008 | tf_op jit(solution)/shard_map/all_to_all | solution.py:421
  87.1 7.9 %mlp.1 = (bf16[4,4,24,1536]{3,2,1,0:T(8,128)(2,1)}, f32[4,4,24,1536]{3,2,1,0:T(8,128)}, f32[512,768]{1,0:T(8,128)}, f32[1,768]{1,0:T(1,128)S(1)}, f32[512,768]{1,0:T(8,128)}) custom-call(s32[4]{0:T(128)S(1)} %pad_add_fusion.refs_0_, bf16[512,768]{1,0:T(8,128)(2,1)S(1)} %copy-done.28, bf16[512,768]{1,0:T(8,128)(2,1)} %get-tuple-element.82.refs_2_.refs_3_, ...), custom_call_target="tpu_custom_call" | custom-call | bytes 360000 | tf_op jit(solution)/shard_map/mlp/pallas_call | solution.py:446
  95.0 2.0 collective-permute-start.6
  97.1 26.3 %collective-permute-done.6.refs_2_ = bf16[4,4,24,1536]{3,2,1,0:T(8,128)(2,1)S(1)} collective-permute-done((bf16[4,4,24,1536]{3,2,1,0:T(8,128)(2,1)}, bf16[4,4,24,1536]{3,2,1,0:T(8,128)(2,1)S(1)}, u32[]{:S(2)}, u32[]{:S(2)}) %collective-permute-start.6) | collective-permute-done | bytes 1179680 | tf_op jit(solution)/shard_map/ppermute | solution.py:417
  123.3 2.6 mlp_z.1
  130.6 6.7 %post.1 = (bf16[4,4,24,768]{3,2,1,0:T(8,128)(2,1)S(1)}, f32[4,4,24,768]{3,2,1,0:T(8,128)}, f32[1,576]{1,0:T(1,128)S(1)}, f32[384,768]{1,0:T(8,128)}, bf16[4,384,768]{2,1,0:T(8,128)(2,1)}) custom-call(s32[4]{0:T(128)S(1)} %pad_add_fusion.refs_0_, bf16[8,448,128]{2,1,0:T(8,128)(2,1)} %all-to-all-done.2.refs_1_, bf16[512,768]{1,0:T(8,128)(2,1)S(1)} %copy-done.27, ...), custom_call_target="tpu_custom_call" | custom-call | bytes 360000 | tf_op jit(solution)/shard_map/post/pallas_call | solution.py:446
  138.1 4.6 %all-to-all-start.3 = ((bf16[4,384,768]{2,1,0:T(8,128)(2,1)}), bf16[4,384,768]{2,1,0:T(8,128)(2,1)}, u32[]{:S(2)}, u32[]{:S(2)}) async-start(bf16[4,384,768]{2,1,0:T(8,128)(2,1)} %get-tuple-element.93), calls=%async_computation.3 | async-start | bytes 4718592 | tf_op jit(solution)/shard_map/all_to_all | solution.py:421
  143.0 1.5 collective-permute-start.11
  144.4 1.5 collective-permute-start.12
  145.9 1.4 collective-permute-start.13
  147.4 11.3 %collective-permute-done.7.refs_2_ = bf16[4,4,24,768]{3,2,1,0:T(8,128)(2,1)S(1)} collective-permute-done((bf16[4,4,24,768]{3,2,1,0:T(8,128)(2,1)}, bf16[4,4,24,768]{3,2,1,0:T(8,128)(2,1)S(1)}, u32[]{:S(2)}, u32[]{:S(2)}) %collective-permute-start.7) | collective-permute-done | bytes 589856 | tf_op jit(solution)/shard_map/ppermute | solution.py:417
  161.3 1.5 collective-permute-start.8
  162.8 1.5 collective-permute-start.9
  164.2 1.4 collective-permute-start.10
  165.7 2.4 collective-permute-done.12.refs_7_
  170.5 13.4 %collective-permute-done.9.refs_3_ = bf16[4,24,768]{2,1,0:T(8,128)(2,1)S(1)} collective-permute-done((bf16[4,24,768]{2,1,0:T(8,128)(2,1)S(1)}, bf16[4,24,768]{2,1,0:T(8,128)(2,1)S(1)}, u32[]{:S(2)}, u32[]{:S(2)}) %collective-permute-start.9) | collective-permute-done | bytes 147488 | tf_op jit(solution)/shard_map/ppermute | solution.py:417
  190.0 1.6 strip.1
  191.6 3.5 all-to-all-start.4
  197.1 7.4 %all-to-all-done.4.refs_1_ = bf16[4,4,24,768]{3,2,1,0:T(8,128)(2,1)S(1)} async-done(((bf16[4,4,24,768]{3,2,1,0:T(8,128)(2,1)}), bf16[4,4,24,768]{3,2,1,0:T(8,128)(2,1)S(1)}, u32[]{:S(2)}, u32[]{:S(2)}) %all-to-all-start.4) | async-done | bytes 589856 | tf_op jit(solution)/shard_map/all_to_all | solution.py:421
  204.5 2.6 owned.1
  207.9 2.1 collective-permute-start.15
  211.2 2.1 convert_reduce_fusion
  216.5 12.8 %collective-permute-done.15.refs_5_.refs_3_ = bf16[4,24,3072]{2,1,0:T(8,128)(2,1)S(1)} collective-permute-done((bf16[4,24,3072]{2,1,0:T(8,128)(2,1)}, bf16[4,24,3072]{2,1,0:T(8,128)(2,1)S(1)}, u32[]{:S(2)}, u32[]{:S(2)}) %collective-permute-start.15) | collective-permute-done | bytes 589856 | tf_op jit(solution)/shard_map/ppermute | solution.py:417
  229.3 1.7 collective-permute-start.16
  236.3 1.3 constant_dynamic-update-slice_fusion.2
  239.6 4.6 %collective-permute-done.17.refs_3_.refs_7_.refs_5_ = bf16[4,24,3072]{2,1,0:T(8,128)(2,1)S(1)} collective-permute-done((bf16[4,24,3072]{2,1,0:T(8,128)(2,1)}, bf16[4,24,3072]{2,1,0:T(8,128)(2,1)S(1)}, u32[]{:S(2)}, u32[]{:S(2)}) %collective-permute-start.17) | collective-permute-done | bytes 589856 | tf_op jit(solution)/shard_map/ppermute | solution.py:417
  245.3 2.1 collective-permute-start.19
  247.4 1.8 collective-permute-start.14
  249.5 11.4 %collective-permute-done.19.refs_9_.refs_7_ = bf16[4,24,3072]{2,1,0:T(8,128)(2,1)} collective-permute-done((bf16[4,24,3072]{2,1,0:T(8,128)(2,1)S(1)}, bf16[4,24,3072]{2,1,0:T(8,128)(2,1)}, u32[]{:S(2)}, u32[]{:S(2)}) %collective-permute-start.19) | collective-permute-done | bytes 589856 | tf_op jit(solution)/shard_map/ppermute | solution.py:417
  260.9 1.7 collective-permute-start.20
  263.2 4.3 %all-to-all-start.5 = ((bf16[4,24,2112]{2,1,0:T(8,128)(2,1)}), bf16[4,24,2112]{2,1,0:T(8,128)(2,1)}, u32[]{:S(2)}, u32[]{:S(2)}) async-start(bf16[4,24,2112]{2,1,0:T(8,128)(2,1)} %copy-done.33), calls=%async_computation.5 | async-start | bytes 835584 | tf_op jit(solution)/shard_map/all_to_all | solution.py:421
  268.1 2.5 add_bitcast_fusion
  271.4 3.9 all-to-all-done.5.refs_1_
  276.6 9.8 %collective-permute-done.20.refs_10_.refs_8_ = bf16[4,24,3072]{2,1,0:T(8,128)(2,1)} collective-permute-done((bf16[4,24,3072]{2,1,0:T(8,128)(2,1)}, bf16[4,24,3072]{2,1,0:T(8,128)(2,1)}, u32[]{:S(2)}, u32[]{:S(2)}) %collective-permute-start.20) | collective-permute-done | bytes 589856 | tf_op jit(solution)/shard_map/ppermute | solution.py:417
  287.2 1.9 grads.1
  289.2 1.7 collective-permute-start.31
  290.9 1.8 collective-permute-start.27
  292.7 2.6 collective-permute-start.25
  295.6 1.8 bitcast_dynamic-update-slice_fusion.7
  297.4 34.0 %newton.1.refs_1_ = bf16[768,3072]{1,0:T(8,128)(2,1)} custom-call(s32[4]{0:T(128)S(1)} %pad_add_fusion.refs_0_, bf16[4,24,3072]{2,1,0:T(8,128)(2,1)} %get-tuple-element.107.refs_1_, bf16[4,24,3072]{2,1,0:T(8,128)(2,1)S(1)} %collective-permute-done.14.refs_4_.refs_2_, bf16[4,24,3072]{2,1,0:T(8,128)(2,1)S(1)} %collective-permute-done.15.refs_5_.refs_3_, ...), custom_call_target="tpu_custom_call" | custom-call | bytes 129600000 | tf_op jit(solution)/shard_map/newton/pallas_call | solution.py:446
  331.5 12.0 %last_newton.1 = (bf16[4,8,24,3072]{3,2,1,0:T(8,128)(2,1)}, f32[72,128]{1,0:T(8,128)S(1)}) custom-call(s32[4]{0:T(128)S(1)} %pad_add_fusion.refs_0_, bf16[768,3072]{1,0:T(8,128)(2,1)} %newton.1.refs_1_, f32[72,128]{1,0:T(8,128)S(1)} %add.245.refs_2_, bf16[24,9216]{1,0:T(8,128)(2,1)S(1)} %collective-permute-done.25.refs_3_, ...), custom_call_target="tpu_custom_call" | custom-call | bytes 32400000 | tf_op jit(solution)/shard_map/last_newton/pallas_call | solution.py:446
  343.5 1.9 collective-permute-start.30
  345.4 2.6 collective-permute-start.28
  348.1 5.1 %all-to-all-start.6 = ((bf16[4,8,24,3072]{3,2,1,0:T(8,128)(2,1)}), bf16[4,8,24,3072]{3,2,1,0:T(8,128)(2,1)}, u32[]{:S(2)}, u32[]{:S(2)}) async-start(bf16[4,8,24,3072]{3,2,1,0:T(8,128)(2,1)} %get-tuple-element.119), calls=%async_computation.6 | async-start | bytes 9437184 | tf_op jit(solution)/shard_map/all_to_all | solution.py:421
  353.2 1.8 collective-permute-start.34
  355.3 1.8 bitcast_dynamic-update-slice_fusion.6
  358.0 1.7 collective-permute-start.32
  371.5 13.2 %collective-permute-done.32 = bf16[24,9216]{1,0:T(8,128)(2,1)S(1)} collective-permute-done((bf16[24,9216]{1,0:T(8,128)(2,1)S(1)}, bf16[24,9216]{1,0:T(8,128)(2,1)S(1)}, u32[]{:S(2)}, u32[]{:S(2)}) %collective-permute-start.32) | collective-permute-done | bytes 442400 | tf_op jit(solution)/shard_map/ppermute | solution.py:417
  388.7 10.8 %moments.1 = (f32[192,2304]{1,0:T(8,128)}, f32[192,768]{1,0:T(8,128)}, f32[192,3072]{1,0:T(8,128)}, f32[192,3072]{1,0:T(8,128)}, f32[192,2304]{1,0:T(8,128)}, /*...) custom-call(s32[1]{0:T(128)} %bitcast.4.where_ref, ...), custom_call_target="tpu_custom_call" | custom-call | bytes 360000000 | tf_op jit(solution)/shard_map/moments/pallas_call | solution.py:971
  399.5 7.5 %all-to-all-done.6.refs_0_.refs_1_.refs_2_.refs_3_ = bf16[4,8,24,3072]{3,2,1,0:T(8,128)(2,1)} async-done(((bf16[4,8,24,3072]{3,2,1,0:T(8,128)(2,1)}), bf16[4,8,24,3072]{3,2,1,0:T(8,128)(2,1)}, u32[]{:S(2)}, u32[]{:S(2)}) %all-to-all-start.6) | async-done | bytes 4718624 | tf_op jit(solution)/shard_map/all_to_all | solution.py:421
  407.0 9.2 %weights.1 = (f32[192,2304]{1,0:T(8,128)}, f32[192,768]{1,0:T(8,128)}, f32[192,3072]{1,0:T(8,128)}, f32[192,3072]{1,0:T(8,128)}) custom-call(s32[1]{0:T(128)} %bitcast.4.where_ref, bf16[4,8,24,3072]{3,2,1,0:T(8,128)(2,1)} %all-to-all-done.6.refs_0_.refs_1_.refs_2_.refs_3_, bf16[4,8,24,3072]{3,2,1,0:T(8,128)(2,1)} %all-to-all-done.6.refs_0_.refs_1_.refs_2_.refs_3_, ...), custom_call_target="tpu_custom_call" | custom-call | tf_op jit(solution)/shard_map/weights/pallas_call | solution.py:1009
  (269 shorter events, 65.9 us)
Async XLA Ops:
  4.2 24.4 %copy-start.9 = (bf16[272,768]{1,0:T(8,128)(2,1)}, bf16[272,768]{1,0:T(8,128)(2,1)S(1)}, u32[]{:S(2)}) copy-start(bf16[272,768]{1,0:T(8,128)(2,1)S(1)} %pack.1.refs_1_) | copy-start | bytes 1253380
  4.2 12.7 %collective-permute-start.1 = (bf16[272,768]{1,0:T(8,128)(2,1)S(1)}, bf16[272,768]{1,0:T(8,128)(2,1)S(1)}, u32[]{:S(2)}, u32[]{:S(2)}) collective-permute-start(bf16[272,768]{1,0:T(8,128)(2,1)S(1)} %pack.1.refs_1_), channel_id=1, source_target_pairs={{0,2},{1,3},{2,0},{3,1},{4,6},{5,7},{6,4},{7,5},{8,10},{9,11},{10,... | collective-permute-start | bytes 1253384 | tf_op jit(solution)/shard_map/ppermute | solution.py:417
  7.2 12.0 %collective-permute-start = (bf16[272,768]{1,0:T(8,128)(2,1)S(1)}, bf16[272,768]{1,0:T(8,128)(2,1)S(1)}, u32[]{:S(2)}, u32[]{:S(2)}) collective-permute-start(bf16[272,768]{1,0:T(8,128)(2,1)S(1)} %pack.1.refs_1_), channel_id=1, source_target_pairs={{0,1},{1,0},{2,3},{3,2},{4,5},{5,4},{6,7},{7,6},{8,9},{9,8},{10,11... | collective-permute-start | bytes 1253384 | tf_op jit(solution)/shard_map/ppermute | solution.py:417
  10.4 18.2 %all-to-all-start = ((bf16[4,192,576]{2,1,0:T(8,128)(2,1)}), bf16[4,192,576]{2,1,0:T(8,128)(2,1)}, u32[]{:S(2)}, u32[]{:S(2)}) async-start(bf16[4,192,576]{2,1,0:T(8,128)(2,1)} %heads_split.1), calls=%async_computation | async-start | bytes 1966080 | tf_op jit(solution)/shard_map/all_to_all | solution.py:421
  15.5 17.3 %copy-start.16 = (f32[128,384]{1,0:T(8,128)}, f32[128,384]{1,0:T(8,128)S(1)}, u32[]{:S(2)}) copy-start(f32[128,384]{1,0:T(8,128)S(1)} %copy.60.refs_9_.refs_10_) | copy-start | bytes 589828
  15.6 17.1 %copy-start.18 = (f32[128,384]{1,0:T(8,128)}, f32[128,384]{1,0:T(8,128)S(1)}, u32[]{:S(2)}) copy-start(f32[128,384]{1,0:T(8,128)S(1)} %copy.59.refs_8_.refs_9_) | copy-start | bytes 589828
  15.8 16.9 %copy-start.20 = (f32[128,384]{1,0:T(8,128)}, f32[128,384]{1,0:T(8,128)S(1)}, u32[]{:S(2)}) copy-start(f32[128,384]{1,0:T(8,128)S(1)} %copy.58.refs_7_.refs_8_) | copy-start | bytes 589828
  16.9 17.4 %copy-start.31 = (bf16[272,768]{1,0:T(8,128)(2,1)}, bf16[272,768]{1,0:T(8,128)(2,1)S(1)}, u32[]{:S(2)}) copy-start(bf16[272,768]{1,0:T(8,128)(2,1)S(1)} %collective-permute-done.1.refs_3_) | copy-start | bytes 1253380
  17.0 11.7 %collective-permute-start.2 = (bf16[272,768]{1,0:T(8,128)(2,1)S(1)}, bf16[272,768]{1,0:T(8,128)(2,1)S(1)}, u32[]{:S(2)}, u32[]{:S(2)}) collective-permute-start(bf16[272,768]{1,0:T(8,128)(2,1)S(1)} %collective-permute-done.1.refs_3_), channel_id=1, source_target_pairs={{0,1},{1,0},{2,3},{3,2},{4,5},{5,4},{6,7},{7,6},{8,9},{9,8},{10,11... | collective-permute-start | bytes 1253384 | tf_op jit(solution)/shard_map/ppermute | solution.py:417
  19.3 15.1 %copy-start.32 = (bf16[272,768]{1,0:T(8,128)(2,1)}, bf16[272,768]{1,0:T(8,128)(2,1)S(1)}, u32[]{:S(2)}) copy-start(bf16[272,768]{1,0:T(8,128)(2,1)S(1)} %collective-permute-done.refs_2_) | copy-start | bytes 1253380
  34.4 33.1 %all-to-all-start.1 = ((bf16[8,448,128]{2,1,0:T(8,128)(2,1)}), bf16[8,448,128]{2,1,0:T(8,128)(2,1)S(1)}, u32[]{:S(2)}, u32[]{:S(2)}) async-start(bf16[8,448,128]{2,1,0:T(8,128)(2,1)} %get-tuple-element.79), calls=%async_computation.1 | async-start | bytes 1835008 | tf_op jit(solution)/shard_map/all_to_all | solution.py:421
  47.8 19.6 %collective-permute-start.3 = (bf16[240,1536]{1,0:T(8,128)(2,1)}, bf16[240,1536]{1,0:T(8,128)(2,1)S(1)}, u32[]{:S(2)}, u32[]{:S(2)}) collective-permute-start(bf16[240,1536]{1,0:T(8,128)(2,1)} %get-tuple-element.80), channel_id=1, source_target_pairs={{0,2},{1,3},{2,0},{3,1},{4,6},{5,7},{6,4},{7,5},{8,10},{9,11},{10,... | collective-permute-start | bytes 2211848 | tf_op jit(solution)/shard_map/ppermute | solution.py:417
  48.7 38.3 %collective-permute-start.4 = (bf16[240,1536]{1,0:T(8,128)(2,1)}, bf16[240,1536]{1,0:T(8,128)(2,1)S(1)}, u32[]{:S(2)}, u32[]{:S(2)}) collective-permute-start(bf16[240,1536]{1,0:T(8,128)(2,1)} %copy-done.47), channel_id=1, source_target_pairs={{0,1},{1,0},{2,3},{3,2},{4,5},{5,4},{6,7},{7,6},{8,9},{9,8},{10,11... | collective-permute-start | bytes 2211848 | tf_op jit(solution)/shard_map/ppermute | solution.py:417
  48.7 38.4 %collective-permute-start.5 = (bf16[240,1536]{1,0:T(8,128)(2,1)}, bf16[240,1536]{1,0:T(8,128)(2,1)}, u32[]{:S(2)}, u32[]{:S(2)}) collective-permute-start(bf16[240,1536]{1,0:T(8,128)(2,1)} %copy-done.46), channel_id=1, source_target_pairs={{0,3},{1,2},{2,1},{3,0},{4,7},{5,6},{6,5},{7,4},{8,11},{9,10},{10,... | collective-permute-start | bytes 2211848 | tf_op jit(solution)/shard_map/ppermute | solution.py:417
  52.2 34.8 %copy-start.60 = (f32[768]{0:T(1024)S(1)}, f32[768]{0:T(1024)}, u32[]{:S(2)}) copy-start(f32[768]{0:T(1024)} %param.31) | copy-start | bytes 9220
  67.5 19.6 %copy-start.1 = (bf16[240,1536]{1,0:T(8,128)(2,1)}, bf16[240,1536]{1,0:T(8,128)(2,1)S(1)}, u32[]{:S(2)}) copy-start(bf16[240,1536]{1,0:T(8,128)(2,1)S(1)} %collective-permute-done.3.refs_5_.refs_6_) | copy-start | bytes 2211844
  80.6 46.7 %all-to-all-start.2 = ((bf16[8,448,128]{2,1,0:T(8,128)(2,1)}), bf16[8,448,128]{2,1,0:T(8,128)(2,1)}, u32[]{:S(2)}, u32[]{:S(2)}) async-start(bf16[8,448,128]{2,1,0:T(8,128)(2,1)} %attention.1), calls=%async_computation.2 | async-start | bytes 1835008 | tf_op jit(solution)/shard_map/all_to_all | solution.py:421
  95.0 32.4 %copy-start.4 = (bf16[512,768]{1,0:T(8,128)(2,1)S(1)}, bf16[512,768]{1,0:T(8,128)(2,1)}, u32[]{:S(2)}) copy-start(bf16[512,768]{1,0:T(8,128)(2,1)} %get-tuple-element.82.refs_2_.refs_3_) | copy-start | bytes 2359300
  95.0 32.4 %copy-start.17 = (f32[128,384]{1,0:T(8,128)S(1)}, f32[128,384]{1,0:T(8,128)}, u32[]{:S(2)}) copy-start(f32[128,384]{1,0:T(8,128)} %copy-done.16) | copy-start | bytes 589828
  95.0 28.3 %collective-permute-start.6 = (bf16[4,4,24,1536]{3,2,1,0:T(8,128)(2,1)}, bf16[4,4,24,1536]{3,2,1,0:T(8,128)(2,1)S(1)}, u32[]{:S(2)}, u32[]{:S(2)}) collective-permute-start(bf16[4,4,24,1536]{3,2,1,0:T(8,128)(2,1)} %get-tuple-element.90), channel_id=1, source_target_pairs={{0,4},{4,0},{8,12},{12,8},{16,20},{20,16},{24,28},{28,24},{1,5},{5... | collective-permute-start | bytes 3538952 | tf_op jit(solution)/shard_map/ppermute | solution.py:417
  138.1 47.2 %copy-start.6 = (f32[4,24,1536]{2,1,0:T(8,128)S(1)}, f32[4,24,1536]{2,1,0:T(8,128)}, u32[]{:S(2)}) copy-start(f32[4,24,1536]{2,1,0:T(8,128)} %copy-done.5) | copy-start | bytes 1769476
  138.1 47.2 %all-to-all-start.3 = ((bf16[4,384,768]{2,1,0:T(8,128)(2,1)}), bf16[4,384,768]{2,1,0:T(8,128)(2,1)}, u32[]{:S(2)}, u32[]{:S(2)}) async-start(bf16[4,384,768]{2,1,0:T(8,128)(2,1)} %get-tuple-element.93), calls=%async_computation.3 | async-start | bytes 4718592 | tf_op jit(solution)/shard_map/all_to_all | solution.py:421
  142.7 15.9 %collective-permute-start.7 = (bf16[4,4,24,768]{3,2,1,0:T(8,128)(2,1)}, bf16[4,4,24,768]{3,2,1,0:T(8,128)(2,1)S(1)}, u32[]{:S(2)}, u32[]{:S(2)}) collective-permute-start(bf16[4,4,24,768]{3,2,1,0:T(8,128)(2,1)} %copy-done.48), channel_id=1, source_target_pairs={{0,4},{4,0},{8,12},{12,8},{16,20},{20,16},{24,28},{28,24},{1,5},{5... | collective-permute-start | bytes 1769480 | tf_op jit(solution)/shard_map/ppermute | solution.py:417
  143.0 21.3 %collective-permute-start.11 = (bf16[4,24,1536]{2,1,0:T(8,128)(2,1)}, bf16[4,24,1536]{2,1,0:T(8,128)(2,1)S(1)}, u32[]{:S(2)}, u32[]{:S(2)}) collective-permute-start(bf16[4,24,1536]{2,1,0:T(8,128)(2,1)} %get-tuple-element.102), channel_id=1, source_target_pairs={{0,8},{4,12},{8,0},{12,4},{16,24},{20,28},{24,16},{28,20},{1,9},{5... | collective-permute-start | bytes 884744 | tf_op jit(solution)/shard_map/ppermute | solution.py:417
  144.4 23.7 %collective-permute-start.12 = (bf16[4,24,1536]{2,1,0:T(8,128)(2,1)}, bf16[4,24,1536]{2,1,0:T(8,128)(2,1)S(1)}, u32[]{:S(2)}, u32[]{:S(2)}) collective-permute-start(bf16[4,24,1536]{2,1,0:T(8,128)(2,1)} %copy-done.50), channel_id=1, source_target_pairs={{0,16},{4,20},{8,24},{12,28},{16,0},{20,4},{24,8},{28,12},{1,17},{... | collective-permute-start | bytes 884744 | tf_op jit(solution)/shard_map/ppermute | solution.py:417
  145.9 22.9 %collective-permute-start.13 = (bf16[4,24,1536]{2,1,0:T(8,128)(2,1)}, bf16[4,24,1536]{2,1,0:T(8,128)(2,1)S(1)}, u32[]{:S(2)}, u32[]{:S(2)}) collective-permute-start(bf16[4,24,1536]{2,1,0:T(8,128)(2,1)} %copy-done.49), channel_id=1, source_target_pairs={{0,24},{4,28},{8,16},{12,20},{16,8},{20,12},{24,0},{28,4},{1,25},{... | collective-permute-start | bytes 884744 | tf_op jit(solution)/shard_map/ppermute | solution.py:417
  161.3 9.2 %collective-permute-start.8 = (bf16[4,24,768]{2,1,0:T(8,128)(2,1)S(1)}, bf16[4,24,768]{2,1,0:T(8,128)(2,1)S(1)}, u32[]{:S(2)}, u32[]{:S(2)}) collective-permute-start(bf16[4,24,768]{2,1,0:T(8,128)(2,1)S(1)} %get-tuple-element.99), channel_id=1, source_target_pairs={{0,8},{4,12},{8,0},{12,4},{16,24},{20,28},{24,16},{28,20},{1,9},{5... | collective-permute-start | bytes 442376 | tf_op jit(solution)/shard_map/ppermute | solution.py:417
  162.8 21.1 %collective-permute-start.9 = (bf16[4,24,768]{2,1,0:T(8,128)(2,1)S(1)}, bf16[4,24,768]{2,1,0:T(8,128)(2,1)S(1)}, u32[]{:S(2)}, u32[]{:S(2)}) collective-permute-start(bf16[4,24,768]{2,1,0:T(8,128)(2,1)S(1)} %get-tuple-element.100), channel_id=1, source_target_pairs={{0,16},{4,20},{8,24},{12,28},{16,0},{20,4},{24,8},{28,12},{1,17},{... | collective-permute-start | bytes 442376 | tf_op jit(solution)/shard_map/ppermute | solution.py:417
  164.2 20.3 %collective-permute-start.10 = (bf16[4,24,768]{2,1,0:T(8,128)(2,1)S(1)}, bf16[4,24,768]{2,1,0:T(8,128)(2,1)S(1)}, u32[]{:S(2)}, u32[]{:S(2)}) collective-permute-start(bf16[4,24,768]{2,1,0:T(8,128)(2,1)S(1)} %get-tuple-element.101), channel_id=1, source_target_pairs={{0,24},{4,28},{8,16},{12,20},{16,8},{20,12},{24,0},{28,4},{1,25},{... | collective-permute-start | bytes 442376 | tf_op jit(solution)/shard_map/ppermute | solution.py:417
  191.5 15.6 %copy-start.44 = (f32[24,768]{1,0:T(8,128)}, f32[24,768]{1,0:T(8,128)S(1)}, u32[]{:S(2)}) copy-start(f32[24,768]{1,0:T(8,128)S(1)} %get-tuple-element.109.refs_2_) | copy-start | bytes 221188
  191.6 13.0 %all-to-all-start.4 = ((bf16[4,4,24,768]{3,2,1,0:T(8,128)(2,1)}), bf16[4,4,24,768]{3,2,1,0:T(8,128)(2,1)S(1)}, u32[]{:S(2)}, u32[]{:S(2)}) async-start(bf16[4,4,24,768]{3,2,1,0:T(8,128)(2,1)} %get-tuple-element.105), calls=%async_computation.4 | async-start | bytes 1179648 | tf_op jit(solution)/shard_map/all_to_all | solution.py:421
  207.9 21.4 %collective-permute-start.15 = (bf16[4,24,3072]{2,1,0:T(8,128)(2,1)}, bf16[4,24,3072]{2,1,0:T(8,128)(2,1)S(1)}, u32[]{:S(2)}, u32[]{:S(2)}) collective-permute-start(bf16[4,24,3072]{2,1,0:T(8,128)(2,1)} %get-tuple-element.107.refs_1_), channel_id=1, source_target_pairs={{0,8},{4,12},{8,0},{12,4},{16,24},{20,28},{24,16},{28,20},{1,9},{5... | collective-permute-start | bytes 1769480 | tf_op jit(solution)/shard_map/ppermute | solution.py:417
  213.4 21.6 %copy-start.59 = (f32[768]{0:T(1024)S(1)}, f32[768]{0:T(1024)}, u32[]{:S(2)}) copy-start(f32[768]{0:T(1024)} %reduce_sum.186) | copy-start | bytes 9220
  213.5 33.9 %copy-start.51 = (f32[384,768]{1,0:T(8,128)}, f32[384,768]{1,0:T(8,128)S(1)}, u32[]{:S(2)}) copy-start(f32[384,768]{1,0:T(8,128)S(1)} %add.227) | copy-start | bytes 3538948
  213.5 54.5 %copy-start.30 = (bf16[1,128,768]{2,1,0:T(8,128)(2,1)S(1)}, bf16[1,128,768]{2,1,0:T(8,128)(2,1)}, u32[]{:S(2)}) copy-start(bf16[1,128,768]{2,1,0:T(8,128)(2,1)} %param.19) | copy-start | bytes 589828
  215.9 28.2 %collective-permute-start.17 = (bf16[4,24,3072]{2,1,0:T(8,128)(2,1)}, bf16[4,24,3072]{2,1,0:T(8,128)(2,1)S(1)}, u32[]{:S(2)}, u32[]{:S(2)}) collective-permute-start(bf16[4,24,3072]{2,1,0:T(8,128)(2,1)} %get-tuple-element.107.refs_1_), channel_id=1, source_target_pairs={{0,16},{4,20},{8,24},{12,28},{16,0},{20,4},{24,8},{28,12},{1,17},{... | collective-permute-start | bytes 1769480 | tf_op jit(solution)/shard_map/ppermute | solution.py:417
  229.3 14.9 %collective-permute-start.16 = (bf16[4,24,3072]{2,1,0:T(8,128)(2,1)S(1)}, bf16[4,24,3072]{2,1,0:T(8,128)(2,1)S(1)}, u32[]{:S(2)}, u32[]{:S(2)}) collective-permute-start(bf16[4,24,3072]{2,1,0:T(8,128)(2,1)S(1)} %collective-permute-done.15.refs_5_.refs_3_), channel_id=1, source_target_pairs={{0,4},{4,0},{8,12},{12,8},{16,20},{20,16},{24,28},{28,24},{1,5},{5... | collective-permute-start | bytes 1769480 | tf_op jit(solution)/shard_map/ppermute | solution.py:417
  238.9 28.6 %collective-permute-start.23 = (f32[72,128]{1,0:T(8,128)}, f32[72,128]{1,0:T(8,128)}, u32[]{:S(2)}, u32[]{:S(2)}) collective-permute-start(f32[72,128]{1,0:T(8,128)} %bitcast.18), channel_id=1, source_target_pairs={{0,3},{1,2},{2,1},{3,0},{4,7},{5,6},{6,5},{7,4},{8,11},{9,10},{10,... | collective-permute-start | bytes 110600 | tf_op jit(solution)/shard_map/ppermute | solution.py:417
  238.9 31.7 %collective-permute-start.22 = (f32[72,128]{1,0:T(8,128)}, f32[72,128]{1,0:T(8,128)}, u32[]{:S(2)}, u32[]{:S(2)}) collective-permute-start(f32[72,128]{1,0:T(8,128)} %bitcast.18), channel_id=1, source_target_pairs={{0,2},{1,3},{2,0},{3,1},{4,6},{5,7},{6,4},{7,5},{8,10},{9,11},{10,... | collective-permute-start | bytes 110600 | tf_op jit(solution)/shard_map/ppermute | solution.py:417
  245.3 15.6 %collective-permute-start.19 = (bf16[4,24,3072]{2,1,0:T(8,128)(2,1)S(1)}, bf16[4,24,3072]{2,1,0:T(8,128)(2,1)}, u32[]{:S(2)}, u32[]{:S(2)}) collective-permute-start(bf16[4,24,3072]{2,1,0:T(8,128)(2,1)S(1)} %again.1), channel_id=1, source_target_pairs={{0,24},{4,28},{8,16},{12,20},{16,8},{20,12},{24,0},{28,4},{1,25},{... | collective-permute-start | bytes 1769480 | tf_op jit(solution)/shard_map/ppermute | solution.py:417
  247.4 27.9 %collective-permute-start.14 = (bf16[4,24,3072]{2,1,0:T(8,128)(2,1)}, bf16[4,24,3072]{2,1,0:T(8,128)(2,1)S(1)}, u32[]{:S(2)}, u32[]{:S(2)}) collective-permute-start(bf16[4,24,3072]{2,1,0:T(8,128)(2,1)} %get-tuple-element.107.refs_1_), channel_id=1, source_target_pairs={{0,4},{4,0},{8,12},{12,8},{16,20},{20,16},{24,28},{28,24},{1,5},{5... | collective-permute-start | bytes 1769480 | tf_op jit(solution)/shard_map/ppermute | solution.py:417
  249.2 27.4 %collective-permute-start.18 = (bf16[4,24,3072]{2,1,0:T(8,128)(2,1)S(1)}, bf16[4,24,3072]{2,1,0:T(8,128)(2,1)S(1)}, u32[]{:S(2)}, u32[]{:S(2)}) collective-permute-start(bf16[4,24,3072]{2,1,0:T(8,128)(2,1)S(1)} %collective-permute-done.17.refs_3_.refs_7_.refs_5_), channel_id=1, source_target_pairs={{0,4},{4,0},{8,12},{12,8},{16,20},{20,16},{24,28},{28,24},{1,5},{5... | collective-permute-start | bytes 1769480 | tf_op jit(solution)/shard_map/ppermute | solution.py:417
  260.9 25.4 %collective-permute-start.20 = (bf16[4,24,3072]{2,1,0:T(8,128)(2,1)}, bf16[4,24,3072]{2,1,0:T(8,128)(2,1)}, u32[]{:S(2)}, u32[]{:S(2)}) collective-permute-start(bf16[4,24,3072]{2,1,0:T(8,128)(2,1)} %collective-permute-done.19.refs_9_.refs_7_), channel_id=1, source_target_pairs={{0,4},{4,0},{8,12},{12,8},{16,20},{20,16},{24,28},{28,24},{1,5},{5... | collective-permute-start | bytes 1769480 | tf_op jit(solution)/shard_map/ppermute | solution.py:417
  263.2 12.1 %all-to-all-start.5 = ((bf16[4,24,2112]{2,1,0:T(8,128)(2,1)}), bf16[4,24,2112]{2,1,0:T(8,128)(2,1)}, u32[]{:S(2)}, u32[]{:S(2)}) async-start(bf16[4,24,2112]{2,1,0:T(8,128)(2,1)} %copy-done.33), calls=%async_computation.5 | async-start | bytes 835584 | tf_op jit(solution)/shard_map/all_to_all | solution.py:421
  267.5 3.0 collective-permute-start.21
  289.2 65.9 %collective-permute-start.31 = (bf16[24,9216]{1,0:T(8,128)(2,1)}, bf16[24,9216]{1,0:T(8,128)(2,1)}, u32[]{:S(2)}, u32[]{:S(2)}) collective-permute-start(bf16[24,9216]{1,0:T(8,128)(2,1)} %get-tuple-element.112.refs_9_), channel_id=1, source_target_pairs={{0,4},{4,0},{8,12},{12,8},{16,20},{20,16},{24,28},{28,24},{1,5},{5... | collective-permute-start | bytes 1327112 | tf_op jit(solution)/shard_map/ppermute | solution.py:417
  290.9 40.6 %collective-permute-start.27 = (bf16[24,9216]{1,0:T(8,128)(2,1)}, bf16[24,9216]{1,0:T(8,128)(2,1)S(1)}, u32[]{:S(2)}, u32[]{:S(2)}) collective-permute-start(bf16[24,9216]{1,0:T(8,128)(2,1)} %get-tuple-element.112.refs_9_), channel_id=1, source_target_pairs={{0,24},{4,28},{8,16},{12,20},{16,8},{20,12},{24,0},{28,4},{1,25},{... | collective-permute-start | bytes 1327112 | tf_op jit(solution)/shard_map/ppermute | solution.py:417
  292.7 38.8 %collective-permute-start.26 = (bf16[24,9216]{1,0:T(8,128)(2,1)}, bf16[24,9216]{1,0:T(8,128)(2,1)S(1)}, u32[]{:S(2)}, u32[]{:S(2)}) collective-permute-start(bf16[24,9216]{1,0:T(8,128)(2,1)} %get-tuple-element.112.refs_9_), channel_id=1, source_target_pairs={{0,16},{4,20},{8,24},{12,28},{16,0},{20,4},{24,8},{28,12},{1,17},{... | collective-permute-start | bytes 1327112 | tf_op jit(solution)/shard_map/ppermute | solution.py:417
  292.7 38.8 %collective-permute-start.25 = (bf16[24,9216]{1,0:T(8,128)(2,1)}, bf16[24,9216]{1,0:T(8,128)(2,1)S(1)}, u32[]{:S(2)}, u32[]{:S(2)}) collective-permute-start(bf16[24,9216]{1,0:T(8,128)(2,1)} %get-tuple-element.112.refs_9_), channel_id=1, source_target_pairs={{0,8},{4,12},{8,0},{12,4},{16,24},{20,28},{24,16},{28,20},{1,9},{5... | collective-permute-start | bytes 1327112 | tf_op jit(solution)/shard_map/ppermute | solution.py:417
  295.3 36.2 %collective-permute-start.24 = (f32[72,128]{1,0:T(8,128)S(1)}, f32[72,128]{1,0:T(8,128)S(1)}, u32[]{:S(2)}, u32[]{:S(2)}) collective-permute-start(f32[72,128]{1,0:T(8,128)S(1)} %get-tuple-element.113), channel_id=1, source_target_pairs={{0,4},{4,0},{8,12},{12,8},{16,20},{20,16},{24,28},{28,24},{1,5},{5... | collective-permute-start | bytes 110600 | tf_op jit(solution)/shard_map/ppermute | solution.py:417
  343.5 14.4 %collective-permute-start.30 = (f32[72,128]{1,0:T(8,128)S(1)}, f32[72,128]{1,0:T(8,128)S(1)}, u32[]{:S(2)}, u32[]{:S(2)}) collective-permute-start(f32[72,128]{1,0:T(8,128)S(1)} %get-tuple-element.114), channel_id=1, source_target_pairs={{0,24},{4,28},{8,16},{12,20},{16,8},{20,12},{24,0},{28,4},{1,25},{... | collective-permute-start | bytes 110600 | tf_op jit(solution)/shard_map/ppermute | solution.py:417
  345.4 14.3 %collective-permute-start.29 = (f32[72,128]{1,0:T(8,128)S(1)}, f32[72,128]{1,0:T(8,128)S(1)}, u32[]{:S(2)}, u32[]{:S(2)}) collective-permute-start(f32[72,128]{1,0:T(8,128)S(1)} %get-tuple-element.114), channel_id=1, source_target_pairs={{0,16},{4,20},{8,24},{12,28},{16,0},{20,4},{24,8},{28,12},{1,17},{... | collective-permute-start | bytes 110600 | tf_op jit(solution)/shard_map/ppermute | solution.py:417
  345.4 14.3 %collective-permute-start.28 = (f32[72,128]{1,0:T(8,128)S(1)}, f32[72,128]{1,0:T(8,128)S(1)}, u32[]{:S(2)}, u32[]{:S(2)}) collective-permute-start(f32[72,128]{1,0:T(8,128)S(1)} %get-tuple-element.114), channel_id=1, source_target_pairs={{0,8},{4,12},{8,0},{12,4},{16,24},{20,28},{24,16},{28,20},{1,9},{5... | collective-permute-start | bytes 110600 | tf_op jit(solution)/shard_map/ppermute | solution.py:417
  348.0 19.6 %copy-start.61 = (f32[768]{0:T(1024)S(1)}, f32[768]{0:T(1024)}, u32[]{:S(2)}) copy-start(f32[768]{0:T(1024)} %param.31) | copy-start | bytes 9220
  348.0 20.3 %copy-start.66 = (f32[192]{0:T(256)S(1)}, f32[192]{0:T(256)}, u32[]{:S(2)}) copy-start(f32[192]{0:T(256)} %param.25) | copy-start | bytes 2308
  348.0 20.9 %copy-start.67 = (f32[192]{0:T(256)S(1)}, f32[192]{0:T(256)}, u32[]{:S(2)}) copy-start(f32[192]{0:T(256)} %param.24) | copy-start | bytes 2308
  348.0 21.5 %copy-start.68 = (f32[192]{0:T(256)S(1)}, f32[192]{0:T(256)}, u32[]{:S(2)}) copy-start(f32[192]{0:T(256)} %param.23) | copy-start | bytes 2308
  348.1 22.2 %copy-start.69 = (f32[192]{0:T(256)S(1)}, f32[192]{0:T(256)}, u32[]{:S(2)}) copy-start(f32[192]{0:T(256)} %param.22) | copy-start | bytes 2308
  348.1 22.8 %copy-start.62 = (f32[576]{0:T(1024)S(1)}, f32[576]{0:T(1024)}, u32[]{:S(2)}) copy-start(f32[576]{0:T(1024)} %param.27) | copy-start | bytes 6916
  348.1 59.0 %all-to-all-start.6 = ((bf16[4,8,24,3072]{3,2,1,0:T(8,128)(2,1)}), bf16[4,8,24,3072]{3,2,1,0:T(8,128)(2,1)}, u32[]{:S(2)}, u32[]{:S(2)}) async-start(bf16[4,8,24,3072]{3,2,1,0:T(8,128)(2,1)} %get-tuple-element.119), calls=%async_computation.6 | async-start | bytes 9437184 | tf_op jit(solution)/shard_map/all_to_all | solution.py:421
  353.2 34.7 %collective-permute-start.34 = (bf16[24,9216]{1,0:T(8,128)(2,1)S(1)}, bf16[24,9216]{1,0:T(8,128)(2,1)S(1)}, u32[]{:S(2)}, u32[]{:S(2)}) collective-permute-start(bf16[24,9216]{1,0:T(8,128)(2,1)S(1)} %copy-done.11), channel_id=1, source_target_pairs={{0,4},{4,0},{8,12},{12,8},{16,20},{20,16},{24,28},{28,24},{1,5},{5... | collective-permute-start | bytes 1327112 | tf_op jit(solution)/shard_map/ppermute | solution.py:417
  355.0 31.3 %collective-permute-start.33 = (bf16[24,9216]{1,0:T(8,128)(2,1)S(1)}, bf16[24,9216]{1,0:T(8,128)(2,1)S(1)}, u32[]{:S(2)}, u32[]{:S(2)}) collective-permute-start(bf16[24,9216]{1,0:T(8,128)(2,1)S(1)} %copy-done.13), channel_id=1, source_target_pairs={{0,4},{4,0},{8,12},{12,8},{16,20},{20,16},{24,28},{28,24},{1,5},{5... | collective-permute-start | bytes 1327112 | tf_op jit(solution)/shard_map/ppermute | solution.py:417
  358.0 26.7 %collective-permute-start.32 = (bf16[24,9216]{1,0:T(8,128)(2,1)S(1)}, bf16[24,9216]{1,0:T(8,128)(2,1)S(1)}, u32[]{:S(2)}, u32[]{:S(2)}) collective-permute-start(bf16[24,9216]{1,0:T(8,128)(2,1)S(1)} %copy-done.15), channel_id=1, source_target_pairs={{0,4},{4,0},{8,12},{12,8},{16,20},{20,16},{24,28},{28,24},{1,5},{5... | collective-permute-start | bytes 1327112 | tf_op jit(solution)/shard_map/ppermute | solution.py:417
  362.9 53.4 %copy-start.63 = (f32[192]{0:T(256)}, f32[192]{0:T(256)S(1)}, u32[]{:S(2)}) copy-start(f32[192]{0:T(256)S(1)} %get-tuple-element.229) | copy-start | bytes 2308
  (49 other events, 190.9 us)

commit v4 on v3

--- a/solution.py
+++ b/solution.py
@@ -1171,7 +1171,7 @@
             pltpu.VMEM((SHARDS * rows, 3 * part), half),
             pltpu.VMEM((width, width), single),
         ],
-        [mlp_sums[0]],
+        [mlp_came],
     )
     _, heads_sums = scatter_ctx(send, keep, where, "heads_z")
     home = exchange(home)

time: 423 us -> 419 us (level)
  local copies, waits for them, and re-layouts: 52.9 us -> 44.4 us
  starting transfers between devices: 77.8 us -> 82.9 us
    unnamed x156 -> x128, local copies, waits for them, and re-layouts: 41.8 us -> 34.6 us
    ppermute x35, starting transfers between devices: 43.1 us -> 48.3 us  [swap(): return lax.ppermute(x, axis, [(i, i ^ offset) for i in range(count)])]
  transfers between devices with their start and end apart: 42 -> 42, of which waited for: 16 -> 18; matrix products, arithmetic and copies ran while one was open for 11% -> 10% of each run, Pallas kernels for 21% -> 21%
where the time goes in v4:
time: 419 us; the launch traced here: 414 us
  waiting for transfers between devices  150 us (36%)
  Pallas kernels  111 us (26%)
  starting transfers between devices  82.9 us (20%)
  local copies, waits for them, and re-layouts  44.4 us (11%)
  other arithmetic  18.5 us (4%)
  between operations  6.52 us (2%)
    ppermute x35, waiting for transfers between devices, swap(): return lax.ppermute(x, axis, [(i, i ^ offset) for i in range(count)])  122 us
    pallas_call x15, Pallas kernels, call(): pl.pallas_call(body, in_specs=[pl.BlockSpec(memory_space=pltpu.SMEM)] + [...  91 us
    ppermute x35, starting transfers between devices, swap(): return lax.ppermute(x, axis, [(i, i ^ offset) for i in range(count)])  48.3 us
    unnamed x128, local copies, waits for them, and re-layouts  34.6 us
    all_to_all x7, starting transfers between devices, exchange(): return lax.all_to_all(x, axis, 0, 0)  34.6 us
    all_to_all x7, waiting for transfers between devices, exchange(): return lax.all_to_all(x, axis, 0, 0)  28.7 us
    pallas_call x1, Pallas kernels, write_moments(): pl.pallas_call(moment_kernel, grid_spec=pltpu.PrefetchScalarGridSpec(num_...  10.8 us
    pallas_call x1, Pallas kernels, write_weights(): pl.pallas_call(weight_kernel, grid_spec=pltpu.PrefetchScalarGridSpec(num_...  9.25 us
  transfers between devices with their start and end apart: 42, of which 18 were waited for; matrix products, arithmetic and copies ran while one was open for 10% of the time, Pallas kernels for 21%

profile of v4, /device:TPU:0, one launch (start us, length us, event | category | flops | bytes accessed | tf_op | source)
XLA Modules:
  0.0 413.7 jit_solution(8178356940581379383)
XLA Ops:
  4.2 3.0 collective-permute-start.1
  7.2 1.5 copy-done
  8.7 1.7 heads_split.1
  10.4 4.4 %all-to-all-start = ((bf16[4,192,576]{2,1,0:T(8,128)(2,1)}), bf16[4,192,576]{2,1,0:T(8,128)(2,1)}, u32[]{:S(2)}, u32[]{:S(2)}) async-start(bf16[4,192,576]{2,1,0:T(8,128)(2,1)} %heads_split.1), calls=%async_computation | async-start | bytes 1966080 | tf_op jit(solution)/shard_map/all_to_all | solution.py:421
  19.3 9.4 %all-to-all-done = bf16[4,192,576]{2,1,0:T(8,128)(2,1)} async-done(((bf16[4,192,576]{2,1,0:T(8,128)(2,1)}), bf16[4,192,576]{2,1,0:T(8,128)(2,1)}, u32[]{:S(2)}, u32[]{:S(2)}) %all-to-all-start) | async-done | bytes 884768 | tf_op jit(solution)/shard_map/all_to_all | solution.py:421
  28.6 4.1 pre.1
  34.4 6.5 %all-to-all-start.1 = ((bf16[8,448,128]{2,1,0:T(8,128)(2,1)}), bf16[8,448,128]{2,1,0:T(8,128)(2,1)S(1)}, u32[]{:S(2)}, u32[]{:S(2)}) async-start(bf16[8,448,128]{2,1,0:T(8,128)(2,1)} %get-tuple-element.79), calls=%async_computation.1 | async-start | bytes 1835008 | tf_op jit(solution)/shard_map/all_to_all | solution.py:421
  43.1 4.3 %mlp_split.1 = (bf16[240,1536]{1,0:T(8,128)(2,1)S(1)}, bf16[240,1536]{1,0:T(8,128)(2,1)}, bf16[240,1536]{1,0:T(8,128)(2,1)}, bf16[240,1536]{1,0:T(8,128)(2,1)}) custom-call(s32[4]{0:T(128)S(1)} %pad_add_fusion.refs_0_, f32[192,3072]{1,0:T(8,128)} %refs_6_.1, f32[192,3072]{1,0:T(8,128)} %refs_7_.1, f32[4,24,3072]{2,1,0:T(8,128)} %pad_maximum_fusion.refs_3_, ...), custom_call_target="tpu_custom_call" | custom-call | bytes 360000 | tf_op jit(solution)/shard_map/mlp_split/pallas_call | solution.py:446
  49.1 1.5 collective-permute-start.5
  53.0 14.9 %collective-permute-done.3.refs_5_.refs_6_ = bf16[240,1536]{1,0:T(8,128)(2,1)S(1)} collective-permute-done((bf16[240,1536]{1,0:T(8,128)(2,1)}, bf16[240,1536]{1,0:T(8,128)(2,1)S(1)}, u32[]{:S(2)}, u32[]{:S(2)}) %collective-permute-start.3) | collective-permute-done | bytes 737312 | tf_op jit(solution)/shard_map/ppermute | solution.py:417
  67.9 10.9 %attention.1 = bf16[8,448,128]{2,1,0:T(8,128)(2,1)} custom-call(s32[4]{0:T(128)S(1)} %pad_add_fusion.refs_0_, bf16[8,448,128]{2,1,0:T(8,128)(2,1)S(1)} %all-to-all-done.1.refs_1_, s32[1,1024]{1,0:T(1,128)S(1)} %fusion.12.refs_2_, s32[1024,1]{1,0:T(8,128)S(1)} %fusion.refs_3_, s32[512,1]{1,0:T(8,128)S(1)} %broadcast_in_dim_reshape.4.refs_4_, ...), custom_call_target="tpu_custom_call" | custom-call | bytes 360000 | tf_op jit(solution)/shard_map/attention/pallas_call | solution.py:446
  78.8 6.2 %all-to-all-start.2 = ((bf16[8,448,128]{2,1,0:T(8,128)(2,1)}), bf16[8,448,128]{2,1,0:T(8,128)(2,1)S(1)}, u32[]{:S(2)}, u32[]{:S(2)}) async-start(bf16[8,448,128]{2,1,0:T(8,128)(2,1)} %attention.1), calls=%async_computation.2 | async-start | bytes 1835008 | tf_op jit(solution)/shard_map/all_to_all | solution.py:421
  87.4 8.2 %mlp.1 = (bf16[4,4,24,1536]{3,2,1,0:T(8,128)(2,1)}, f32[4,4,24,1536]{3,2,1,0:T(8,128)}, f32[512,768]{1,0:T(8,128)}, f32[1,768]{1,0:T(1,128)S(1)}, f32[512,768]{1,0:T(8,128)}) custom-call(s32[4]{0:T(128)S(1)} %pad_add_fusion.refs_0_, bf16[512,768]{1,0:T(8,128)(2,1)S(1)} %copy-done.27, bf16[512,768]{1,0:T(8,128)(2,1)} %get-tuple-element.82.refs_2_.refs_3_, ...), custom_call_target="tpu_custom_call" | custom-call | bytes 360000 | tf_op jit(solution)/shard_map/mlp/pallas_call | solution.py:446
  95.6 2.0 collective-permute-start.6
  97.6 24.6 %collective-permute-done.6.refs_11_.refs_2_ = bf16[4,4,24,1536]{3,2,1,0:T(8,128)(2,1)S(1)} collective-permute-done((bf16[4,4,24,1536]{3,2,1,0:T(8,128)(2,1)}, bf16[4,4,24,1536]{3,2,1,0:T(8,128)(2,1)S(1)}, u32[]{:S(2)}, u32[]{:S(2)}) %collective-permute-start.6) | collective-permute-done | bytes 1179680 | tf_op jit(solution)/shard_map/ppermute | solution.py:417
  126.2 6.5 %post.1 = (bf16[4,4,24,768]{3,2,1,0:T(8,128)(2,1)}, f32[4,4,24,768]{3,2,1,0:T(8,128)}, f32[1,576]{1,0:T(1,128)S(1)}, f32[384,768]{1,0:T(8,128)}, bf16[4,384,768]{2,1,0:T(8,128)(2,1)}) custom-call(s32[4]{0:T(128)S(1)} %pad_add_fusion.refs_0_, bf16[8,448,128]{2,1,0:T(8,128)(2,1)S(1)} %all-to-all-done.2.refs_1_, bf16[512,768]{1,0:T(8,128)(2,1)S(1)} %copy-done.26, ...), custom_call_target="tpu_custom_call" | custom-call | bytes 360000 | tf_op jit(solution)/shard_map/post/pallas_call | solution.py:446
  132.7 4.6 %all-to-all-start.3 = ((bf16[4,384,768]{2,1,0:T(8,128)(2,1)}), bf16[4,384,768]{2,1,0:T(8,128)(2,1)}, u32[]{:S(2)}, u32[]{:S(2)}) async-start(bf16[4,384,768]{2,1,0:T(8,128)(2,1)} %get-tuple-element.91), calls=%async_computation.3 | async-start | bytes 4718592 | tf_op jit(solution)/shard_map/all_to_all | solution.py:421
  137.4 1.3 collective-permute-start.7
  138.7 1.9 mlp_z.1
  140.6 1.8 collective-permute-start.11
  142.4 2.1 collective-permute-start.12
  145.4 7.8 %collective-permute-done.7.refs_2_ = bf16[4,4,24,768]{3,2,1,0:T(8,128)(2,1)S(1)} collective-permute-done((bf16[4,4,24,768]{3,2,1,0:T(8,128)(2,1)}, bf16[4,4,24,768]{3,2,1,0:T(8,128)(2,1)S(1)}, u32[]{:S(2)}, u32[]{:S(2)}) %collective-permute-start.7) | collective-permute-done | bytes 589856 | tf_op jit(solution)/shard_map/ppermute | solution.py:417
  153.9 2.5 collective-permute-start.8
  156.5 2.1 collective-permute-start.9
  158.5 1.4 collective-permute-start.10
  159.9 5.9 %collective-permute-done.12.refs_7_ = bf16[4,24,1536]{2,1,0:T(8,128)(2,1)S(1)} collective-permute-done((bf16[4,24,1536]{2,1,0:T(8,128)(2,1)S(1)}, bf16[4,24,1536]{2,1,0:T(8,128)(2,1)S(1)}, u32[]{:S(2)}, u32[]{:S(2)}) %collective-permute-start.12) | collective-permute-done | bytes 294944 | tf_op jit(solution)/shard_map/ppermute | solution.py:417
  166.7 15.0 %collective-permute-done.9.refs_3_ = bf16[4,24,768]{2,1,0:T(8,128)(2,1)S(1)} collective-permute-done((bf16[4,24,768]{2,1,0:T(8,128)(2,1)S(1)}, bf16[4,24,768]{2,1,0:T(8,128)(2,1)S(1)}, u32[]{:S(2)}, u32[]{:S(2)}) %collective-permute-start.9) | collective-permute-done | bytes 147488 | tf_op jit(solution)/shard_map/ppermute | solution.py:417
  184.8 1.6 strip.1
  187.1 3.5 all-to-all-start.4
  192.1 8.0 %all-to-all-done.4.refs_1_ = bf16[4,4,24,768]{3,2,1,0:T(8,128)(2,1)S(1)} async-done(((bf16[4,4,24,768]{3,2,1,0:T(8,128)(2,1)}), bf16[4,4,24,768]{3,2,1,0:T(8,128)(2,1)S(1)}, u32[]{:S(2)}, u32[]{:S(2)}) %all-to-all-start.4) | async-done | bytes 589856 | tf_op jit(solution)/shard_map/all_to_all | solution.py:421
  200.1 2.0 owned.1
  202.8 2.0 collective-permute-start.15
  206.1 2.1 convert_reduce_fusion
  209.5 1.3 constant_dynamic-update-slice_fusion
  210.8 1.7 collective-permute-start.17
  212.6 12.6 %collective-permute-done.15.refs_5_.refs_3_ = bf16[4,24,3072]{2,1,0:T(8,128)(2,1)S(1)} collective-permute-done((bf16[4,24,3072]{2,1,0:T(8,128)(2,1)S(1)}, bf16[4,24,3072]{2,1,0:T(8,128)(2,1)S(1)}, u32[]{:S(2)}, u32[]{:S(2)}) %collective-permute-start.15) | collective-permute-done | bytes 589856 | tf_op jit(solution)/shard_map/ppermute | solution.py:417
  225.2 1.6 collective-permute-start.16
  228.1 1.3 constant_dynamic-update-slice_fusion.5
  232.0 1.3 constant_dynamic-update-slice_fusion.2
  234.6 4.2 %collective-permute-done.17.refs_3_.refs_7_.refs_5_ = bf16[4,24,3072]{2,1,0:T(8,128)(2,1)S(1)} collective-permute-done((bf16[4,24,3072]{2,1,0:T(8,128)(2,1)S(1)}, bf16[4,24,3072]{2,1,0:T(8,128)(2,1)S(1)}, u32[]{:S(2)}, u32[]{:S(2)}) %collective-permute-start.17) | collective-permute-done | bytes 589856 | tf_op jit(solution)/shard_map/ppermute | solution.py:417
  239.9 3.4 collective-permute-start.19
  244.8 1.6 collective-permute-start.14
  246.8 8.3 %collective-permute-done.19.refs_9_.refs_7_ = bf16[4,24,3072]{2,1,0:T(8,128)(2,1)} collective-permute-done((bf16[4,24,3072]{2,1,0:T(8,128)(2,1)S(1)}, bf16[4,24,3072]{2,1,0:T(8,128)(2,1)}, u32[]{:S(2)}, u32[]{:S(2)}) %collective-permute-start.19) | collective-permute-done | bytes 589856 | tf_op jit(solution)/shard_map/ppermute | solution.py:417
  255.1 1.7 collective-permute-start.20
  257.3 4.3 %all-to-all-start.5 = ((bf16[4,24,2112]{2,1,0:T(8,128)(2,1)}), bf16[4,24,2112]{2,1,0:T(8,128)(2,1)}, u32[]{:S(2)}, u32[]{:S(2)}) async-start(bf16[4,24,2112]{2,1,0:T(8,128)(2,1)} %copy-done.32), calls=%async_computation.5 | async-start | bytes 835584 | tf_op jit(solution)/shard_map/all_to_all | solution.py:421
  262.2 2.5 add_bitcast_fusion
  265.5 3.9 all-to-all-done.5.refs_1_
  269.4 4.4 %collective-permute-done.18.refs_8_.refs_6_ = bf16[4,24,3072]{2,1,0:T(8,128)(2,1)} collective-permute-done((bf16[4,24,3072]{2,1,0:T(8,128)(2,1)S(1)}, bf16[4,24,3072]{2,1,0:T(8,128)(2,1)}, u32[]{:S(2)}, u32[]{:S(2)}) %collective-permute-start.18) | collective-permute-done | bytes 589856 | tf_op jit(solution)/shard_map/ppermute | solution.py:417
  273.8 9.1 %collective-permute-done.20.refs_10_.refs_8_ = bf16[4,24,3072]{2,1,0:T(8,128)(2,1)} collective-permute-done((bf16[4,24,3072]{2,1,0:T(8,128)(2,1)}, bf16[4,24,3072]{2,1,0:T(8,128)(2,1)}, u32[]{:S(2)}, u32[]{:S(2)}) %collective-permute-start.20) | collective-permute-done | bytes 589856 | tf_op jit(solution)/shard_map/ppermute | solution.py:417
  283.8 1.9 grads.1
  285.7 1.6 collective-permute-start.31
  288.1 3.7 collective-permute-start.25
  292.1 1.8 bitcast_dynamic-update-slice_fusion.7
  294.0 34.1 %newton.1.refs_1_ = bf16[768,3072]{1,0:T(8,128)(2,1)} custom-call(s32[4]{0:T(128)S(1)} %pad_add_fusion.refs_0_, bf16[4,24,3072]{2,1,0:T(8,128)(2,1)S(1)} %get-tuple-element.107.refs_1_, bf16[4,24,3072]{2,1,0:T(8,128)(2,1)S(1)} %collective-permute-done.14.refs_4_.refs_2_, bf16[4,24,3072]{2,1,0:T(8,128)(2,1)S(1)} %collective-permute-done.15.refs_5_.refs_3_, ...), custom_call_target="tpu_custom_call" | custom-call | bytes 129600000 | tf_op jit(solution)/shard_map/newton/pallas_call | solution.py:446
  328.1 12.0 %last_newton.1 = (bf16[4,8,24,3072]{3,2,1,0:T(8,128)(2,1)}, f32[72,128]{1,0:T(8,128)S(1)}) custom-call(s32[4]{0:T(128)S(1)} %pad_add_fusion.refs_0_, bf16[768,3072]{1,0:T(8,128)(2,1)} %newton.1.refs_1_, f32[72,128]{1,0:T(8,128)S(1)} %add.245.refs_2_, bf16[24,9216]{1,0:T(8,128)(2,1)S(1)} %collective-permute-done.25.refs_3_, ...), custom_call_target="tpu_custom_call" | custom-call | bytes 32400000 | tf_op jit(solution)/shard_map/last_newton/pallas_call | solution.py:446
  341.6 2.9 collective-permute-start.28
  344.6 5.1 %all-to-all-start.6 = ((bf16[4,8,24,3072]{3,2,1,0:T(8,128)(2,1)}), bf16[4,8,24,3072]{3,2,1,0:T(8,128)(2,1)}, u32[]{:S(2)}, u32[]{:S(2)}) async-start(bf16[4,8,24,3072]{3,2,1,0:T(8,128)(2,1)} %get-tuple-element.119), calls=%async_computation.6 | async-start | bytes 9437184 | tf_op jit(solution)/shard_map/all_to_all | solution.py:421
  349.8 1.7 collective-permute-start.34
  351.9 1.8 bitcast_dynamic-update-slice_fusion.6
  354.5 1.6 collective-permute-start.32
  368.0 13.3 %collective-permute-done.32 = bf16[24,9216]{1,0:T(8,128)(2,1)S(1)} collective-permute-done((bf16[24,9216]{1,0:T(8,128)(2,1)S(1)}, bf16[24,9216]{1,0:T(8,128)(2,1)S(1)}, u32[]{:S(2)}, u32[]{:S(2)}) %collective-permute-start.32) | collective-permute-done | bytes 442400 | tf_op jit(solution)/shard_map/ppermute | solution.py:417
  385.3 10.8 %moments.1 = (f32[192,2304]{1,0:T(8,128)}, f32[192,768]{1,0:T(8,128)}, f32[192,3072]{1,0:T(8,128)}, f32[192,3072]{1,0:T(8,128)}, f32[192,2304]{1,0:T(8,128)}, /*...) custom-call(s32[1]{0:T(128)} %bitcast.4.where_ref, ...), custom_call_target="tpu_custom_call" | custom-call | bytes 360000000 | tf_op jit(solution)/shard_map/moments/pallas_call | solution.py:971
  396.1 7.5 %all-to-all-done.6.refs_0_.refs_1_.refs_2_.refs_3_ = bf16[4,8,24,3072]{3,2,1,0:T(8,128)(2,1)} async-done(((bf16[4,8,24,3072]{3,2,1,0:T(8,128)(2,1)}), bf16[4,8,24,3072]{3,2,1,0:T(8,128)(2,1)}, u32[]{:S(2)}, u32[]{:S(2)}) %all-to-all-start.6) | async-done | bytes 4718624 | tf_op jit(solution)/shard_map/all_to_all | solution.py:421
  403.6 9.2 %weights.1 = (f32[192,2304]{1,0:T(8,128)}, f32[192,768]{1,0:T(8,128)}, f32[192,3072]{1,0:T(8,128)}, f32[192,3072]{1,0:T(8,128)}) custom-call(s32[1]{0:T(128)} %bitcast.4.where_ref, bf16[4,8,24,3072]{3,2,1,0:T(8,128)(2,1)} %all-to-all-done.6.refs_0_.refs_1_.refs_2_.refs_3_, bf16[4,8,24,3072]{3,2,1,0:T(8,128)(2,1)} %all-to-all-done.6.refs_0_.refs_1_.refs_2_.refs_3_, ...), custom_call_target="tpu_custom_call" | custom-call | tf_op jit(solution)/shard_map/weights/pallas_call | solution.py:1009
  (241 shorter events, 59.4 us)
Async XLA Ops:
  4.2 24.4 %copy-start.11 = (bf16[272,768]{1,0:T(8,128)(2,1)}, bf16[272,768]{1,0:T(8,128)(2,1)S(1)}, u32[]{:S(2)}) copy-start(bf16[272,768]{1,0:T(8,128)(2,1)S(1)} %pack.1.refs_1_) | copy-start | bytes 1253380
  4.2 12.7 %collective-permute-start.1 = (bf16[272,768]{1,0:T(8,128)(2,1)S(1)}, bf16[272,768]{1,0:T(8,128)(2,1)S(1)}, u32[]{:S(2)}, u32[]{:S(2)}) collective-permute-start(bf16[272,768]{1,0:T(8,128)(2,1)S(1)} %pack.1.refs_1_), channel_id=1, source_target_pairs={{0,2},{1,3},{2,0},{3,1},{4,6},{5,7},{6,4},{7,5},{8,10},{9,11},{10,... | collective-permute-start | bytes 1253384 | tf_op jit(solution)/shard_map/ppermute | solution.py:417
  7.2 12.0 %collective-permute-start = (bf16[272,768]{1,0:T(8,128)(2,1)S(1)}, bf16[272,768]{1,0:T(8,128)(2,1)S(1)}, u32[]{:S(2)}, u32[]{:S(2)}) collective-permute-start(bf16[272,768]{1,0:T(8,128)(2,1)S(1)} %pack.1.refs_1_), channel_id=1, source_target_pairs={{0,1},{1,0},{2,3},{3,2},{4,5},{5,4},{6,7},{7,6},{8,9},{9,8},{10,11... | collective-permute-start | bytes 1253384 | tf_op jit(solution)/shard_map/ppermute | solution.py:417
  10.4 18.2 %all-to-all-start = ((bf16[4,192,576]{2,1,0:T(8,128)(2,1)}), bf16[4,192,576]{2,1,0:T(8,128)(2,1)}, u32[]{:S(2)}, u32[]{:S(2)}) async-start(bf16[4,192,576]{2,1,0:T(8,128)(2,1)} %heads_split.1), calls=%async_computation | async-start | bytes 1966080 | tf_op jit(solution)/shard_map/all_to_all | solution.py:421
  15.6 17.1 %copy-start.18 = (f32[128,384]{1,0:T(8,128)}, f32[128,384]{1,0:T(8,128)S(1)}, u32[]{:S(2)}) copy-start(f32[128,384]{1,0:T(8,128)S(1)} %copy.59.refs_8_.refs_9_) | copy-start | bytes 589828
  15.8 16.9 %copy-start.20 = (f32[128,384]{1,0:T(8,128)}, f32[128,384]{1,0:T(8,128)S(1)}, u32[]{:S(2)}) copy-start(f32[128,384]{1,0:T(8,128)S(1)} %copy.58.refs_7_.refs_8_) | copy-start | bytes 589828
  16.9 17.4 %copy-start.30 = (bf16[272,768]{1,0:T(8,128)(2,1)}, bf16[272,768]{1,0:T(8,128)(2,1)S(1)}, u32[]{:S(2)}) copy-start(bf16[272,768]{1,0:T(8,128)(2,1)S(1)} %collective-permute-done.1.refs_3_) | copy-start | bytes 1253380
  17.0 11.7 %collective-permute-start.2 = (bf16[272,768]{1,0:T(8,128)(2,1)S(1)}, bf16[272,768]{1,0:T(8,128)(2,1)S(1)}, u32[]{:S(2)}, u32[]{:S(2)}) collective-permute-start(bf16[272,768]{1,0:T(8,128)(2,1)S(1)} %collective-permute-done.1.refs_3_), channel_id=1, source_target_pairs={{0,1},{1,0},{2,3},{3,2},{4,5},{5,4},{6,7},{7,6},{8,9},{9,8},{10,11... | collective-permute-start | bytes 1253384 | tf_op jit(solution)/shard_map/ppermute | solution.py:417
  19.2 15.1 %copy-start.31 = (bf16[272,768]{1,0:T(8,128)(2,1)}, bf16[272,768]{1,0:T(8,128)(2,1)S(1)}, u32[]{:S(2)}) copy-start(bf16[272,768]{1,0:T(8,128)(2,1)S(1)} %collective-permute-done.refs_2_) | copy-start | bytes 1253380
  28.6 14.5 %copy-start.10 = (bf16[272,768]{1,0:T(8,128)(2,1)}, bf16[272,768]{1,0:T(8,128)(2,1)S(1)}, u32[]{:S(2)}) copy-start(bf16[272,768]{1,0:T(8,128)(2,1)S(1)} %collective-permute-done.2.refs_4_) | copy-start | bytes 1253380
  34.4 33.5 %all-to-all-start.1 = ((bf16[8,448,128]{2,1,0:T(8,128)(2,1)}), bf16[8,448,128]{2,1,0:T(8,128)(2,1)S(1)}, u32[]{:S(2)}, u32[]{:S(2)}) async-start(bf16[8,448,128]{2,1,0:T(8,128)(2,1)} %get-tuple-element.79), calls=%async_computation.1 | async-start | bytes 1835008 | tf_op jit(solution)/shard_map/all_to_all | solution.py:421
  48.3 19.6 %collective-permute-start.3 = (bf16[240,1536]{1,0:T(8,128)(2,1)}, bf16[240,1536]{1,0:T(8,128)(2,1)S(1)}, u32[]{:S(2)}, u32[]{:S(2)}) collective-permute-start(bf16[240,1536]{1,0:T(8,128)(2,1)} %get-tuple-element.80), channel_id=1, source_target_pairs={{0,2},{1,3},{2,0},{3,1},{4,6},{5,7},{6,4},{7,5},{8,10},{9,11},{10,... | collective-permute-start | bytes 2211848 | tf_op jit(solution)/shard_map/ppermute | solution.py:417
  49.0 36.0 %collective-permute-start.4 = (bf16[240,1536]{1,0:T(8,128)(2,1)}, bf16[240,1536]{1,0:T(8,128)(2,1)}, u32[]{:S(2)}, u32[]{:S(2)}) collective-permute-start(bf16[240,1536]{1,0:T(8,128)(2,1)} %get-tuple-element.85), channel_id=1, source_target_pairs={{0,1},{1,0},{2,3},{3,2},{4,5},{5,4},{6,7},{7,6},{8,9},{9,8},{10,11... | collective-permute-start | bytes 2211848 | tf_op jit(solution)/shard_map/ppermute | solution.py:417
  49.1 36.0 %collective-permute-start.5 = (bf16[240,1536]{1,0:T(8,128)(2,1)}, bf16[240,1536]{1,0:T(8,128)(2,1)}, u32[]{:S(2)}, u32[]{:S(2)}) collective-permute-start(bf16[240,1536]{1,0:T(8,128)(2,1)} %get-tuple-element.86), channel_id=1, source_target_pairs={{0,3},{1,2},{2,1},{3,0},{4,7},{5,6},{6,5},{7,4},{8,11},{9,10},{10,... | collective-permute-start | bytes 2211848 | tf_op jit(solution)/shard_map/ppermute | solution.py:417
  53.0 32.0 %copy-start.46 = (f32[768]{0:T(1024)S(1)}, f32[768]{0:T(1024)}, u32[]{:S(2)}) copy-start(f32[768]{0:T(1024)} %param.31) | copy-start | bytes 9220
  67.9 17.2 %copy-start.1 = (bf16[240,1536]{1,0:T(8,128)(2,1)}, bf16[240,1536]{1,0:T(8,128)(2,1)S(1)}, u32[]{:S(2)}) copy-start(bf16[240,1536]{1,0:T(8,128)(2,1)S(1)} %collective-permute-done.3.refs_5_.refs_6_) | copy-start | bytes 2211844
  78.8 43.4 %all-to-all-start.2 = ((bf16[8,448,128]{2,1,0:T(8,128)(2,1)}), bf16[8,448,128]{2,1,0:T(8,128)(2,1)S(1)}, u32[]{:S(2)}, u32[]{:S(2)}) async-start(bf16[8,448,128]{2,1,0:T(8,128)(2,1)} %attention.1), calls=%async_computation.2 | async-start | bytes 1835008 | tf_op jit(solution)/shard_map/all_to_all | solution.py:421
  85.0 38.2 %copy-start.6 = (bf16[512,768]{1,0:T(8,128)(2,1)S(1)}, bf16[512,768]{1,0:T(8,128)(2,1)}, u32[]{:S(2)}) copy-start(bf16[512,768]{1,0:T(8,128)(2,1)} %get-tuple-element.82.refs_2_.refs_3_) | copy-start | bytes 2359300
  95.6 26.6 %collective-permute-start.6 = (bf16[4,4,24,1536]{3,2,1,0:T(8,128)(2,1)}, bf16[4,4,24,1536]{3,2,1,0:T(8,128)(2,1)S(1)}, u32[]{:S(2)}, u32[]{:S(2)}) collective-permute-start(bf16[4,4,24,1536]{3,2,1,0:T(8,128)(2,1)} %get-tuple-element.89), channel_id=1, source_target_pairs={{0,4},{4,0},{8,12},{12,8},{16,20},{20,16},{24,28},{28,24},{1,5},{5... | collective-permute-start | bytes 3538952 | tf_op jit(solution)/shard_map/ppermute | solution.py:417
  132.7 50.3 %all-to-all-start.3 = ((bf16[4,384,768]{2,1,0:T(8,128)(2,1)}), bf16[4,384,768]{2,1,0:T(8,128)(2,1)}, u32[]{:S(2)}, u32[]{:S(2)}) async-start(bf16[4,384,768]{2,1,0:T(8,128)(2,1)} %get-tuple-element.91), calls=%async_computation.3 | async-start | bytes 4718592 | tf_op jit(solution)/shard_map/all_to_all | solution.py:421
  137.4 15.9 %copy-start.24 = (f32[4,4,24,768]{3,2,1,0:T(8,128)S(1)}, f32[4,4,24,768]{3,2,1,0:T(8,128)}, u32[]{:S(2)}) copy-start(f32[4,4,24,768]{3,2,1,0:T(8,128)} %get-tuple-element.94.refs_1_) | copy-start | bytes 3538948
  137.4 15.9 %collective-permute-start.7 = (bf16[4,4,24,768]{3,2,1,0:T(8,128)(2,1)}, bf16[4,4,24,768]{3,2,1,0:T(8,128)(2,1)S(1)}, u32[]{:S(2)}, u32[]{:S(2)}) collective-permute-start(bf16[4,4,24,768]{3,2,1,0:T(8,128)(2,1)} %get-tuple-element.95), channel_id=1, source_target_pairs={{0,4},{4,0},{8,12},{12,8},{16,20},{20,16},{24,28},{28,24},{1,5},{5... | collective-permute-start | bytes 1769480 | tf_op jit(solution)/shard_map/ppermute | solution.py:417
  140.6 17.9 %collective-permute-start.11 = (bf16[4,24,1536]{2,1,0:T(8,128)(2,1)S(1)}, bf16[4,24,1536]{2,1,0:T(8,128)(2,1)S(1)}, u32[]{:S(2)}, u32[]{:S(2)}) collective-permute-start(bf16[4,24,1536]{2,1,0:T(8,128)(2,1)S(1)} %get-tuple-element.102), channel_id=1, source_target_pairs={{0,8},{4,12},{8,0},{12,4},{16,24},{20,28},{24,16},{28,20},{1,9},{5... | collective-permute-start | bytes 884744 | tf_op jit(solution)/shard_map/ppermute | solution.py:417
  142.4 23.4 %collective-permute-start.12 = (bf16[4,24,1536]{2,1,0:T(8,128)(2,1)S(1)}, bf16[4,24,1536]{2,1,0:T(8,128)(2,1)S(1)}, u32[]{:S(2)}, u32[]{:S(2)}) collective-permute-start(bf16[4,24,1536]{2,1,0:T(8,128)(2,1)S(1)} %get-tuple-element.103), channel_id=1, source_target_pairs={{0,16},{4,20},{8,24},{12,28},{16,0},{20,4},{24,8},{28,12},{1,17},{... | collective-permute-start | bytes 884744 | tf_op jit(solution)/shard_map/ppermute | solution.py:417
  144.5 21.5 %collective-permute-start.13 = (bf16[4,24,1536]{2,1,0:T(8,128)(2,1)S(1)}, bf16[4,24,1536]{2,1,0:T(8,128)(2,1)S(1)}, u32[]{:S(2)}, u32[]{:S(2)}) collective-permute-start(bf16[4,24,1536]{2,1,0:T(8,128)(2,1)S(1)} %get-tuple-element.104), channel_id=1, source_target_pairs={{0,24},{4,28},{8,16},{12,20},{16,8},{20,12},{24,0},{28,4},{1,25},{... | collective-permute-start | bytes 884744 | tf_op jit(solution)/shard_map/ppermute | solution.py:417
  153.9 12.7 %collective-permute-start.8 = (bf16[4,24,768]{2,1,0:T(8,128)(2,1)S(1)}, bf16[4,24,768]{2,1,0:T(8,128)(2,1)S(1)}, u32[]{:S(2)}, u32[]{:S(2)}) collective-permute-start(bf16[4,24,768]{2,1,0:T(8,128)(2,1)S(1)} %get-tuple-element.97), channel_id=1, source_target_pairs={{0,8},{4,12},{8,0},{12,4},{16,24},{20,28},{24,16},{28,20},{1,9},{5... | collective-permute-start | bytes 442376 | tf_op jit(solution)/shard_map/ppermute | solution.py:417
  156.5 25.2 %collective-permute-start.9 = (bf16[4,24,768]{2,1,0:T(8,128)(2,1)S(1)}, bf16[4,24,768]{2,1,0:T(8,128)(2,1)S(1)}, u32[]{:S(2)}, u32[]{:S(2)}) collective-permute-start(bf16[4,24,768]{2,1,0:T(8,128)(2,1)S(1)} %get-tuple-element.98), channel_id=1, source_target_pairs={{0,16},{4,20},{8,24},{12,28},{16,0},{20,4},{24,8},{28,12},{1,17},{... | collective-permute-start | bytes 442376 | tf_op jit(solution)/shard_map/ppermute | solution.py:417
  158.5 23.8 %collective-permute-start.10 = (bf16[4,24,768]{2,1,0:T(8,128)(2,1)S(1)}, bf16[4,24,768]{2,1,0:T(8,128)(2,1)S(1)}, u32[]{:S(2)}, u32[]{:S(2)}) collective-permute-start(bf16[4,24,768]{2,1,0:T(8,128)(2,1)S(1)} %get-tuple-element.99), channel_id=1, source_target_pairs={{0,24},{4,28},{8,16},{12,20},{16,8},{20,12},{24,0},{28,4},{1,25},{... | collective-permute-start | bytes 442376 | tf_op jit(solution)/shard_map/ppermute | solution.py:417
  184.8 15.2 %copy-start.9 = (bf16[240,1536]{1,0:T(8,128)(2,1)S(1)}, bf16[240,1536]{1,0:T(8,128)(2,1)}, u32[]{:S(2)}) copy-start(bf16[240,1536]{1,0:T(8,128)(2,1)} %copy-done.7) | copy-start | bytes 2211844
  187.1 13.0 %all-to-all-start.4 = ((bf16[4,4,24,768]{3,2,1,0:T(8,128)(2,1)}), bf16[4,4,24,768]{3,2,1,0:T(8,128)(2,1)S(1)}, u32[]{:S(2)}, u32[]{:S(2)}) async-start(bf16[4,4,24,768]{3,2,1,0:T(8,128)(2,1)} %get-tuple-element.105), calls=%async_computation.4 | async-start | bytes 1179648 | tf_op jit(solution)/shard_map/all_to_all | solution.py:421
  190.5 14.3 %copy-start.40 = (f32[128,128]{1,0:T(8,128)S(1)}, f32[128,128]{1,0:T(8,128)}, u32[]{:S(2)}) copy-start(f32[128,128]{1,0:T(8,128)} %copy-done.39) | copy-start | bytes 196612
  202.8 22.3 %collective-permute-start.15 = (bf16[4,24,3072]{2,1,0:T(8,128)(2,1)S(1)}, bf16[4,24,3072]{2,1,0:T(8,128)(2,1)S(1)}, u32[]{:S(2)}, u32[]{:S(2)}) collective-permute-start(bf16[4,24,3072]{2,1,0:T(8,128)(2,1)S(1)} %get-tuple-element.107.refs_1_), channel_id=1, source_target_pairs={{0,8},{4,12},{8,0},{12,4},{16,24},{20,28},{24,16},{28,20},{1,9},{5... | collective-permute-start | bytes 1769480 | tf_op jit(solution)/shard_map/ppermute | solution.py:417
  208.4 30.5 %copy-start.41 = (f32[384,768]{1,0:T(8,128)}, f32[384,768]{1,0:T(8,128)S(1)}, u32[]{:S(2)}) copy-start(f32[384,768]{1,0:T(8,128)S(1)} %add.227) | copy-start | bytes 3538948
  208.4 53.8 %copy-start.29 = (bf16[1,128,768]{2,1,0:T(8,128)(2,1)S(1)}, bf16[1,128,768]{2,1,0:T(8,128)(2,1)}, u32[]{:S(2)}) copy-start(bf16[1,128,768]{2,1,0:T(8,128)(2,1)} %param.19) | copy-start | bytes 589828
  210.8 28.0 %collective-permute-start.17 = (bf16[4,24,3072]{2,1,0:T(8,128)(2,1)S(1)}, bf16[4,24,3072]{2,1,0:T(8,128)(2,1)S(1)}, u32[]{:S(2)}, u32[]{:S(2)}) collective-permute-start(bf16[4,24,3072]{2,1,0:T(8,128)(2,1)S(1)} %get-tuple-element.107.refs_1_), channel_id=1, source_target_pairs={{0,16},{4,20},{8,24},{12,28},{16,0},{20,4},{24,8},{28,12},{1,17},{... | collective-permute-start | bytes 1769480 | tf_op jit(solution)/shard_map/ppermute | solution.py:417
  225.2 14.1 %collective-permute-start.16 = (bf16[4,24,3072]{2,1,0:T(8,128)(2,1)S(1)}, bf16[4,24,3072]{2,1,0:T(8,128)(2,1)S(1)}, u32[]{:S(2)}, u32[]{:S(2)}) collective-permute-start(bf16[4,24,3072]{2,1,0:T(8,128)(2,1)S(1)} %collective-permute-done.15.refs_5_.refs_3_), channel_id=1, source_target_pairs={{0,4},{4,0},{8,12},{12,8},{16,20},{20,16},{24,28},{28,24},{1,5},{5... | collective-permute-start | bytes 1769480 | tf_op jit(solution)/shard_map/ppermute | solution.py:417
  233.9 27.7 %collective-permute-start.23 = (f32[72,128]{1,0:T(8,128)}, f32[72,128]{1,0:T(8,128)}, u32[]{:S(2)}, u32[]{:S(2)}) collective-permute-start(f32[72,128]{1,0:T(8,128)} %bitcast.18), channel_id=1, source_target_pairs={{0,3},{1,2},{2,1},{3,0},{4,7},{5,6},{6,5},{7,4},{8,11},{9,10},{10,... | collective-permute-start | bytes 110600 | tf_op jit(solution)/shard_map/ppermute | solution.py:417
  233.9 30.8 %collective-permute-start.22 = (f32[72,128]{1,0:T(8,128)}, f32[72,128]{1,0:T(8,128)}, u32[]{:S(2)}, u32[]{:S(2)}) collective-permute-start(f32[72,128]{1,0:T(8,128)} %bitcast.18), channel_id=1, source_target_pairs={{0,2},{1,3},{2,0},{3,1},{4,6},{5,7},{6,4},{7,5},{8,10},{9,11},{10,... | collective-permute-start | bytes 110600 | tf_op jit(solution)/shard_map/ppermute | solution.py:417
  239.9 15.3 %collective-permute-start.19 = (bf16[4,24,3072]{2,1,0:T(8,128)(2,1)S(1)}, bf16[4,24,3072]{2,1,0:T(8,128)(2,1)}, u32[]{:S(2)}, u32[]{:S(2)}) collective-permute-start(bf16[4,24,3072]{2,1,0:T(8,128)(2,1)S(1)} %again.1), channel_id=1, source_target_pairs={{0,24},{4,28},{8,16},{12,20},{16,8},{20,12},{24,0},{28,4},{1,25},{... | collective-permute-start | bytes 1769480 | tf_op jit(solution)/shard_map/ppermute | solution.py:417
  244.8 24.6 %collective-permute-start.14 = (bf16[4,24,3072]{2,1,0:T(8,128)(2,1)S(1)}, bf16[4,24,3072]{2,1,0:T(8,128)(2,1)S(1)}, u32[]{:S(2)}, u32[]{:S(2)}) collective-permute-start(bf16[4,24,3072]{2,1,0:T(8,128)(2,1)S(1)} %get-tuple-element.107.refs_1_), channel_id=1, source_target_pairs={{0,4},{4,0},{8,12},{12,8},{16,20},{20,16},{24,28},{28,24},{1,5},{5... | collective-permute-start | bytes 1769480 | tf_op jit(solution)/shard_map/ppermute | solution.py:417
  246.4 27.4 %collective-permute-start.18 = (bf16[4,24,3072]{2,1,0:T(8,128)(2,1)S(1)}, bf16[4,24,3072]{2,1,0:T(8,128)(2,1)}, u32[]{:S(2)}, u32[]{:S(2)}) collective-permute-start(bf16[4,24,3072]{2,1,0:T(8,128)(2,1)S(1)} %collective-permute-done.17.refs_3_.refs_7_.refs_5_), channel_id=1, source_target_pairs={{0,4},{4,0},{8,12},{12,8},{16,20},{20,16},{24,28},{28,24},{1,5},{5... | collective-permute-start | bytes 1769480 | tf_op jit(solution)/shard_map/ppermute | solution.py:417
  255.1 27.8 %collective-permute-start.20 = (bf16[4,24,3072]{2,1,0:T(8,128)(2,1)}, bf16[4,24,3072]{2,1,0:T(8,128)(2,1)}, u32[]{:S(2)}, u32[]{:S(2)}) collective-permute-start(bf16[4,24,3072]{2,1,0:T(8,128)(2,1)} %collective-permute-done.19.refs_9_.refs_7_), channel_id=1, source_target_pairs={{0,4},{4,0},{8,12},{12,8},{16,20},{20,16},{24,28},{28,24},{1,5},{5... | collective-permute-start | bytes 1769480 | tf_op jit(solution)/shard_map/ppermute | solution.py:417
  257.3 12.1 %all-to-all-start.5 = ((bf16[4,24,2112]{2,1,0:T(8,128)(2,1)}), bf16[4,24,2112]{2,1,0:T(8,128)(2,1)}, u32[]{:S(2)}, u32[]{:S(2)}) async-start(bf16[4,24,2112]{2,1,0:T(8,128)(2,1)} %copy-done.32), calls=%async_computation.5 | async-start | bytes 835584 | tf_op jit(solution)/shard_map/all_to_all | solution.py:421
  261.7 3.0 collective-permute-start.21
  285.7 65.8 %collective-permute-start.31 = (bf16[24,9216]{1,0:T(8,128)(2,1)}, bf16[24,9216]{1,0:T(8,128)(2,1)}, u32[]{:S(2)}, u32[]{:S(2)}) collective-permute-start(bf16[24,9216]{1,0:T(8,128)(2,1)} %get-tuple-element.112.refs_9_), channel_id=1, source_target_pairs={{0,4},{4,0},{8,12},{12,8},{16,20},{20,16},{24,28},{28,24},{1,5},{5... | collective-permute-start | bytes 1327112 | tf_op jit(solution)/shard_map/ppermute | solution.py:417
  287.4 40.7 %collective-permute-start.27 = (bf16[24,9216]{1,0:T(8,128)(2,1)}, bf16[24,9216]{1,0:T(8,128)(2,1)S(1)}, u32[]{:S(2)}, u32[]{:S(2)}) collective-permute-start(bf16[24,9216]{1,0:T(8,128)(2,1)} %get-tuple-element.112.refs_9_), channel_id=1, source_target_pairs={{0,24},{4,28},{8,16},{12,20},{16,8},{20,12},{24,0},{28,4},{1,25},{... | collective-permute-start | bytes 1327112 | tf_op jit(solution)/shard_map/ppermute | solution.py:417
  288.1 40.0 %collective-permute-start.26 = (bf16[24,9216]{1,0:T(8,128)(2,1)}, bf16[24,9216]{1,0:T(8,128)(2,1)S(1)}, u32[]{:S(2)}, u32[]{:S(2)}) collective-permute-start(bf16[24,9216]{1,0:T(8,128)(2,1)} %get-tuple-element.112.refs_9_), channel_id=1, source_target_pairs={{0,16},{4,20},{8,24},{12,28},{16,0},{20,4},{24,8},{28,12},{1,17},{... | collective-permute-start | bytes 1327112 | tf_op jit(solution)/shard_map/ppermute | solution.py:417
  288.1 40.0 %collective-permute-start.25 = (bf16[24,9216]{1,0:T(8,128)(2,1)}, bf16[24,9216]{1,0:T(8,128)(2,1)S(1)}, u32[]{:S(2)}, u32[]{:S(2)}) collective-permute-start(bf16[24,9216]{1,0:T(8,128)(2,1)} %get-tuple-element.112.refs_9_), channel_id=1, source_target_pairs={{0,8},{4,12},{8,0},{12,4},{16,24},{20,28},{24,16},{28,20},{1,9},{5... | collective-permute-start | bytes 1327112 | tf_op jit(solution)/shard_map/ppermute | solution.py:417
  291.7 36.3 %collective-permute-start.24 = (f32[72,128]{1,0:T(8,128)S(1)}, f32[72,128]{1,0:T(8,128)S(1)}, u32[]{:S(2)}, u32[]{:S(2)}) collective-permute-start(f32[72,128]{1,0:T(8,128)S(1)} %get-tuple-element.113), channel_id=1, source_target_pairs={{0,4},{4,0},{8,12},{12,8},{16,20},{20,16},{24,28},{28,24},{1,5},{5... | collective-permute-start | bytes 110600 | tf_op jit(solution)/shard_map/ppermute | solution.py:417
  340.1 14.4 %collective-permute-start.30 = (f32[72,128]{1,0:T(8,128)S(1)}, f32[72,128]{1,0:T(8,128)S(1)}, u32[]{:S(2)}, u32[]{:S(2)}) collective-permute-start(f32[72,128]{1,0:T(8,128)S(1)} %get-tuple-element.114), channel_id=1, source_target_pairs={{0,24},{4,28},{8,16},{12,20},{16,8},{20,12},{24,0},{28,4},{1,25},{... | collective-permute-start | bytes 110600 | tf_op jit(solution)/shard_map/ppermute | solution.py:417
  340.8 15.3 %collective-permute-start.29 = (f32[72,128]{1,0:T(8,128)S(1)}, f32[72,128]{1,0:T(8,128)S(1)}, u32[]{:S(2)}, u32[]{:S(2)}) collective-permute-start(f32[72,128]{1,0:T(8,128)S(1)} %get-tuple-element.114), channel_id=1, source_target_pairs={{0,16},{4,20},{8,24},{12,28},{16,0},{20,4},{24,8},{28,12},{1,17},{... | collective-permute-start | bytes 110600 | tf_op jit(solution)/shard_map/ppermute | solution.py:417
  341.6 14.5 %collective-permute-start.28 = (f32[72,128]{1,0:T(8,128)S(1)}, f32[72,128]{1,0:T(8,128)S(1)}, u32[]{:S(2)}, u32[]{:S(2)}) collective-permute-start(f32[72,128]{1,0:T(8,128)S(1)} %get-tuple-element.114), channel_id=1, source_target_pairs={{0,8},{4,12},{8,0},{12,4},{16,24},{20,28},{24,16},{28,20},{1,9},{5... | collective-permute-start | bytes 110600 | tf_op jit(solution)/shard_map/ppermute | solution.py:417
  344.6 14.8 %copy-start.51 = (f32[192]{0:T(256)S(1)}, f32[192]{0:T(256)}, u32[]{:S(2)}) copy-start(f32[192]{0:T(256)} %param.29) | copy-start | bytes 2308
  344.6 19.5 %copy-start.47 = (f32[768]{0:T(1024)S(1)}, f32[768]{0:T(1024)}, u32[]{:S(2)}) copy-start(f32[768]{0:T(1024)} %param.31) | copy-start | bytes 9220
  344.6 20.1 %copy-start.52 = (f32[192]{0:T(256)S(1)}, f32[192]{0:T(256)}, u32[]{:S(2)}) copy-start(f32[192]{0:T(256)} %param.25) | copy-start | bytes 2308
  344.6 20.8 %copy-start.53 = (f32[192]{0:T(256)S(1)}, f32[192]{0:T(256)}, u32[]{:S(2)}) copy-start(f32[192]{0:T(256)} %param.24) | copy-start | bytes 2308
  344.6 21.4 %copy-start.54 = (f32[192]{0:T(256)S(1)}, f32[192]{0:T(256)}, u32[]{:S(2)}) copy-start(f32[192]{0:T(256)} %param.23) | copy-start | bytes 2308
  344.6 22.0 %copy-start.55 = (f32[192]{0:T(256)S(1)}, f32[192]{0:T(256)}, u32[]{:S(2)}) copy-start(f32[192]{0:T(256)} %param.22) | copy-start | bytes 2308
  344.6 22.7 %copy-start.48 = (f32[576]{0:T(1024)S(1)}, f32[576]{0:T(1024)}, u32[]{:S(2)}) copy-start(f32[576]{0:T(1024)} %param.27) | copy-start | bytes 6916
  344.6 59.0 %all-to-all-start.6 = ((bf16[4,8,24,3072]{3,2,1,0:T(8,128)(2,1)}), bf16[4,8,24,3072]{3,2,1,0:T(8,128)(2,1)}, u32[]{:S(2)}, u32[]{:S(2)}) async-start(bf16[4,8,24,3072]{3,2,1,0:T(8,128)(2,1)} %get-tuple-element.119), calls=%async_computation.6 | async-start | bytes 9437184 | tf_op jit(solution)/shard_map/all_to_all | solution.py:421
  349.8 34.7 %collective-permute-start.34 = (bf16[24,9216]{1,0:T(8,128)(2,1)S(1)}, bf16[24,9216]{1,0:T(8,128)(2,1)S(1)}, u32[]{:S(2)}, u32[]{:S(2)}) collective-permute-start(bf16[24,9216]{1,0:T(8,128)(2,1)S(1)} %copy-done.13), channel_id=1, source_target_pairs={{0,4},{4,0},{8,12},{12,8},{16,20},{20,16},{24,28},{28,24},{1,5},{5... | collective-permute-start | bytes 1327112 | tf_op jit(solution)/shard_map/ppermute | solution.py:417
  351.5 31.3 %collective-permute-start.33 = (bf16[24,9216]{1,0:T(8,128)(2,1)S(1)}, bf16[24,9216]{1,0:T(8,128)(2,1)S(1)}, u32[]{:S(2)}, u32[]{:S(2)}) collective-permute-start(bf16[24,9216]{1,0:T(8,128)(2,1)S(1)} %copy-done.15), channel_id=1, source_target_pairs={{0,4},{4,0},{8,12},{12,8},{16,20},{20,16},{24,28},{28,24},{1,5},{5... | collective-permute-start | bytes 1327112 | tf_op jit(solution)/shard_map/ppermute | solution.py:417
  354.5 26.8 %collective-permute-start.32 = (bf16[24,9216]{1,0:T(8,128)(2,1)S(1)}, bf16[24,9216]{1,0:T(8,128)(2,1)S(1)}, u32[]{:S(2)}, u32[]{:S(2)}) collective-permute-start(bf16[24,9216]{1,0:T(8,128)(2,1)S(1)} %copy-done.17), channel_id=1, source_target_pairs={{0,4},{4,0},{8,12},{12,8},{16,20},{20,16},{24,28},{28,24},{1,5},{5... | collective-permute-start | bytes 1327112 | tf_op jit(solution)/shard_map/ppermute | solution.py:417
  359.3 53.5 %copy-start.49 = (f32[192]{0:T(256)}, f32[192]{0:T(256)S(1)}, u32[]{:S(2)}) copy-start(f32[192]{0:T(256)S(1)} %get-tuple-element.229) | copy-start | bytes 2308
  (35 other events, 147.9 us)
